TPU v7x, 32 devices: a whole 2x2x4 slice. The times are simulated.
32 devices in a mesh: cols: 8 (over z, x), edge: 4 (over y, core).
Axes of the slice: x: 2, y: 2, z: 4, core: 2. Of those that a mesh axis runs over, the one named last changes fastest.
Arguments:
- state: float32 [4, 1024, 512], P('edge', 'cols'), may hold values from -6 to 6
- owners: int32 [4, 1024, 1], P('edge', 'cols'), may hold values from 0 to 7; in each aligned block of 128 rows (0 to 127, 128 to 255, ..., all dimensions but the last counted through in order) at most 32 rows name the same one
- orient: int32 [4, 8, 2], P('edge', 'cols'), may hold values from 0 to 1
- crm_state: bfloat16 [4, 8, 58, 16384], P('edge', 'cols'), may hold values from -6 to 6
- active_levels: int32 [4, 8, 256], P('edge', 'cols'), may hold values from 14 to 58
- vertical_map: float32 [58, 64], replicated, may hold values from -0.75 to 0.75
- diffusion: float32 [57], replicated, may hold values from 0.1 to 4
Outputs:
- new_state: float32 [4, 1024, 512], P('edge', 'cols')
- crm_out: bfloat16 [4, 8, 58, 16384], P('edge', 'cols')
Inputs may be any that keep to these rules, and one draw needn't show every extreme that they name: `owners`: within the columns of one tile no group is named more than 32 times.
All inputs are finite; a program needn't handle non-finite values.
Results may differ from a plain program's by a relative error of at most 0.001.
Values sent between devices are 32-bit elements; how exact they have to be, the bound alone decides.
No kernel may reach another device: no remote copies, remote signals or barrier semaphores. Data moves between devices by JAX's collectives and lax.ppermute only.
A program may use at most 64 MiB of HBM per device.

v0:
```python
import jax
import jax.numpy as jnp
from jax import lax
from jax.sharding import PartitionSpec as P

L = 64
CX = 64
CZ = 58
TW = 8
SUBSTEPS = 2


kappa_edge = 0.25
max_courant = 0.9
relax_rate = 0.5


def from_behind(value, axis, steps):
    count = lax.axis_size(axis)
    pairs = [(source, (source + steps) % count) for source in range(count)]
    return lax.ppermute(value, axis, pairs)


def factorize(lower, diagonal, upper):
    depth = diagonal.shape[0]
    prev_c = jnp.zeros(diagonal.shape[1:], jnp.float32)
    factors = []
    denoms = []
    for level in range(depth):
        denom = diagonal[level] + lower[level] * prev_c
        prev_c = -upper[level] / denom
        factors.append(prev_c)
        denoms.append(denom)
    return (factors, denoms)


def tridiag(lower, factors, denoms, values):
    depth = values.shape[0]
    prev_d = jnp.zeros(values.shape[1:], jnp.float32)
    offsets = []
    for level in range(depth):
        prev_d = (values[level] + lower[level][None, :] * prev_d) / denoms[level][None, :]
        offsets.append(prev_d)
    after = jnp.zeros(values.shape[1:], jnp.float32)
    solved = [None] * depth
    for level in range(depth - 1, -1, -1):
        after = offsets[level] - factors[level][None, :] * after
        solved[level] = after
    return jnp.stack(solved, axis=0)


def physics(columns, crm_slab, active_count, vertical_map, diffusion):
    slots = columns.shape[0]
    temper = columns[:, 0:L]
    moisture = columns[:, L : 2 * L]
    forcing = jnp.einsum(
        "zl,sl->zs",
        vertical_map,
        temper,
        precision=lax.Precision.HIGHEST,
        preferred_element_type=jnp.float32,
    )
    courant = max_courant * jax.nn.sigmoid(
        jnp.einsum(
            "zl,sl->zs",
            vertical_map,
            moisture,
            precision=lax.Precision.HIGHEST,
            preferred_element_type=jnp.float32,
        )
    )
    field = crm_slab.reshape(CZ, CX, slots).astype(jnp.float32)
    mean_before = jnp.mean(field, axis=1)
    spread_before = jnp.mean(field * field, axis=1) - mean_before * mean_before
    field = field + relax_rate * (forcing - mean_before)[:, None, :]
    heights = jnp.arange(CZ - 1, dtype=jnp.int32)
    coupled = (heights[:, None] + 1 < active_count[None, :]).astype(jnp.float32)
    interfaces = diffusion[:, None] * coupled
    zero_row = jnp.zeros((1, slots), jnp.float32)
    lower = jnp.concatenate([zero_row, interfaces], axis=0)
    upper = jnp.concatenate([interfaces, zero_row], axis=0)
    diagonal = 1.0 + lower + upper
    factors, denoms = factorize(lower, diagonal, upper)
    for substep in range(SUBSTEPS):
        field = field - courant[:, None, :] * (field - jnp.roll(field, 1, axis=1))
        field = tridiag(lower, factors, denoms, field)
    mean_after = jnp.mean(field, axis=1)
    spread_after = jnp.mean(field * field, axis=1) - mean_after * mean_after
    tend_mean = jnp.einsum(
        "zs,zl->sl",
        mean_after - mean_before,
        vertical_map,
        precision=lax.Precision.HIGHEST,
        preferred_element_type=jnp.float32,
    )
    tend_spread = jnp.einsum(
        "zs,zl->sl",
        spread_after - spread_before,
        vertical_map,
        precision=lax.Precision.HIGHEST,
        preferred_element_type=jnp.float32,
    )
    tend = jnp.concatenate([tend_mean, tend_spread], axis=1)
    return (tend, field.reshape(CZ, CX * slots).astype(jnp.bfloat16))


def shards(state, owners, orient, crm_state, active_levels, vertical_map, diffusion):
    n_tiles = lax.axis_size("cols")
    per_tile = state.shape[1]
    width = state.shape[2]
    cap_slots = max(2, 2 * per_tile // n_tiles)
    rows_along = per_tile // TW
    tiles = state[0].reshape(rows_along, TW, width)
    upper_row = tiles[rows_along - 1]
    lower_row = tiles[0]
    ghost_low = from_behind(upper_row, "edge", 1)
    ghost_high = from_behind(lower_row, "edge", -1)
    flags = orient[0, 0]
    ghost_low = jnp.where(flags[0] == 1, ghost_low[::-1], ghost_low)
    ghost_high = jnp.where(flags[1] == 1, ghost_high[::-1], ghost_high)
    padded = jnp.concatenate([ghost_low[None], tiles, ghost_high[None]], axis=0)
    moved = tiles + kappa_edge * (padded[2:] + padded[:-2] - 2.0 * tiles)
    moved = moved.reshape(per_tile, width)
    group_of = owners[0, :, 0]
    same = group_of[:, None] == group_of[None, :]
    order = jnp.arange(per_tile, dtype=jnp.int32)
    earlier = order[None, :] < order[:, None]
    ranking = jnp.sum((same & earlier).astype(jnp.int32), axis=1)
    slot_index = group_of * cap_slots + ranking
    payload = moved[:, 0 : 2 * L]
    outgoing = (
        jnp.zeros((n_tiles * cap_slots, payload.shape[1]), jnp.float32).at[slot_index].set(payload)
    )
    received = lax.all_to_all(outgoing, "cols", split_axis=0, concat_axis=0, tiled=True)
    tend, crm_new = physics(received, crm_state[0, 0], active_levels[0, 0], vertical_map, diffusion)
    updated = received + tend
    returned = lax.all_to_all(updated, "cols", split_axis=0, concat_axis=0, tiled=True)
    gathered = returned[slot_index]
    new_state = jnp.concatenate([gathered, moved[:, 2 * L :]], axis=1)
    return (new_state[None], crm_new[None, None])


def solution(mesh):
    in_specs = (
        P("edge", "cols", None),
        P("edge", "cols", None),
        P("edge", "cols", None),
        P("edge", "cols", None, None),
        P("edge", "cols", None),
        P(),
        P(),
    )
    out_specs = (P("edge", "cols", None), P("edge", "cols", None, None))
    return jax.shard_map(shards, mesh=mesh, in_specs=in_specs, out_specs=out_specs, check_vma=False)
```

profile of v0, /device:TPU:0, one launch (start us, length us, event | category | flops | bytes accessed | tf_op | source)
XLA Modules:
  0.0 85.4 jit_solution(5529947687027960808)
XLA Ops:
  1.4 2.4 %collective-permute-start = (f32[8,512]{1,0:T(8,128)S(1)}, f32[8,512]{1,0:T(8,128)S(1)}, u32[]{:S(2)}, u32[]{:S(2)}) collective-permute-start(f32[8,512]{1,0:T(8,128)S(1)} %get-tuple-element.318), channel_id=1, source_target_pairs={{0,3},{1,0},{2,1},{3,2},{4,7},{5,4},{6,5},{7,6},{8,11},{9,8},{10,9... | collective-permute-start | bytes 49160 | tf_op jit(solution)/shard_map/ppermute | solution.py:21
  7.0 1.9 %convert_element_type.29 = f32[1,1,58,16384]{3,2,1,0:T(8,128)S(1)} convert(bf16[1,1,58,16384]{3,2,1,0:T(8,128)(2,1)} %param.10) | non-fusion elementwise | flops 950272 | bytes 5701632 | tf_op jit(solution)/shard_map/convert_element_type | solution.py:72
  8.8 1.3 %copy.16 = f32[8,8,64,256]{3,2,1,0:T(8,128)S(1)} copy(f32[8,8,64,256]{3,1,2,0:T(8,128)S(1)} %bitcast.1262) | data formatting | bytes 8388608
  10.1 2.0 %copy-done.1 = f32[8,8,64,256]{3,2,1,0:T(8,128)} copy-done((f32[8,8,64,256]{3,2,1,0:T(8,128)}, f32[8,8,64,256]{3,2,1,0:T(8,128)S(1)}, u32[]{:S(2)}) %copy-start.1) | copy-done | bytes 4194328
  12.1 1.2 %slice_reduce_fusion = (f32[58,256]{1,0:T(8,128)S(1)}, f32[58,256]{1,0:T(8,128)S(1)}) fusion(f32[64,64,256]{2,1,0:T(8,128)S(1)} %bitcast.1259), kind=kLoop, calls=%fused_computation.11 | loop fusion | flops 2821120 | bytes 3919872 | tf_op jit(solution)/shard_map/reduce_sum | solution.py:73
  15.5 1.5 %scatter_custom_fusion = f32[256,128]{1,0:T(8,128)} fusion(s32[128]{0:T(128)S(1)} %fusion.244, f32[128,512]{1,0:T(8,128)S(1)} %fusion.15, f32[]{:T(128)} %constant.13.clone.1), kind=kCustom, calls=%fused_computation.148 | custom fusion | bytes 196612 | tf_op jit(solution)/shard_map/scatter | solution.py:132
  17.0 5.8 %all-to-all-start = ((f32[8,32,128]{2,1,0:T(8,128)}), f32[8,32,128]{2,1,0:T(8,128)S(1)}, u32[]{:S(2)}, u32[]{:S(2)}) async-start(f32[8,32,128]{2,1,0:T(8,128)} %bitcast.12), calls=%async_computation | async-start | bytes 262144 | tf_op jit(solution)/shard_map/all_to_all | solution.py:134
  23.2 7.4 %all-to-all-done = f32[8,32,128]{2,1,0:T(8,128)S(1)} async-done(((f32[8,32,128]{2,1,0:T(8,128)}), f32[8,32,128]{2,1,0:T(8,128)S(1)}, u32[]{:S(2)}, u32[]{:S(2)}) %all-to-all-start) | async-done | bytes 131104 | tf_op jit(solution)/shard_map/all_to_all | solution.py:134
  31.3 2.7 %slice_add_fusion = f32[58,64,256]{2,1,0:T(8,128)S(1)} fusion(f32[64,64,256]{2,1,0:T(8,128)} %bitcast.1260, f32[58,256]{1,0:T(8,128)S(1)} %fusion.10), kind=kLoop, calls=%fused_computation.10 | loop fusion | flops 950272 | bytes 7661568 | tf_op jit(solution)/shard_map/add | solution.py:75
  34.6 1.5 %fusion.1 = f32[58,64,256]{2,1,0:T(8,128)S(1)} fusion(f32[58,63,256]{2,1,0:T(8,128)S(1)} %bitcast.1264, f32[58,1,256]{2,1,0:T(1,128)S(1)} %slice.1164, f32[58,256]{1,0:T(8,128)S(1)} %fusion.8, f32[58,256]{1,0:T(8,128)S(1)} %fusion.10, f32[64,64,256]{2,1,0:T(8,128)S(1)} %bitcast.1261), kind=kLoop, calls=%fused_computation.4 | loop fusion | flops 4751360 | bytes 11522048 | tf_op jit(solution)/shard_map/sub | solution.py:85
  37.7 1.0 %constant_dynamic-update-slice_fusion.14 = (f32[58,64,256]{2,1,0:T(8,128)S(1)}, f32[64,256]{1,0:T(8,128)S(1)}, f32[64,256]{1,0:T(8,128)S(1)}, f32[64,256]{1,0:T(...) fusion(f32[58,64,256]{2,1,0:T(8,128)S(1)} %constant_dynamic-upd, ...), kind=kLoop, calls=%fused_computation.43 | loop fusion | flops 3293184 | bytes 4851712
  39.0 1.4 %fusion.3 = f32[58,64,256]{2,1,0:T(8,128)S(1)} fusion(f32[58,64,256]{2,1,0:T(8,128)S(1)} %constant_dynamic-update-slice_fusion, f32[58,63,256]{2,1,0:T(8,128)S(1)} %bitcast.1263, f32[58,1,256]{2,1,0:T(1,128)S(1)} %slice.1339, f32[58,256]{1,0:T(8,128)S(1)} %fusion.8), kind=kLoop, calls=%fused_computation.7 | loop fusion | flops 3801088 | bytes 11462656 | tf_op jit(solution)/shard_map/sub | solution.py:85
  49.9 1.2 %fusion.247 = (f32[58,256]{1,0:T(8,128)S(1)}, f32[58,256]{1,0:T(8,128)S(1)}) fusion(f32[58,64,256]{2,1,0:T(8,128)S(1)} %constant_dynamic-update-slice_fusion.58), kind=kLoop, calls=%fused_computation.772 | loop fusion | flops 2821120 | bytes 3919872 | tf_op jit(solution)/shard_map/reduce_sum | solution.py:87
  52.7 3.6 %all-to-all-start.1 = ((f32[8,32,128]{2,1,0:T(8,128)}), f32[8,32,128]{2,1,0:T(8,128)S(1)}, u32[]{:S(2)}, u32[]{:S(2)}) async-start(f32[8,32,128]{2,1,0:T(8,128)} %maximum_add_fusion), calls=%async_computation.1 | async-start | bytes 262144 | tf_op jit(solution)/shard_map/all_to_all | solution.py:137
  58.2 1.4 %stack.365 = bf16[1,1,1,16384]{3,2,1,0:T(2,128)(2,1)} reshape(bf16[1,64,256]{2,1,0:T(8,128)(2,1)} %get-tuple-element.79) | data formatting | bytes 65536 | tf_op jit(solution)/shard_map/stack | solution.py:49
  59.6 1.4 %stack.366 = bf16[1,1,1,16384]{3,2,1,0:T(2,128)(2,1)} reshape(bf16[1,64,256]{2,1,0:T(8,128)(2,1)} %get-tuple-element.77) | data formatting | bytes 65536 | tf_op jit(solution)/shard_map/stack | solution.py:49
  61.0 1.4 %stack.367 = bf16[1,1,1,16384]{3,2,1,0:T(2,128)(2,1)} reshape(bf16[1,64,256]{2,1,0:T(8,128)(2,1)} %get-tuple-element.75) | data formatting | bytes 65536 | tf_op jit(solution)/shard_map/stack | solution.py:49
  62.4 1.4 %stack.368 = bf16[1,1,1,16384]{3,2,1,0:T(2,128)(2,1)} reshape(bf16[1,64,256]{2,1,0:T(8,128)(2,1)} %get-tuple-element.73) | data formatting | bytes 65536 | tf_op jit(solution)/shard_map/stack | solution.py:49
  63.8 1.4 %stack.369 = bf16[1,1,1,16384]{3,2,1,0:T(2,128)(2,1)} reshape(bf16[1,64,256]{2,1,0:T(8,128)(2,1)} %get-tuple-element.71) | data formatting | bytes 65536 | tf_op jit(solution)/shard_map/stack | solution.py:49
  65.2 1.4 %stack.370 = bf16[1,1,1,16384]{3,2,1,0:T(2,128)(2,1)} reshape(bf16[1,64,256]{2,1,0:T(8,128)(2,1)} %get-tuple-element.69) | data formatting | bytes 65536 | tf_op jit(solution)/shard_map/stack | solution.py:49
  66.5 1.4 %stack.371 = bf16[1,1,1,16384]{3,2,1,0:T(2,128)(2,1)} reshape(bf16[1,64,256]{2,1,0:T(8,128)(2,1)} %get-tuple-element.67) | data formatting | bytes 65536 | tf_op jit(solution)/shard_map/stack | solution.py:49
  67.9 1.4 %stack.372 = bf16[1,1,1,16384]{3,2,1,0:T(2,128)(2,1)} reshape(bf16[1,64,256]{2,1,0:T(8,128)(2,1)} %get-tuple-element.65) | data formatting | bytes 65536 | tf_op jit(solution)/shard_map/stack | solution.py:49
  69.3 1.4 %stack.373 = bf16[1,1,1,16384]{3,2,1,0:T(2,128)(2,1)} reshape(bf16[1,64,256]{2,1,0:T(8,128)(2,1)} %get-tuple-element.63) | data formatting | bytes 65536 | tf_op jit(solution)/shard_map/stack | solution.py:49
  71.4 12.6 %stack.390 = bf16[1,1,58,16384]{3,2,1,0:T(8,128)(2,1)} concatenate(bf16[1,1,1,16384]{3,2,1,0:T(2,128)(2,1)S(1)} %stack.332, bf16[1,1,1,16384]{3,2,1,0:T(2,128)(2,1)S(1)} %stack.333, bf16[1,1,1,16384]{3,2,1,0:T(2,128)(2,1)S(1)} %stack.334, bf16[1,1,1,16384]{3,2,1,0:T(2,128)(2,1)S(1)} %stack.335, bf16[1,1,1,16384]{3,2,1,0:T(2,128)(2,1)S(1)} %stack.336, ...), dimensions={2} | concatenate | bytes 3801088 | tf_op jit(solution)/shard_map/stack | solution.py:49
  (270 shorter events, 21.8 us)
Async XLA Ops:
  0.6 30.0 %copy-start = (f32[58,64]{1,0:T(8,128)S(1)}, f32[58,64]{1,0:T(8,128)}, u32[]{:S(2)}) copy-start(f32[58,64]{1,0:T(8,128)} %param.12) | copy-start | bytes 44548
  1.4 13.7 %collective-permute-start = (f32[8,512]{1,0:T(8,128)S(1)}, f32[8,512]{1,0:T(8,128)S(1)}, u32[]{:S(2)}, u32[]{:S(2)}) collective-permute-start(f32[8,512]{1,0:T(8,128)S(1)} %get-tuple-element.318), channel_id=1, source_target_pairs={{0,3},{1,0},{2,1},{3,2},{4,7},{5,4},{6,5},{7,6},{8,11},{9,8},{10,9... | collective-permute-start | bytes 49160 | tf_op jit(solution)/shard_map/ppermute | solution.py:21
  3.8 11.4 %collective-permute-start.1 = (f32[8,512]{1,0:T(8,128)S(1)}, f32[8,512]{1,0:T(8,128)S(1)}, u32[]{:S(2)}, u32[]{:S(2)}) collective-permute-start(f32[8,512]{1,0:T(8,128)S(1)} %get-tuple-element.319), channel_id=1, source_target_pairs={{0,1},{1,2},{2,3},{3,0},{4,5},{5,6},{6,7},{7,4},{8,9},{9,10},{10,1... | collective-permute-start | bytes 49160 | tf_op jit(solution)/shard_map/ppermute | solution.py:21
  10.1 2.0 %copy-start.1 = (f32[8,8,64,256]{3,2,1,0:T(8,128)}, f32[8,8,64,256]{3,2,1,0:T(8,128)S(1)}, u32[]{:S(2)}) copy-start(f32[8,8,64,256]{3,2,1,0:T(8,128)S(1)} %copy.16) | copy-start | bytes 12582916
  10.1 3.1 %copy-start.5 = (s32[1,1,2]{2,1,0:T(1,128)S(1)}, s32[1,1,2]{2,1,0:T(1,128)}, u32[]{:S(2)}) copy-start(s32[1,1,2]{2,1,0:T(1,128)} %param.9) | copy-start | bytes 28
  10.1 5.3 %copy-start.4 = (f32[1,128,512]{2,1,0:T(8,128)S(1)}, f32[1,128,512]{2,1,0:T(8,128)}, u32[]{:S(2)}) copy-start(f32[1,128,512]{2,1,0:T(8,128)} %param.7) | copy-start | bytes 786436
  15.4 18.5 %copy-start.3 = (f32[128,512]{1,0:T(8,128)}, f32[128,512]{1,0:T(8,128)S(1)}, u32[]{:S(2)}) copy-start(f32[128,512]{1,0:T(8,128)S(1)} %fusion.15) | copy-start | bytes 786436
  17.0 13.7 %all-to-all-start = ((f32[8,32,128]{2,1,0:T(8,128)}), f32[8,32,128]{2,1,0:T(8,128)S(1)}, u32[]{:S(2)}, u32[]{:S(2)}) async-start(f32[8,32,128]{2,1,0:T(8,128)} %bitcast.12), calls=%async_computation | async-start | bytes 262144 | tf_op jit(solution)/shard_map/all_to_all | solution.py:134
  31.3 3.3 %copy-start.2 = (f32[8,8,64,256]{3,2,1,0:T(8,128)S(1)}, f32[8,8,64,256]{3,2,1,0:T(8,128)}, u32[]{:S(2)}) copy-start(f32[8,8,64,256]{3,2,1,0:T(8,128)} %copy-done.1) | copy-start | bytes 12582916
  52.7 31.4 %all-to-all-start.1 = ((f32[8,32,128]{2,1,0:T(8,128)}), f32[8,32,128]{2,1,0:T(8,128)S(1)}, u32[]{:S(2)}, u32[]{:S(2)}) async-start(f32[8,32,128]{2,1,0:T(8,128)} %maximum_add_fusion), calls=%async_computation.1 | async-start | bytes 262144 | tf_op jit(solution)/shard_map/all_to_all | solution.py:137
  57.3 27.3 %slice-start = ((f32[128,512]{1,0:T(8,128)}), f32[128,384]{1,0:T(8,128)S(1)}, s32[]{:S(2)}) async-start(f32[128,512]{1,0:T(8,128)} %copy-done.3), calls=%async_computation.2 | async-start | bytes 393216 | tf_op jit(solution)/shard_map/slice | solution.py:139
where the time goes:
time: 86.6 us; the launch traced here: 85.4 us
  local copies, waits for them, and re-layouts  35.7 us (41%)
  other arithmetic  25.3 us (29%)
  starting transfers between devices  11.8 us (14%)
  waiting for transfers between devices  7.43 us (9%)
  between operations  3.71 us (4%)
  matrix products  1.41 us (2%)
    another operation x60, local copies, waits for them, and re-layouts, tridiag(): return jnp.stack(solved, axis=0)  27.5 us
    another operation x58, other arithmetic  8.29 us
    all_to_all x1, waiting for transfers between devices, shards(): lax.all_to_all(outgoing, 'cols', split_axis=0, concat_axis=0, tiled=True)  7.42 us
    all_to_all x1, starting transfers between devices, shards(): lax.all_to_all(outgoing, 'cols', split_axis=0, concat_axis=0, tiled=True)  5.81 us
    unnamed x95, local copies, waits for them, and re-layouts  4.33 us
    all_to_all x1, starting transfers between devices, shards(): lax.all_to_all(updated, 'cols', split_axis=0, concat_axis=0, tiled=True)  3.59 us
    sub x2, other arithmetic, physics(): field = field - courant[:, None, :] * (field - jnp.roll(field, 1, axis=1))  2.86 us
    add x1, other arithmetic, physics(): field = field + relax_rate * (forcing - mean_before)[:, None, :]  2.71 us
  transfers between devices with their start and end apart: 4, of which 1 were waited for; matrix products, arithmetic and copies ran while one was open for 42% of the time, Pallas kernels for 0%

commit v1 on v0

v1 whole, which is shorter than its diff:
```python
import functools

import jax
import jax.numpy as jnp
from jax import lax
from jax.experimental import pallas as pl
from jax.experimental.pallas import tpu as pltpu
from jax.sharding import PartitionSpec as P

L = 64
CX = 64
CZ = 58
TW = 8
SUBSTEPS = 2
ZP = 64
LANES = 128
SUB = 8
NI = CX // SUB
TZ = 16

kappa_edge = 0.25
max_courant = 0.9
relax_rate = 0.5

HI = lax.Precision.HIGHEST


def call(body, outs, args, scratch=(), in_specs=None, cost=None, limit=32 << 20, aliases=None):
    kw = {}
    if in_specs is not None:
        kw["in_specs"] = in_specs
    return pl.pallas_call(
        body,
        out_shape=outs,
        scratch_shapes=list(scratch),
        compiler_params=pltpu.CompilerParams(vmem_limit_bytes=limit),
        cost_estimate=cost,
        input_output_aliases=aliases or {},
        **kw,
    )(*args)


def dot(a, b, dims):
    return lax.dot_general(a, b, (dims, ((), ())), precision=HI, preferred_element_type=jnp.float32)


def from_behind(value, axis, steps):
    count = lax.axis_size(axis)
    pairs = [(source, (source + steps) % count) for source in range(count)]
    return lax.ppermute(value, axis, pairs)


def slots_kernel(cap, owners_ref, put_ref, take_ref):
    per_tile = owners_ref.shape[0]
    n_slots = put_ref.shape[0]
    down = jnp.broadcast_to(owners_ref[...], (per_tile, per_tile))
    across = down.T
    row = lax.broadcasted_iota(jnp.int32, (per_tile, per_tile), 0)
    col = lax.broadcasted_iota(jnp.int32, (per_tile, per_tile), 1)
    same = down == across
    before_col = jnp.where(same & (row < col), 1.0, 0.0)
    before_row = jnp.where(same & (col < row), 1.0, 0.0)
    rank_across = jnp.sum(before_col, axis=0, keepdims=True).astype(jnp.int32)
    rank_down = jnp.sum(before_row, axis=1, keepdims=True).astype(jnp.int32)
    slot_across = across[0:1, :] * cap + rank_across
    slot_down = owners_ref[...] * cap + rank_down
    q_down = lax.broadcasted_iota(jnp.int32, (n_slots, per_tile), 0)
    q_across = lax.broadcasted_iota(jnp.int32, (per_tile, n_slots), 1)
    put_ref[...] = jnp.where(q_down == slot_across, 1.0, 0.0)
    take_ref[...] = jnp.where(q_across == slot_down, 1.0, 0.0)


def edge_kernel(state_ref, low_ref, high_ref, flag_ref, put_ref, moved_ref, out_ref):
    per_tile = state_ref.shape[0]

    def turned(ref, flag):
        value = ref[...]
        back = jnp.concatenate([value[TW - 1 - w : TW - w] for w in range(TW)], axis=0)
        return jnp.where(flag == 1, back, value)

    low = turned(low_ref, flag_ref[0, 0])
    high = turned(high_ref, flag_ref[0, 1])
    tiles = state_ref[...]
    below = jnp.concatenate([low, tiles[: per_tile - TW]], axis=0)
    above = jnp.concatenate([tiles[TW:], high], axis=0)
    moved = tiles + kappa_edge * ((above + below) - 2.0 * tiles)
    moved_ref[...] = moved
    out_ref[...] = dot(put_ref[...], moved[:, : 2 * L], ((1,), (0,)))


def prepare_kernel(crm_ref, active_ref, diff_ref, vm_ref, f_ref, mean_ref, sq_ref, coef_ref, w_ref):
    slots = active_ref.shape[1]
    halves = slots // LANES
    zero = jnp.zeros((TZ, LANES), jnp.float32)
    n_t = ZP // TZ

    def column(x, sums):
        sums = list(sums)
        place = (x % NI) * SUB + x // NI
        for h in range(halves):
            lane = pl.multiple_of(x * slots + h * LANES, LANES)
            for t in range(n_t):
                rows = min(TZ, CZ - t * TZ)
                v = crm_ref[t * TZ : t * TZ + rows, pl.ds(lane, LANES)].astype(jnp.float32)
                first = (t * TZ * halves + h) * CX + place
                f_ref[pl.ds(first, rows, stride=halves * CX), :] = v
                k = (h * n_t + t) * 2
                if rows < TZ:
                    v = jnp.concatenate([v, jnp.zeros((TZ - rows, LANES), jnp.float32)], axis=0)
                sums[k] = sums[k] + v
                sums[k + 1] = sums[k + 1] + v * v
        return tuple(sums)

    sums = lax.fori_loop(0, CX, column, (zero,) * (halves * n_t * 2))
    for h in range(halves):
        for t in range(n_t):
            k = (h * n_t + t) * 2
            here = (slice(t * TZ, (t + 1) * TZ), slice(h * LANES, (h + 1) * LANES))
            mean_ref[here] = sums[k] * (1.0 / CX)
            sq_ref[here] = sums[k + 1] * (1.0 / CX)

    coef_ref[...] = jnp.zeros_like(coef_ref)
    active = active_ref[...]
    nothing = jnp.zeros((1, slots), jnp.float32)

    def link(i):
        if i < 0 or i >= CZ - 1:
            return nothing
        return jnp.where(i + 1 < active, diff_ref[i], 0.0)

    inv = nothing
    for z in range(CZ):
        lower, upper = link(z - 1), link(z)
        scaled = lower * inv
        inv = 1.0 / (1.0 + lower + upper - lower * scaled)
        coef_ref[0, z : z + 1, :] = inv
        coef_ref[1, z : z + 1, :] = lower * inv
        coef_ref[2, z : z + 1, :] = upper * inv
    inv = nothing
    for z in range(CZ - 1, -1, -1):
        lower, upper = link(z - 1), link(z)
        scaled = upper * inv
        inv = 1.0 / (1.0 + lower + upper - upper * scaled)
        coef_ref[3, z : z + 1, :] = inv
        coef_ref[4, z : z + 1, :] = upper * inv
        coef_ref[5, z : z + 1, :] = lower * inv

    w_ref[...] = jnp.zeros_like(w_ref)
    pad = jnp.zeros((CZ, L), jnp.float32)
    w_ref[0:CZ, :] = jnp.concatenate([vm_ref[...], pad], axis=1)
    w_ref[ZP : ZP + CZ, :] = jnp.concatenate([pad, vm_ref[...]], axis=1)


def physics_kernel(cols_ref, f_ref, mean_ref, sq_ref, coef_ref, w_ref, tend_ref, y_ref, adv_ref, acc_ref):
    slots = cols_ref.shape[0]
    halves = slots // LANES
    w = w_ref[...]
    mapped = dot(w, cols_ref[...], ((1,), (1,)))
    forcing = mapped[0:ZP]
    courant = max_courant * jax.nn.sigmoid(mapped[ZP:])
    inv1 = coef_ref[0]
    inv2 = coef_ref[3]
    adv_ref[0] = inv1 * (1.0 - courant)
    adv_ref[1] = inv1 * courant
    adv_ref[2] = inv2 * (1.0 - courant)
    adv_ref[3] = inv2 * courant
    adv_ref[4] = inv1 * (relax_rate * (forcing - mean_ref[...]))

    def spread(ref, k, z, lane):
        return jnp.broadcast_to(ref[k, z : z + 1, lane], (SUB, LANES))

    dev = []
    for h in range(halves):
        lane = slice(h * LANES, (h + 1) * LANES)

        def at(z, i):
            base = (z * halves + h) * CX + i * SUB
            return slice(base, base + SUB)

        zero = jnp.zeros((SUB, LANES), jnp.float32)
        prev = [zero] * NI
        for z in range(CZ):
            a, b = spread(adv_ref, 0, z, lane), spread(adv_ref, 1, z, lane)
            d, e = spread(adv_ref, 4, z, lane), spread(coef_ref, 1, z, lane)
            f = [f_ref[at(z, i), :] for i in range(NI)]
            behind = [pltpu.roll(f[NI - 1], 1, axis=0)] + f[: NI - 1]
            prev = [(a * f[i] + b * behind[i]) + (d + e * prev[i]) for i in range(NI)]
            for i in range(NI):
                y_ref[at(z, i), :] = prev[i]
        after = [zero] * NI
        prev = [zero] * NI
        for z in range(CZ - 1, -1, -1):
            g = spread(coef_ref, 2, z, lane)
            a, b = spread(adv_ref, 2, z, lane), spread(adv_ref, 3, z, lane)
            e = spread(coef_ref, 4, z, lane)
            after = [y_ref[at(z, i), :] + g * after[i] for i in range(NI)]
            behind = [pltpu.roll(after[NI - 1], 1, axis=0)] + after[: NI - 1]
            prev = [(a * after[i] + b * behind[i]) + e * prev[i] for i in range(NI)]
            for i in range(NI):
                y_ref[at(z, i), :] = prev[i]
        after = [zero] * NI
        for z in range(CZ):
            g = spread(coef_ref, 5, z, lane)
            after = [y_ref[at(z, i), :] + g * after[i] for i in range(NI)]
            total, square = after[0], after[0] * after[0]
            for i in range(NI):
                y_ref[at(z, i), :] = after[i]
                if i > 0:
                    total = total + after[i]
                    square = square + after[i] * after[i]
            acc_ref[0, z * SUB : (z + 1) * SUB, :] = total
            acc_ref[1, z * SUB : (z + 1) * SUB, :] = square
        acc_ref[:, CZ * SUB :, :] = jnp.zeros((2, (ZP - CZ) * SUB, LANES), jnp.float32)
        sums = []
        for k in range(2):
            part = acc_ref[k, pl.ds(0, ZP, stride=SUB), :]
            for s in range(1, SUB):
                part = part + acc_ref[k, pl.ds(s, ZP, stride=SUB), :]
            sums.append(part * (1.0 / CX))
        mean0, sq0 = mean_ref[:, lane], sq_ref[:, lane]
        mean1, sq1 = sums
        dev.append(jnp.concatenate([mean1 - mean0, (sq1 - mean1 * mean1) - (sq0 - mean0 * mean0)], axis=0))
    x = jnp.concatenate(dev, axis=1)
    tend_ref[...] = dot(x, w, ((0,), (0,)))


def store_kernel(y_ref, crm_ref):
    slots = crm_ref.shape[1] // CX
    halves = slots // LANES

    def column(x, carry):
        place = (x % NI) * SUB + x // NI
        for h in range(halves):
            lane = pl.multiple_of(x * slots + h * LANES, LANES)
            for t in range(ZP // TZ):
                rows = min(TZ, CZ - t * TZ)
                first = (t * TZ * halves + h) * CX + place
                v = y_ref[pl.ds(first, rows, stride=halves * CX), :]
                crm_ref[t * TZ : t * TZ + rows, pl.ds(lane, LANES)] = v.astype(jnp.bfloat16)
        return carry

    lax.fori_loop(0, CX, column, 0)


def finish_kernel(moved_ref, take_ref, back_ref, out_ref):
    out_ref[:, 2 * L :] = moved_ref[:, 2 * L :]
    out_ref[:, : 2 * L] = moved_ref[:, : 2 * L] + dot(take_ref[...], back_ref[...], ((1,), (0,)))


def cost(us):
    return pl.CostEstimate(flops=0, bytes_accessed=int(us * 3.0e6), transcendentals=0)


def shards(state, owners, orient, crm_state, active_levels, vertical_map, diffusion):
    f32 = jnp.float32
    n_tiles = lax.axis_size("cols")
    per_tile = state.shape[1]
    width = state.shape[2]
    cap_slots = max(2, 2 * per_tile // n_tiles)
    slots = n_tiles * cap_slots
    rows_f = CZ * CX * slots // LANES
    tile = state[0]
    low = from_behind(tile[per_tile - TW :], "edge", 1)
    high = from_behind(tile[:TW], "edge", -1)
    put, take = call(
        functools.partial(slots_kernel, cap_slots),
        (jax.ShapeDtypeStruct((slots, per_tile), f32), jax.ShapeDtypeStruct((per_tile, slots), f32)),
        (owners[0],),
        cost=cost(0.6),
    )
    vmem = pl.BlockSpec(memory_space=pltpu.VMEM)
    smem = pl.BlockSpec(memory_space=pltpu.SMEM)
    moved, outgoing = call(
        edge_kernel,
        (jax.ShapeDtypeStruct((per_tile, width), f32), jax.ShapeDtypeStruct((slots, 2 * L), f32)),
        (tile, low, high, orient[0], put),
        in_specs=[vmem, vmem, vmem, smem, vmem],
        cost=cost(1),
    )
    received = lax.all_to_all(
        outgoing.reshape(n_tiles, cap_slots, 2 * L), "cols", split_axis=0, concat_axis=0, tiled=True
    ).reshape(slots, 2 * L)
    prepared = call(
        prepare_kernel,
        (
            pltpu.VMEM((rows_f, LANES), f32),
            pltpu.VMEM((ZP, slots), f32),
            pltpu.VMEM((ZP, slots), f32),
            pltpu.VMEM((6, ZP, slots), f32),
            pltpu.VMEM((2 * ZP, 2 * L), f32),
        ),
        (crm_state[0, 0], active_levels[0], diffusion, vertical_map),
        in_specs=[vmem, vmem, smem, vmem],
        cost=cost(4),
    )
    tend, after = call(
        physics_kernel,
        (jax.ShapeDtypeStruct((slots, 2 * L), f32), pltpu.VMEM((rows_f, LANES), f32)),
        (received, *prepared),
        scratch=(pltpu.VMEM((5, ZP, slots), f32), pltpu.VMEM((2, ZP * SUB, LANES), f32)),
        cost=cost(5),
    )
    returned = lax.all_to_all(
        tend.reshape(n_tiles, cap_slots, 2 * L), "cols", split_axis=0, concat_axis=0, tiled=True
    ).reshape(slots, 2 * L)
    crm_new = call(
        store_kernel,
        jax.ShapeDtypeStruct((CZ, CX * slots), jnp.bfloat16),
        (after,),
        cost=cost(3),
    )
    new_state = call(
        finish_kernel,
        jax.ShapeDtypeStruct((per_tile, width), f32),
        (moved, take, returned),
        cost=cost(0.7),
    )
    return (new_state[None], crm_new[None, None])


def solution(mesh):
    in_specs = (
        P("edge", "cols", None),
        P("edge", "cols", None),
        P("edge", "cols", None),
        P("edge", "cols", None, None),
        P("edge", "cols", None),
        P(),
        P(),
    )
    out_specs = (P("edge", "cols", None), P("edge", "cols", None, None))
    return jax.shard_map(shards, mesh=mesh, in_specs=in_specs, out_specs=out_specs, check_vma=False)
```

time: 86.6 us -> 50.1 us (0.58)
  other arithmetic: 25.3 us -> 0 us
  local copies, waits for them, and re-layouts: 35.7 us -> 14.6 us
  Pallas kernels: 0 us -> 18 us
  waiting for transfers between devices: 7.43 us -> 2.08 us
  between operations: 3.71 us -> 0.67 us
  starting transfers between devices: 11.8 us -> 14.2 us
  matrix products: 1.41 us -> 0 us
    another operation x60 -> x0, local copies, waits for them, and re-layouts: 27.5 us -> none  [tridiag(): return jnp.stack(solved, axis=0)]
    pallas_call x0 -> x6, Pallas kernels: none -> 18 us  [call(): pl.pallas_call(body, out_shape=outs, scratch_shapes=list(scratch), compil...]
    unnamed x95 -> x20, local copies, waits for them, and re-layouts: 4.33 us -> 13.1 us
    another operation x59 -> x0, other arithmetic: 8.31 us -> none
    all_to_all x2, waiting for transfers between devices: 7.42 us -> 0.01 us  [the longest x1 0.01 us: shards(): lax.all_to_all(outgoing.reshape(n_tiles, cap_slots, 2 * L), 'cols', split...]
    add x5 -> x0, other arithmetic: 4.05 us -> none  [the longest x1 2.71 us: physics(): field = field + relax_rate * (forcing - mean_before)[:, None, :]]
    reduce_sum x3 -> x0, other arithmetic: 3.25 us -> none  [the longest x1 1.19 us: physics(): mean_after = jnp.mean(field, axis=1)]
    sub x2 -> x0, other arithmetic: 2.86 us -> none  [physics(): field = field - courant[:, None, :] * (field - jnp.roll(field, 1, axis=1))]
  transfers between devices with their start and end apart: 4 -> 4, of which waited for: 1 -> 2; matrix products, arithmetic and copies ran while one was open for 42% -> 2% of each run, Pallas kernels for 0% -> 24%
where the time goes in v1:
time: 50.1 us; the launch traced here: 49.5 us
  Pallas kernels  18 us (36%)
  local copies, waits for them, and re-layouts  14.6 us (29%)
  starting transfers between devices  14.2 us (28%)
  waiting for transfers between devices  2.08 us (4%)
  between operations  0.67 us (1%)
    pallas_call x6, Pallas kernels, call(): pl.pallas_call(body, out_shape=outs, scratch_shapes=list(scratch), compil...  18 us
    unnamed x20, local copies, waits for them, and re-layouts  13.1 us
    all_to_all x1, starting transfers between devices, shards(): lax.all_to_all(tend.reshape(n_tiles, cap_slots, 2 * L), 'cols', split_axi...  6 us
    all_to_all x1, starting transfers between devices, shards(): lax.all_to_all(outgoing.reshape(n_tiles, cap_slots, 2 * L), 'cols', split...  5.81 us
    ppermute x2, starting transfers between devices, from_behind(): return lax.ppermute(value, axis, pairs)  2.41 us
    ppermute x2, waiting for transfers between devices, from_behind(): return lax.ppermute(value, axis, pairs)  2.08 us
  transfers between devices with their start and end apart: 4, of which 2 were waited for; matrix products, arithmetic and copies ran while one was open for 2% of the time, Pallas kernels for 24%

profile of v1, /device:TPU:0, one launch (start us, length us, event | category | flops | bytes accessed | tf_op | source)
XLA Modules:
  0.0 49.5 jit_solution(9251134804750312976)
XLA Ops:
  0.6 0.7 %slice_bitcast_fusion = (f32[8,512]{1,0:T(8,128)S(1)}, f32[8,512]{1,0:T(8,128)S(1)}) fusion(f32[1,128,512]{2,1,0:T(8,128)} %param.7), kind=kLoop, calls=%fused_computation | loop fusion | bytes 65536 | tf_op jit(solution)/shard_map/slice | solution.py:264
  1.4 2.4 %collective-permute-start.1 = (f32[8,512]{1,0:T(8,128)S(1)}, f32[8,512]{1,0:T(8,128)S(1)}, u32[]{:S(2)}, u32[]{:S(2)}) collective-permute-start(f32[8,512]{1,0:T(8,128)S(1)} %get-tuple-element.24), channel_id=1, source_target_pairs={{0,3},{1,0},{2,1},{3,2},{4,7},{5,4},{6,5},{7,6},{8,11},{9,8},{10,9... | collective-permute-start | bytes 49160 | tf_op jit(solution)/shard_map/ppermute | solution.py:50
  3.8 0.0 collective-permute-start
  3.8 0.8 %copy.9.owners_ref = s32[128,1]{1,0:T(8,128)S(1)} copy(s32[128,1]{0,1:T(1,128)} %bitcast.23) | data formatting | bytes 1024 | tf_op jit(solution)/shard_map/squeeze | solution.py:268
  4.5 0.3 shard_map.86
  4.9 0.4 collective-permute-done.1.high_ref
  5.2 1.7 %collective-permute-done.low_ref = f32[8,512]{1,0:T(8,128)S(1)} collective-permute-done((f32[8,512]{1,0:T(8,128)S(1)}, f32[8,512]{1,0:T(8,128)S(1)}, u32[]{:S(2)}, u32[]{:S(2)}) %collective-permute-start) | collective-permute-done | bytes 16416 | tf_op jit(solution)/shard_map/ppermute | solution.py:50
  6.9 0.9 %copy-done.5 = f32[1,128,512]{2,1,0:T(8,128)S(1)} copy-done((f32[1,128,512]{2,1,0:T(8,128)S(1)}, f32[1,128,512]{2,1,0:T(8,128)}, u32[]{:S(2)}) %copy-start.5) | copy-done | bytes 262168
  7.9 0.7 %copy-done.8 = s32[1,1,2]{2,1,0:T(1,128)S(1)} copy-done((s32[1,1,2]{2,1,0:T(1,128)S(1)}, s32[1,1,2]{2,1,0:T(1,128)}, u32[]{:S(2)}) %copy-start.8) | copy-done | bytes 32
  8.5 1.5 %shard_map.87 = (f32[128,512]{1,0:T(8,128)S(1)}, f32[256,128]{1,0:T(8,128)}) custom-call(f32[128,512]{1,0:T(8,128)S(1)} %bitcast.18, f32[8,512]{1,0:T(8,128)S(1)} %collective-permute-done.low_ref, f32[8,512]{1,0:T(8,128)S(1)} %collective-permute-done.1.high_ref, s32[1,2]{1,0:T(1,128)S(1)} %bitcast.20, f32[256,128]{1,0:T(8,128)S(1)} %get-tuple-element.13.put_ref), custom_call_target="tpu_custom_call" | custom-call | bytes 3000000 | tf_op jit(solution)/shard_map/pallas_call | solution.py:32
  10.0 5.8 %all-to-all-start = ((f32[8,32,128]{2,1,0:T(8,128)}), f32[8,32,128]{2,1,0:T(8,128)S(1)}, u32[]{:S(2)}, u32[]{:S(2)}) async-start(f32[8,32,128]{2,1,0:T(8,128)} %bitcast.5), calls=%async_computation | async-start | bytes 262144 | tf_op jit(solution)/shard_map/all_to_all | solution.py:280
  15.9 1.6 %copy-done.4 = bf16[1,1,58,16384]{3,2,1,0:T(8,128)(2,1)S(1)} copy-done((bf16[1,1,58,16384]{3,2,1,0:T(8,128)(2,1)S(1)}, bf16[1,1,58,16384]{3,2,1,0:T(8,128)(2,1)}, u32[]{:S(2)}) %copy-start.4) | copy-done | bytes 1900568
  17.4 0.8 %copy-done.6 = f32[58,64]{1,0:T(8,128)S(1)} copy-done((f32[58,64]{1,0:T(8,128)S(1)}, f32[58,64]{1,0:T(8,128)}, u32[]{:S(2)}) %copy-start.6) | copy-done | bytes 14872
  18.2 0.7 %copy-done.7 = s32[1,1,256]{2,1,0:T(1,128)S(1)} copy-done((s32[1,1,256]{2,1,0:T(1,128)S(1)}, s32[1,1,256]{2,1,0:T(1,128)}, u32[]{:S(2)}) %copy-start.7) | copy-done | bytes 1048
  18.9 0.7 %copy-done.9 = f32[57]{0:T(128)S(1)} copy-done((f32[57]{0:T(128)S(1)}, f32[57]{0:T(128)}, u32[]{:S(2)}) %copy-start.9) | copy-done | bytes 252
  19.5 5.4 %shard_map.88 = (f32[7424,128]{1,0:T(8,128)S(1)}, f32[64,256]{1,0:T(8,128)S(1)}, f32[64,256]{1,0:T(8,128)S(1)}, f32[6,64,256]{2,1,0:T(8,128)S(1)}, f32[128,128]{1,0:T(8,128)S(1)}) custom-call(bf16[58,16384]{1,0:T(8,128)(2,1)S(1)} %bitcast.15, s32[1,256]{1,0:T(1,128)S(1)} %bitcast.19, f32[57]{0:T(128)S(1)} %copy-done.9, f32[58,64]{1,0:T(8,128)S(1)} %copy-done.6), custom_call_target="tpu_custom_call" | custom-call | bytes 12000000 | tf_op jit(solution)/shard_map/pallas_call | solution.py:32
  24.9 1.8 %copy-done = f32[7424,128]{1,0:T(8,128)} copy-done((f32[7424,128]{1,0:T(8,128)}, f32[7424,128]{1,0:T(8,128)S(1)}, u32[]{:S(2)}) %copy-start) | copy-done | bytes 3801112
  26.8 2.1 %copy-done.1 = f32[7424,128]{1,0:T(8,128)S(1)} copy-done((f32[7424,128]{1,0:T(8,128)S(1)}, f32[7424,128]{1,0:T(8,128)}, u32[]{:S(2)}) %copy-start.1) | copy-done | bytes 3801112
  28.8 3.8 %shard_map.89 = (f32[256,128]{1,0:T(8,128)}, f32[7424,128]{1,0:T(8,128)S(1)}) custom-call(f32[256,128]{1,0:T(8,128)S(1)} %bitcast.16, f32[7424,128]{1,0:T(8,128)S(1)} %copy-done.1, f32[64,256]{1,0:T(8,128)S(1)} %get-tuple-element.18.mean_ref, f32[64,256]{1,0:T(8,128)S(1)} %get-tuple-element.19.sq_ref, f32[6,64,256]{2,1,0:T(8,128)S(1)} %get-tuple-element.20.coef_ref, ...), custom_call_target="tpu_custom_call" | custom-call | bytes 15000000 | tf_op jit(solution)/shard_map/pallas_call | solution.py:32
  32.7 1.8 %copy-done.2 = f32[7424,128]{1,0:T(8,128)} copy-done((f32[7424,128]{1,0:T(8,128)}, f32[7424,128]{1,0:T(8,128)S(1)}, u32[]{:S(2)}) %copy-start.2) | copy-done | bytes 3801112
  34.5 6.0 %all-to-all-start.1 = ((f32[8,32,128]{2,1,0:T(8,128)}), f32[8,32,128]{2,1,0:T(8,128)S(1)}, u32[]{:S(2)}, u32[]{:S(2)}) async-start(f32[8,32,128]{2,1,0:T(8,128)} %bitcast.9), calls=%async_computation.1 | async-start | bytes 262144 | tf_op jit(solution)/shard_map/all_to_all | solution.py:303
  40.5 2.1 %copy-done.3 = f32[7424,128]{1,0:T(8,128)S(1)} copy-done((f32[7424,128]{1,0:T(8,128)S(1)}, f32[7424,128]{1,0:T(8,128)}, u32[]{:S(2)}) %copy-start.3) | copy-done | bytes 3801112
  42.6 6.0 %shard_map.91 = bf16[58,16384]{1,0:T(8,128)(2,1)} custom-call(f32[7424,128]{1,0:T(8,128)S(1)} %copy-done.3), custom_call_target="tpu_custom_call" | custom-call | bytes 9000000 | tf_op jit(solution)/shard_map/pallas_call | solution.py:32
  48.5 1.0 %shard_map.90 = f32[128,512]{1,0:T(8,128)} custom-call(f32[128,512]{1,0:T(8,128)S(1)} %get-tuple-element.14.moved_ref, f32[128,256]{1,0:T(8,128)S(1)} %get-tuple-element.15.take_ref, f32[256,128]{1,0:T(8,128)S(1)} %bitcast.17), custom_call_target="tpu_custom_call" | custom-call | bytes 2100000 | tf_op jit(solution)/shard_map/pallas_call | solution.py:32
  (12 shorter events, 0.0 us)
Async XLA Ops:
  1.4 3.9 %collective-permute-start.1 = (f32[8,512]{1,0:T(8,128)S(1)}, f32[8,512]{1,0:T(8,128)S(1)}, u32[]{:S(2)}, u32[]{:S(2)}) collective-permute-start(f32[8,512]{1,0:T(8,128)S(1)} %get-tuple-element.24), channel_id=1, source_target_pairs={{0,3},{1,0},{2,1},{3,2},{4,7},{5,4},{6,5},{7,6},{8,11},{9,8},{10,9... | collective-permute-start | bytes 49160 | tf_op jit(solution)/shard_map/ppermute | solution.py:50
  3.8 3.2 %collective-permute-start = (f32[8,512]{1,0:T(8,128)S(1)}, f32[8,512]{1,0:T(8,128)S(1)}, u32[]{:S(2)}, u32[]{:S(2)}) collective-permute-start(f32[8,512]{1,0:T(8,128)S(1)} %get-tuple-element.25), channel_id=1, source_target_pairs={{0,1},{1,2},{2,3},{3,0},{4,5},{5,6},{6,7},{7,4},{8,9},{9,10},{10,1... | collective-permute-start | bytes 49160 | tf_op jit(solution)/shard_map/ppermute | solution.py:50
  6.9 1.0 %copy-start.5 = (f32[1,128,512]{2,1,0:T(8,128)S(1)}, f32[1,128,512]{2,1,0:T(8,128)}, u32[]{:S(2)}) copy-start(f32[1,128,512]{2,1,0:T(8,128)} %param.7) | copy-start | bytes 786436
  7.9 0.7 %copy-start.8 = (s32[1,1,2]{2,1,0:T(1,128)S(1)}, s32[1,1,2]{2,1,0:T(1,128)}, u32[]{:S(2)}) copy-start(s32[1,1,2]{2,1,0:T(1,128)} %param.9) | copy-start | bytes 28
  10.0 16.7 %all-to-all-start = ((f32[8,32,128]{2,1,0:T(8,128)}), f32[8,32,128]{2,1,0:T(8,128)S(1)}, u32[]{:S(2)}, u32[]{:S(2)}) async-start(f32[8,32,128]{2,1,0:T(8,128)} %bitcast.5), calls=%async_computation | async-start | bytes 262144 | tf_op jit(solution)/shard_map/all_to_all | solution.py:280
  15.9 1.6 %copy-start.4 = (bf16[1,1,58,16384]{3,2,1,0:T(8,128)(2,1)S(1)}, bf16[1,1,58,16384]{3,2,1,0:T(8,128)(2,1)}, u32[]{:S(2)}) copy-start(bf16[1,1,58,16384]{3,2,1,0:T(8,128)(2,1)} %param.10) | copy-start | bytes 5701636
  17.4 0.8 %copy-start.6 = (f32[58,64]{1,0:T(8,128)S(1)}, f32[58,64]{1,0:T(8,128)}, u32[]{:S(2)}) copy-start(f32[58,64]{1,0:T(8,128)} %vm_ref.1) | copy-start | bytes 44548
  18.2 0.7 %copy-start.7 = (s32[1,1,256]{2,1,0:T(1,128)S(1)}, s32[1,1,256]{2,1,0:T(1,128)}, u32[]{:S(2)}) copy-start(s32[1,1,256]{2,1,0:T(1,128)} %param.11) | copy-start | bytes 3076
  18.9 0.7 %copy-start.9 = (f32[57]{0:T(128)S(1)}, f32[57]{0:T(128)}, u32[]{:S(2)}) copy-start(f32[57]{0:T(128)} %diff_ref.1) | copy-start | bytes 688
  24.9 1.8 %copy-start = (f32[7424,128]{1,0:T(8,128)}, f32[7424,128]{1,0:T(8,128)S(1)}, u32[]{:S(2)}) copy-start(f32[7424,128]{1,0:T(8,128)S(1)} %get-tuple-element.17.f_ref) | copy-start | bytes 11403268
  26.8 2.1 %copy-start.1 = (f32[7424,128]{1,0:T(8,128)S(1)}, f32[7424,128]{1,0:T(8,128)}, u32[]{:S(2)}) copy-start(f32[7424,128]{1,0:T(8,128)} %copy-done) | copy-start | bytes 11403268
  32.7 1.8 %copy-start.2 = (f32[7424,128]{1,0:T(8,128)}, f32[7424,128]{1,0:T(8,128)S(1)}, u32[]{:S(2)}) copy-start(f32[7424,128]{1,0:T(8,128)S(1)} %get-tuple-element.23.y_ref) | copy-start | bytes 11403268
  34.5 14.1 %all-to-all-start.1 = ((f32[8,32,128]{2,1,0:T(8,128)}), f32[8,32,128]{2,1,0:T(8,128)S(1)}, u32[]{:S(2)}, u32[]{:S(2)}) async-start(f32[8,32,128]{2,1,0:T(8,128)} %bitcast.9), calls=%async_computation.1 | async-start | bytes 262144 | tf_op jit(solution)/shard_map/all_to_all | solution.py:303
  40.5 2.1 %copy-start.3 = (f32[7424,128]{1,0:T(8,128)S(1)}, f32[7424,128]{1,0:T(8,128)}, u32[]{:S(2)}) copy-start(f32[7424,128]{1,0:T(8,128)} %copy-done.2) | copy-start | bytes 11403268

commit v2 on v1

v2 whole, which is shorter than its diff:
```python
import functools

import jax
import jax.numpy as jnp
from jax import lax
from jax.experimental import pallas as pl
from jax.experimental.pallas import tpu as pltpu
from jax.sharding import PartitionSpec as P

L = 64
CX = 64
CZ = 58
TW = 8
SUBSTEPS = 2
ZP = 64
LANES = 128
SUB = 8
NI = CX // SUB
TZ = 16

kappa_edge = 0.25
max_courant = 0.9
relax_rate = 0.5

HI = lax.Precision.HIGHEST


def call(body, outs, args, scratch=(), in_specs=None, out_specs=None, cost=None, limit=32 << 20, aliases=None):
    kw = {}
    if out_specs is not None:
        kw["out_specs"] = out_specs
    if in_specs is not None:
        kw["in_specs"] = in_specs
    return pl.pallas_call(
        body,
        out_shape=outs,
        scratch_shapes=list(scratch),
        compiler_params=pltpu.CompilerParams(vmem_limit_bytes=limit),
        cost_estimate=cost,
        input_output_aliases=aliases or {},
        **kw,
    )(*args)


def dot(a, b, dims):
    return lax.dot_general(a, b, (dims, ((), ())), precision=HI, preferred_element_type=jnp.float32)


def from_behind(value, axis, steps):
    count = lax.axis_size(axis)
    pairs = [(source, (source + steps) % count) for source in range(count)]
    return lax.ppermute(value, axis, pairs)


def split_dot(chosen, value):
    high = value.astype(jnp.bfloat16)
    low = (value - high.astype(jnp.float32)).astype(jnp.bfloat16)
    pick = lambda part: lax.dot_general(chosen, part, (((1,), (0,)), ((), ())), preferred_element_type=jnp.float32)
    return pick(high) + pick(low)


def slots_kernel(cap, state_hbm, owners_hbm, orient_hbm, tile_ref, put_ref, take_ref, flip_ref, own_ref, turn_ref, sems):
    per_tile = owners_hbm.shape[1]
    n_slots = put_ref.shape[0]
    copies = [
        pltpu.make_async_copy(owners_hbm, own_ref, sems.at[0]),
        pltpu.make_async_copy(orient_hbm, turn_ref, sems.at[1]),
        pltpu.make_async_copy(state_hbm, tile_ref, sems.at[2]),
    ]
    for copy in copies:
        copy.start()
    row = lax.broadcasted_iota(jnp.int32, (per_tile, per_tile), 0)
    col = lax.broadcasted_iota(jnp.int32, (per_tile, per_tile), 1)
    q_down = lax.broadcasted_iota(jnp.int32, (n_slots, per_tile), 0)
    q_across = lax.broadcasted_iota(jnp.int32, (per_tile, n_slots), 1)
    copies[0].wait()
    across = jnp.broadcast_to(own_ref[...], (per_tile, per_tile))
    down = across.T
    same = down == across
    before_col = jnp.where(same & (row < col), 1.0, 0.0)
    before_row = jnp.where(same & (col < row), 1.0, 0.0)
    rank_across = jnp.sum(before_col, axis=0, keepdims=True).astype(jnp.int32)
    rank_down = jnp.sum(before_row, axis=1, keepdims=True).astype(jnp.int32)
    slot_across = across[0:1, :] * cap + rank_across
    slot_down = down[:, 0:1] * cap + rank_down
    put_ref[...] = jnp.where(q_down == slot_across, 1.0, 0.0).astype(jnp.bfloat16)
    take_ref[...] = jnp.where(q_across == slot_down, 1.0, 0.0).astype(jnp.bfloat16)
    copies[1].wait()
    for k in range(2):
        flip_ref[k] = jnp.broadcast_to(turn_ref[0:1, k : k + 1], (TW, LANES))
    copies[2].wait()


def edge_kernel(tile_ref, low_ref, high_ref, flip_ref, put_ref, moved_ref, out_ref):
    per_tile, width = tile_ref.shape

    def turned(ref, k):
        value = ref[...]
        back = jnp.concatenate([value[TW - 1 - w : TW - w] for w in range(TW)], axis=0)
        flip = jnp.concatenate([flip_ref[k]] * (width // LANES), axis=1)
        return jnp.where(flip == 1, back, value)

    low = turned(low_ref, 0)
    high = turned(high_ref, 1)
    tiles = tile_ref[...]
    below = jnp.concatenate([low, tiles[: per_tile - TW]], axis=0)
    above = jnp.concatenate([tiles[TW:], high], axis=0)
    moved = tiles + kappa_edge * ((above + below) - 2.0 * tiles)
    out_ref[...] = split_dot(put_ref[...], moved[:, : 2 * L])
    moved_ref[...] = moved


def rows_from_levels(flipped):
    n = 2 * SUB * TZ
    a = lax.broadcasted_iota(jnp.int32, (n, n), 1 if flipped else 0)
    b = lax.broadcasted_iota(jnp.int32, (n, n), 0 if flipped else 1)
    z, p, s = a >> 4, (a >> 3) & 1, a & 7
    return jnp.where(b == p * (SUB * TZ) + s * TZ + z, 1.0, 0.0).astype(jnp.bfloat16)


def prepare_kernel(
    crm_hbm, active_hbm, diff_hbm, vm_hbm, f_ref, mean_ref, sq_ref, coef_ref, w_ref, crm_ref, act_ref, diff_ref, vm_ref, sems
):
    slots = active_hbm.shape[1]
    copies = [
        pltpu.make_async_copy(active_hbm, act_ref, sems.at[0]),
        pltpu.make_async_copy(diff_hbm, diff_ref, sems.at[1]),
        pltpu.make_async_copy(vm_hbm, vm_ref, sems.at[2]),
        pltpu.make_async_copy(crm_hbm, crm_ref, sems.at[3]),
    ]
    for copy in copies:
        copy.start()
    order = rows_from_levels(False)
    coef_ref[...] = jnp.zeros_like(coef_ref)
    w_ref[...] = jnp.zeros_like(w_ref)
    copies[0].wait()
    copies[1].wait()
    active = act_ref[...]
    nothing = jnp.zeros((1, slots), jnp.float32)

    def link(i):
        if i < 0 or i >= CZ - 1:
            return nothing
        return jnp.where(i + 1 < active, diff_ref[i], 0.0)

    up, down = nothing, nothing
    for z in range(CZ):
        lower, upper = link(z - 1), link(z)
        up = 1.0 / (1.0 + lower + upper - lower * (lower * up))
        coef_ref[0, z : z + 1, :] = up
        coef_ref[1, z : z + 1, :] = lower * up
        coef_ref[2, z : z + 1, :] = upper * up
        y = CZ - 1 - z
        lower, upper = link(y - 1), link(y)
        down = 1.0 / (1.0 + lower + upper - upper * (upper * down))
        coef_ref[3, y : y + 1, :] = down
        coef_ref[4, y : y + 1, :] = upper * down
        coef_ref[5, y : y + 1, :] = lower * down
    copies[2].wait()
    pad = jnp.zeros((CZ, L), jnp.float32)
    w_ref[0:CZ, :] = jnp.concatenate([vm_ref[...], pad], axis=1)
    w_ref[ZP : ZP + CZ, :] = jnp.concatenate([pad, vm_ref[...]], axis=1)

    copies[3].wait()
    for t in range(ZP // TZ):
        rows = min(TZ, CZ - t * TZ)
        total = jnp.zeros((TZ, slots), jnp.float32)
        square = jnp.zeros((TZ, slots), jnp.float32)
        for p in range(NI // 2):
            parts = []
            for i in (2 * p, 2 * p + 1):
                for s in range(SUB):
                    x = s * NI + i
                    v = crm_ref[t * TZ : t * TZ + rows, x * slots : (x + 1) * slots]
                    wide = v.astype(jnp.float32)
                    if rows < TZ:
                        wide = jnp.concatenate([wide, jnp.zeros((TZ - rows, slots), jnp.float32)], axis=0)
                        v = wide.astype(jnp.bfloat16)
                    total = total + wide
                    square = square + wide * wide
                    parts.append(v)
            turned = lax.dot_general(
                order, jnp.concatenate(parts, axis=0), (((1,), (0,)), ((), ())), preferred_element_type=jnp.float32
            ).astype(jnp.bfloat16)
            for z in range(rows):
                base = (t * TZ + z) * CX + p * 2 * SUB
                f_ref[base : base + 2 * SUB, :] = turned[z * 2 * SUB : (z + 1) * 2 * SUB]
        mean_ref[t * TZ : (t + 1) * TZ, :] = total * (1.0 / CX)
        sq_ref[t * TZ : (t + 1) * TZ, :] = square * (1.0 / CX)


def physics_kernel(cols_ref, f_ref, mean_ref, sq_ref, coef_ref, w_ref, tend_ref, y_ref, g_ref, adv_ref, acc_ref):
    slots = cols_ref.shape[0]
    halves = slots // LANES
    w = w_ref[...]
    mapped = dot(w, cols_ref[...], ((1,), (1,)))
    forcing = mapped[0:ZP]
    courant = max_courant * jax.nn.sigmoid(mapped[ZP:])
    inv1 = coef_ref[0]
    inv2 = coef_ref[3]
    adv_ref[0] = inv1 * (1.0 - courant)
    adv_ref[1] = inv1 * courant
    adv_ref[2] = inv2 * (1.0 - courant)
    adv_ref[3] = inv2 * courant
    adv_ref[4] = inv1 * (relax_rate * (forcing - mean_ref[...]))

    def spread(ref, k, z, lane):
        return jnp.broadcast_to(ref[k, z : z + 1, lane], (SUB, LANES))

    dev = []
    for h in range(halves):
        lane = slice(h * LANES, (h + 1) * LANES)

        def at(z, i, n=1):
            base = z * CX + i * SUB
            return slice(base, base + n * SUB)

        zero = jnp.zeros((SUB, LANES), jnp.float32)
        prev = [zero] * NI
        for z in range(CZ):
            a, b = spread(adv_ref, 0, z, lane), spread(adv_ref, 1, z, lane)
            d, e = spread(adv_ref, 4, z, lane), spread(coef_ref, 1, z, lane)
            f = []
            for i in range(0, NI, 2):
                pair = f_ref[at(z, i, 2), lane].astype(jnp.float32)
                f += [pair[:SUB], pair[SUB:]]
            behind = [pltpu.roll(f[NI - 1], 1, axis=0)] + f[: NI - 1]
            prev = [(a * f[i] + b * behind[i]) + (d + e * prev[i]) for i in range(NI)]
            for i in range(NI):
                g_ref[at(z, i), lane] = prev[i]
        after = [zero] * NI
        prev = [zero] * NI
        for z in range(CZ - 1, -1, -1):
            g = spread(coef_ref, 2, z, lane)
            a, b = spread(adv_ref, 2, z, lane), spread(adv_ref, 3, z, lane)
            e = spread(coef_ref, 4, z, lane)
            after = [g_ref[at(z, i), lane] + g * after[i] for i in range(NI)]
            behind = [pltpu.roll(after[NI - 1], 1, axis=0)] + after[: NI - 1]
            prev = [(a * after[i] + b * behind[i]) + e * prev[i] for i in range(NI)]
            for i in range(NI):
                g_ref[at(z, i), lane] = prev[i]
        after = [zero] * NI
        for z in range(CZ):
            g = spread(coef_ref, 5, z, lane)
            after = [g_ref[at(z, i), lane] + g * after[i] for i in range(NI)]
            total, square = after[0], after[0] * after[0]
            for i in range(1, NI):
                total = total + after[i]
                square = square + after[i] * after[i]
            for i in range(0, NI, 2):
                y_ref[at(z, i, 2), lane] = jnp.concatenate(after[i : i + 2], axis=0).astype(jnp.bfloat16)
            acc_ref[0, z * SUB : (z + 1) * SUB, :] = total
            acc_ref[1, z * SUB : (z + 1) * SUB, :] = square
        acc_ref[:, CZ * SUB :, :] = jnp.zeros((2, (ZP - CZ) * SUB, LANES), jnp.float32)
        sums = []
        for k in range(2):
            part = acc_ref[k, pl.ds(0, ZP, stride=SUB), :]
            for s in range(1, SUB):
                part = part + acc_ref[k, pl.ds(s, ZP, stride=SUB), :]
            sums.append(part * (1.0 / CX))
        mean0, sq0 = mean_ref[:, lane], sq_ref[:, lane]
        mean1, sq1 = sums
        dev.append(jnp.concatenate([mean1 - mean0, (sq1 - mean1 * mean1) - (sq0 - mean0 * mean0)], axis=0))
    x = jnp.concatenate(dev, axis=1)
    tend_ref[...] = dot(x, w, ((0,), (0,)))


def store_kernel(y_ref, crm_hbm, crm_ref, sems):
    slots = crm_hbm.shape[1] // CX
    order = rows_from_levels(True)
    copies = []
    for p in range(NI // 2):
        for t in range(ZP // TZ):
            rows = min(TZ, CZ - t * TZ)
            parts = [y_ref[(t * TZ + z) * CX + p * 2 * SUB : (t * TZ + z) * CX + (p + 1) * 2 * SUB, :] for z in range(rows)]
            if rows < TZ:
                parts.append(jnp.zeros(((TZ - rows) * 2 * SUB, slots), jnp.bfloat16))
            turned = lax.dot_general(
                order, jnp.concatenate(parts, axis=0), (((1,), (0,)), ((), ())), preferred_element_type=jnp.float32
            ).astype(jnp.bfloat16)
            for i in range(2):
                for s in range(SUB):
                    x = s * NI + 2 * p + i
                    k = (i * SUB + s) * TZ
                    crm_ref[t * TZ : t * TZ + rows, x * slots : (x + 1) * slots] = turned[k : k + rows]
        for s in range(SUB):
            here = pl.ds((s * NI + 2 * p) * slots, 2 * slots)
            copy = pltpu.make_async_copy(crm_ref.at[:, here], crm_hbm.at[:, here], sems.at[p * SUB + s])
            copy.start()
            copies.append(copy)
    for copy in copies:
        copy.wait()


def finish_kernel(moved_ref, take_ref, back_ref, out_ref):
    out_ref[:, 2 * L :] = moved_ref[:, 2 * L :]
    out_ref[:, : 2 * L] = moved_ref[:, : 2 * L] + split_dot(take_ref[...], back_ref[...])


def cost(us):
    return pl.CostEstimate(flops=0, bytes_accessed=int(us * 3.0e6), transcendentals=0)


def far(x):
    return pltpu.with_memory_space_constraint(x, pltpu.HBM)


def shards(state, owners, orient, crm_state, active_levels, vertical_map, diffusion):
    f32, bf16 = jnp.float32, jnp.bfloat16
    n_tiles = lax.axis_size("cols")
    per_tile = state.shape[1]
    width = state.shape[2]
    cap_slots = max(2, 2 * per_tile // n_tiles)
    slots = n_tiles * cap_slots
    rows_f = CZ * CX
    hbm = pl.BlockSpec(memory_space=pltpu.HBM)
    dma = pltpu.SemaphoreType.DMA
    tile = state[0]
    low = from_behind(tile[per_tile - TW :], "edge", 1)
    high = from_behind(tile[:TW], "edge", -1)
    near, put, take, flip = call(
        functools.partial(slots_kernel, cap_slots),
        (
            pltpu.VMEM((per_tile, width), f32),
            pltpu.VMEM((slots, per_tile), bf16),
            pltpu.VMEM((per_tile, slots), bf16),
            pltpu.VMEM((2, TW, LANES), jnp.int32),
        ),
        (far(tile), far(owners.reshape(1, per_tile)), far(orient[0])),
        in_specs=[hbm] * 3,
        scratch=(pltpu.VMEM((1, per_tile), jnp.int32), pltpu.VMEM((1, 2), jnp.int32), dma((3,))),
        cost=cost(1),
    )
    moved, outgoing = call(
        edge_kernel,
        (pltpu.VMEM((per_tile, width), f32), jax.ShapeDtypeStruct((slots, 2 * L), f32)),
        (near, low, high, flip, put),
        cost=cost(1),
    )
    received = lax.all_to_all(
        outgoing.reshape(n_tiles, cap_slots, 2 * L), "cols", split_axis=0, concat_axis=0, tiled=True
    ).reshape(slots, 2 * L)
    prepared = call(
        prepare_kernel,
        (
            pltpu.VMEM((rows_f, slots), bf16),
            pltpu.VMEM((ZP, slots), f32),
            pltpu.VMEM((ZP, slots), f32),
            pltpu.VMEM((6, ZP, slots), f32),
            pltpu.VMEM((2 * ZP, 2 * L), f32),
        ),
        (far(crm_state[0, 0]), far(active_levels[0]), far(diffusion), far(vertical_map)),
        in_specs=[hbm] * 4,
        scratch=(
            pltpu.VMEM((CZ, CX * slots), bf16),
            pltpu.VMEM((1, slots), jnp.int32),
            pltpu.SMEM((CZ - 1,), f32),
            pltpu.VMEM((CZ, L), f32),
            dma((4,)),
        ),
        cost=cost(4),
    )
    tend, after = call(
        physics_kernel,
        (jax.ShapeDtypeStruct((slots, 2 * L), f32), pltpu.VMEM((rows_f, slots), bf16)),
        (received, *prepared),
        scratch=(
            pltpu.VMEM((rows_f, slots), f32),
            pltpu.VMEM((5, ZP, slots), f32),
            pltpu.VMEM((2, ZP * SUB, LANES), f32),
        ),
        cost=cost(5),
    )
    returned = lax.all_to_all(
        tend.reshape(n_tiles, cap_slots, 2 * L), "cols", split_axis=0, concat_axis=0, tiled=True
    ).reshape(slots, 2 * L)
    crm_new = call(
        store_kernel,
        jax.ShapeDtypeStruct((CZ, CX * slots), bf16),
        (after,),
        scratch=(pltpu.VMEM((CZ, CX * slots), bf16), dma((NI // 2 * SUB,))),
        out_specs=hbm,
        cost=cost(3),
    )
    new_state = call(
        finish_kernel,
        jax.ShapeDtypeStruct((per_tile, width), f32),
        (moved, take, returned),
        cost=cost(0.7),
    )
    return (new_state[None], crm_new[None, None])


def solution(mesh):
    in_specs = (
        P("edge", "cols", None),
        P("edge", "cols", None),
        P("edge", "cols", None),
        P("edge", "cols", None, None),
        P("edge", "cols", None),
        P(),
        P(),
    )
    out_specs = (P("edge", "cols", None), P("edge", "cols", None, None))
    return jax.shard_map(shards, mesh=mesh, in_specs=in_specs, out_specs=out_specs, check_vma=False)
```

time: 50.1 us -> 38.6 us (0.77)
  local copies, waits for them, and re-layouts: 14.6 us -> 3.51 us
  waiting for transfers between devices: 2.08 us -> 10.9 us
  Pallas kernels: 18 us -> 11.4 us
  starting transfers between devices: 14.2 us -> 11.6 us
    unnamed x20 -> x4, local copies, waits for them, and re-layouts: 13.1 us -> 2.77 us
    pallas_call x6, Pallas kernels: 18 us -> 11.4 us  [call(): pl.pallas_call(body, out_shape=outs, scratch_shapes=list(scratch), compil...]
    all_to_all x1, waiting for transfers between devices: 0.01 us -> 4.87 us  [shards(): lax.all_to_all(outgoing.reshape(n_tiles, cap_slots, 2 * L), 'cols', split...]
    all_to_all x1, waiting for transfers between devices: 0.01 us -> 3.88 us  [shards(): lax.all_to_all(tend.reshape(n_tiles, cap_slots, 2 * L), 'cols', split_axi...]
    all_to_all x1, starting transfers between devices: 6 us -> 3.37 us  [shards(): lax.all_to_all(tend.reshape(n_tiles, cap_slots, 2 * L), 'cols', split_axi...]
    squeeze x1 -> x0, local copies, waits for them, and re-layouts: 0.76 us -> none  [shards(): owners[0]]
  transfers between devices with their start and end apart: 4 -> 4, of which waited for: 2 -> 4; matrix products, arithmetic and copies ran while one was open for 2% -> 0% of each run, Pallas kernels for 24% -> 14%
where the time goes in v2:
time: 38.6 us; the launch traced here: 38 us
  starting transfers between devices  11.6 us (30%)
  Pallas kernels  11.4 us (30%)
  waiting for transfers between devices  10.9 us (28%)
  local copies, waits for them, and re-layouts  3.51 us (9%)
  between operations  0.68 us (2%)
    pallas_call x6, Pallas kernels, call(): pl.pallas_call(body, out_shape=outs, scratch_shapes=list(scratch), compil...  11.4 us
    all_to_all x1, starting transfers between devices, shards(): lax.all_to_all(outgoing.reshape(n_tiles, cap_slots, 2 * L), 'cols', split...  5.81 us
    all_to_all x1, waiting for transfers between devices, shards(): lax.all_to_all(outgoing.reshape(n_tiles, cap_slots, 2 * L), 'cols', split...  4.87 us
    all_to_all x1, waiting for transfers between devices, shards(): lax.all_to_all(tend.reshape(n_tiles, cap_slots, 2 * L), 'cols', split_axi...  3.88 us
    all_to_all x1, starting transfers between devices, shards(): lax.all_to_all(tend.reshape(n_tiles, cap_slots, 2 * L), 'cols', split_axi...  3.37 us
    unnamed x4, local copies, waits for them, and re-layouts  2.77 us
    ppermute x2, starting transfers between devices, from_behind(): return lax.ppermute(value, axis, pairs)  2.41 us
    ppermute x2, waiting for transfers between devices, from_behind(): return lax.ppermute(value, axis, pairs)  2.12 us
  transfers between devices with their start and end apart: 4, of which 4 were waited for; matrix products, arithmetic and copies ran while one was open for 0% of the time, Pallas kernels for 14%

profile of v2, /device:TPU:0, one launch (start us, length us, event | category | flops | bytes accessed | tf_op | source)
XLA Modules:
  0.0 38.0 jit_solution(4876504813170565883)
XLA Ops:
  0.6 0.7 %slice_bitcast_fusion = (f32[8,512]{1,0:T(8,128)S(1)}, f32[8,512]{1,0:T(8,128)S(1)}) fusion(f32[1,128,512]{2,1,0:T(8,128)} %param.7), kind=kLoop, calls=%fused_computation | loop fusion | bytes 65536 | tf_op jit(solution)/shard_map/slice | solution.py:320
  1.4 2.4 %collective-permute-start.1 = (f32[8,512]{1,0:T(8,128)S(1)}, f32[8,512]{1,0:T(8,128)S(1)}, u32[]{:S(2)}, u32[]{:S(2)}) collective-permute-start(f32[8,512]{1,0:T(8,128)S(1)} %get-tuple-element.28), channel_id=1, source_target_pairs={{0,3},{1,0},{2,1},{3,2},{4,7},{5,4},{6,5},{7,6},{8,11},{9,8},{10,9... | collective-permute-start | bytes 49160 | tf_op jit(solution)/shard_map/ppermute | solution.py:52
  3.8 0.0 collective-permute-start
  3.8 1.0 %shard_map.86 = (f32[128,512]{1,0:T(8,128)S(1)}, bf16[256,128]{1,0:T(8,128)(2,1)S(1)}, bf16[128,256]{1,0:T(8,128)(2,1)S(1)}, s32[2,8,128]{2,1,0:T(8,128)S(1)}) custom-call(f32[128,512]{1,0:T(8,128)} %bitcast.19, s32[1,128]{1,0:T(1,128)} %bitcast.22, s32[1,2]{1,0:T(1,128)} %bitcast.23), custom_call_target="tpu_custom_call" | custom-call | bytes 3000000 | tf_op jit(solution)/shard_map/pallas_call | solution.py:34
  4.8 0.4 %collective-permute-done.1.high_ref = f32[8,512]{1,0:T(8,128)S(1)} collective-permute-done((f32[8,512]{1,0:T(8,128)S(1)}, f32[8,512]{1,0:T(8,128)S(1)}, u32[]{:S(2)}, u32[]{:S(2)}) %collective-permute-start.1) | collective-permute-done | bytes 16416 | tf_op jit(solution)/shard_map/ppermute | solution.py:52
  5.2 1.7 %collective-permute-done.low_ref = f32[8,512]{1,0:T(8,128)S(1)} collective-permute-done((f32[8,512]{1,0:T(8,128)S(1)}, f32[8,512]{1,0:T(8,128)S(1)}, u32[]{:S(2)}, u32[]{:S(2)}) %collective-permute-start) | collective-permute-done | bytes 16416 | tf_op jit(solution)/shard_map/ppermute | solution.py:52
  6.9 0.9 %shard_map.87 = (f32[128,512]{1,0:T(8,128)S(1)}, f32[256,128]{1,0:T(8,128)}) custom-call(f32[128,512]{1,0:T(8,128)S(1)} %get-tuple-element.15.tile_ref, f32[8,512]{1,0:T(8,128)S(1)} %collective-permute-done.low_ref, f32[8,512]{1,0:T(8,128)S(1)} %collective-permute-done.1.high_ref, s32[2,8,128]{2,1,0:T(8,128)S(1)} %get-tuple-element.16.flip_ref, ...), custom_call_target="tpu_custom_call" | custom-call | bytes 3000000 | tf_op jit(solution)/shard_map/pallas_call | solution.py:34
  7.8 5.8 %all-to-all-start = ((f32[8,32,128]{2,1,0:T(8,128)}), f32[8,32,128]{2,1,0:T(8,128)S(1)}, u32[]{:S(2)}, u32[]{:S(2)}) async-start(f32[8,32,128]{2,1,0:T(8,128)} %bitcast.5), calls=%async_computation | async-start | bytes 262144 | tf_op jit(solution)/shard_map/all_to_all | solution.py:340
  13.6 2.5 %shard_map.88 = (bf16[3712,256]{1,0:T(8,128)(2,1)S(1)}, f32[64,256]{1,0:T(8,128)S(1)}, f32[64,256]{1,0:T(8,128)S(1)}, f32[6,64,256]{2,1,0:T(8,128)S(1)}, f32[128,128]{1,0:T(8,128)S(1)}) custom-call(bf16[58,16384]{1,0:T(8,128)(2,1)} %bitcast.17, s32[1,256]{1,0:T(1,128)} %bitcast.21, f32[57]{0:T(128)} %diff_hbm.1, f32[58,64]{1,0:T(8,128)} %vm_hbm.1), custom_call_target="tpu_custom_call" | custom-call | bytes 12000000 | tf_op jit(solution)/shard_map/pallas_call | solution.py:34
  16.1 4.9 %all-to-all-done = f32[8,32,128]{2,1,0:T(8,128)S(1)} async-done(((f32[8,32,128]{2,1,0:T(8,128)}), f32[8,32,128]{2,1,0:T(8,128)S(1)}, u32[]{:S(2)}, u32[]{:S(2)}) %all-to-all-start) | async-done | bytes 131104 | tf_op jit(solution)/shard_map/all_to_all | solution.py:340
  21.0 4.3 %shard_map.89 = (f32[256,128]{1,0:T(8,128)}, bf16[3712,256]{1,0:T(8,128)(2,1)S(1)}) custom-call(f32[256,128]{1,0:T(8,128)S(1)} %bitcast.15, bf16[3712,256]{1,0:T(8,128)(2,1)S(1)} %get-tuple-element.21.f_ref, f32[64,256]{1,0:T(8,128)S(1)} %get-tuple-element.22.mean_ref, f32[64,256]{1,0:T(8,128)S(1)} %get-tuple-element.23.sq_ref, ...), custom_call_target="tpu_custom_call" | custom-call | bytes 15000000 | tf_op jit(solution)/shard_map/pallas_call | solution.py:34
  25.2 0.0 copy-start
  25.2 1.2 %copy-done = bf16[3712,256]{1,0:T(8,128)(2,1)} copy-done((bf16[3712,256]{1,0:T(8,128)(2,1)}, bf16[3712,256]{1,0:T(8,128)(2,1)S(1)}, u32[]{:S(2)}) %copy-start) | copy-done | bytes 1900568
  26.5 3.4 %all-to-all-start.1 = ((f32[8,32,128]{2,1,0:T(8,128)}), f32[8,32,128]{2,1,0:T(8,128)S(1)}, u32[]{:S(2)}, u32[]{:S(2)}) async-start(f32[8,32,128]{2,1,0:T(8,128)} %bitcast.9), calls=%async_computation.1 | async-start | bytes 262144 | tf_op jit(solution)/shard_map/all_to_all | solution.py:374
  29.9 0.0 copy-start.1
  29.9 1.5 %copy-done.1 = bf16[3712,256]{1,0:T(8,128)(2,1)S(1)} copy-done((bf16[3712,256]{1,0:T(8,128)(2,1)S(1)}, bf16[3712,256]{1,0:T(8,128)(2,1)}, u32[]{:S(2)}) %copy-start.1) | copy-done | bytes 1900568
  31.4 1.9 %shard_map.91 = bf16[58,16384]{1,0:T(8,128)(2,1)} custom-call(bf16[3712,256]{1,0:T(8,128)(2,1)S(1)} %copy-done.1), custom_call_target="tpu_custom_call" | custom-call | bytes 9000000 | tf_op jit(solution)/shard_map/pallas_call | solution.py:34
  33.3 3.9 %all-to-all-done.1 = f32[8,32,128]{2,1,0:T(8,128)S(1)} async-done(((f32[8,32,128]{2,1,0:T(8,128)}), f32[8,32,128]{2,1,0:T(8,128)S(1)}, u32[]{:S(2)}, u32[]{:S(2)}) %all-to-all-start.1) | async-done | bytes 131104 | tf_op jit(solution)/shard_map/all_to_all | solution.py:374
  37.1 0.9 %shard_map.90 = f32[128,512]{1,0:T(8,128)} custom-call(f32[128,512]{1,0:T(8,128)S(1)} %get-tuple-element.18.moved_ref, bf16[128,256]{1,0:T(8,128)(2,1)S(1)} %get-tuple-element.19.take_ref, f32[256,128]{1,0:T(8,128)S(1)} %bitcast.16), custom_call_target="tpu_custom_call" | custom-call | bytes 2100000 | tf_op jit(solution)/shard_map/pallas_call | solution.py:34
Async XLA Ops:
  1.4 3.9 %collective-permute-start.1 = (f32[8,512]{1,0:T(8,128)S(1)}, f32[8,512]{1,0:T(8,128)S(1)}, u32[]{:S(2)}, u32[]{:S(2)}) collective-permute-start(f32[8,512]{1,0:T(8,128)S(1)} %get-tuple-element.28), channel_id=1, source_target_pairs={{0,3},{1,0},{2,1},{3,2},{4,7},{5,4},{6,5},{7,6},{8,11},{9,8},{10,9... | collective-permute-start | bytes 49160 | tf_op jit(solution)/shard_map/ppermute | solution.py:52
  3.8 3.2 %collective-permute-start = (f32[8,512]{1,0:T(8,128)S(1)}, f32[8,512]{1,0:T(8,128)S(1)}, u32[]{:S(2)}, u32[]{:S(2)}) collective-permute-start(f32[8,512]{1,0:T(8,128)S(1)} %get-tuple-element.29), channel_id=1, source_target_pairs={{0,1},{1,2},{2,3},{3,0},{4,5},{5,6},{6,7},{7,4},{8,9},{9,10},{10,1... | collective-permute-start | bytes 49160 | tf_op jit(solution)/shard_map/ppermute | solution.py:52
  7.8 13.1 %all-to-all-start = ((f32[8,32,128]{2,1,0:T(8,128)}), f32[8,32,128]{2,1,0:T(8,128)S(1)}, u32[]{:S(2)}, u32[]{:S(2)}) async-start(f32[8,32,128]{2,1,0:T(8,128)} %bitcast.5), calls=%async_computation | async-start | bytes 262144 | tf_op jit(solution)/shard_map/all_to_all | solution.py:340
  25.2 1.2 %copy-start = (bf16[3712,256]{1,0:T(8,128)(2,1)}, bf16[3712,256]{1,0:T(8,128)(2,1)S(1)}, u32[]{:S(2)}) copy-start(bf16[3712,256]{1,0:T(8,128)(2,1)S(1)} %get-tuple-element.27.y_ref) | copy-start | bytes 5701636
  26.5 10.7 %all-to-all-start.1 = ((f32[8,32,128]{2,1,0:T(8,128)}), f32[8,32,128]{2,1,0:T(8,128)S(1)}, u32[]{:S(2)}, u32[]{:S(2)}) async-start(f32[8,32,128]{2,1,0:T(8,128)} %bitcast.9), calls=%async_computation.1 | async-start | bytes 262144 | tf_op jit(solution)/shard_map/all_to_all | solution.py:374
  29.9 1.5 %copy-start.1 = (bf16[3712,256]{1,0:T(8,128)(2,1)S(1)}, bf16[3712,256]{1,0:T(8,128)(2,1)}, u32[]{:S(2)}) copy-start(bf16[3712,256]{1,0:T(8,128)(2,1)} %copy-done) | copy-start | bytes 5701636

commit v3 on v2

--- a/solution.py
+++ b/solution.py
@@ -52,16 +52,14 @@
     return lax.ppermute(value, axis, pairs)
 
 
-def split_dot(chosen, value):
+def split_dot(chosen, value, dims=((1,), (0,))):
     high = value.astype(jnp.bfloat16)
     low = (value - high.astype(jnp.float32)).astype(jnp.bfloat16)
-    pick = lambda part: lax.dot_general(chosen, part, (((1,), (0,)), ((), ())), preferred_element_type=jnp.float32)
+    pick = lambda part: lax.dot_general(chosen, part, (dims, ((), ())), preferred_element_type=jnp.float32)
     return pick(high) + pick(low)
 
 
-def slots_kernel(cap, state_hbm, owners_hbm, orient_hbm, tile_ref, put_ref, take_ref, flip_ref, own_ref, turn_ref, sems):
-    per_tile = owners_hbm.shape[1]
-    n_slots = put_ref.shape[0]
+def load_kernel(state_hbm, owners_hbm, orient_hbm, tile_ref, named_ref, flip_ref, own_ref, turn_ref, sems):
     copies = [
         pltpu.make_async_copy(owners_hbm, own_ref, sems.at[0]),
         pltpu.make_async_copy(orient_hbm, turn_ref, sems.at[1]),
@@ -69,29 +67,15 @@
     ]
     for copy in copies:
         copy.start()
-    row = lax.broadcasted_iota(jnp.int32, (per_tile, per_tile), 0)
-    col = lax.broadcasted_iota(jnp.int32, (per_tile, per_tile), 1)
-    q_down = lax.broadcasted_iota(jnp.int32, (n_slots, per_tile), 0)
-    q_across = lax.broadcasted_iota(jnp.int32, (per_tile, n_slots), 1)
     copies[0].wait()
-    across = jnp.broadcast_to(own_ref[...], (per_tile, per_tile))
-    down = across.T
-    same = down == across
-    before_col = jnp.where(same & (row < col), 1.0, 0.0)
-    before_row = jnp.where(same & (col < row), 1.0, 0.0)
-    rank_across = jnp.sum(before_col, axis=0, keepdims=True).astype(jnp.int32)
-    rank_down = jnp.sum(before_row, axis=1, keepdims=True).astype(jnp.int32)
-    slot_across = across[0:1, :] * cap + rank_across
-    slot_down = down[:, 0:1] * cap + rank_down
-    put_ref[...] = jnp.where(q_down == slot_across, 1.0, 0.0).astype(jnp.bfloat16)
-    take_ref[...] = jnp.where(q_across == slot_down, 1.0, 0.0).astype(jnp.bfloat16)
+    named_ref[...] = jnp.broadcast_to(own_ref[...].astype(jnp.float32), named_ref.shape)
     copies[1].wait()
     for k in range(2):
         flip_ref[k] = jnp.broadcast_to(turn_ref[0:1, k : k + 1], (TW, LANES))
     copies[2].wait()
 
 
-def edge_kernel(tile_ref, low_ref, high_ref, flip_ref, put_ref, moved_ref, out_ref):
+def edge_kernel(tile_ref, low_ref, high_ref, flip_ref, named_ref, moved_ref, out_ref):
     per_tile, width = tile_ref.shape
 
     def turned(ref, k):
@@ -106,7 +90,8 @@
     below = jnp.concatenate([low, tiles[: per_tile - TW]], axis=0)
     above = jnp.concatenate([tiles[TW:], high], axis=0)
     moved = tiles + kappa_edge * ((above + below) - 2.0 * tiles)
-    out_ref[...] = split_dot(put_ref[...], moved[:, : 2 * L])
+    out_ref[:per_tile, :] = moved[:, : 2 * L]
+    out_ref[per_tile:, :] = named_ref[...]
     moved_ref[...] = moved
 
 
@@ -189,9 +174,29 @@
         sq_ref[t * TZ : (t + 1) * TZ, :] = square * (1.0 / CX)
 
 
-def physics_kernel(cols_ref, f_ref, mean_ref, sq_ref, coef_ref, w_ref, tend_ref, y_ref, g_ref, adv_ref, acc_ref):
-    slots = cols_ref.shape[0]
+def physics_kernel(
+    all_ref, f_ref, mean_ref, sq_ref, coef_ref, w_ref, tend_ref, y_ref, g_ref, adv_ref, acc_ref, sel_ref, cols_ref
+):
+    n_tiles = all_ref.shape[0]
+    slots = f_ref.shape[1]
+    per_tile = all_ref.shape[1] - SUB
+    cap = slots // n_tiles
     halves = slots // LANES
+    me = lax.axis_index("cols").astype(jnp.float32)
+    named = jnp.concatenate([all_ref[t, per_tile : per_tile + 1, :] for t in range(n_tiles)], axis=0)
+    mine = jnp.where(named == me, 1.0, 0.0)
+    row = lax.broadcasted_iota(jnp.int32, (per_tile, per_tile), 0)
+    col = lax.broadcasted_iota(jnp.int32, (per_tile, per_tile), 1)
+    earlier = jnp.where(row < col, 1.0, 0.0).astype(jnp.bfloat16)
+    rank = lax.dot_general(
+        mine.astype(jnp.bfloat16), earlier, (((1,), (0,)), ((), ())), preferred_element_type=jnp.float32
+    )
+    rank = jnp.where(mine == 1.0, rank, -1.0)
+    place = lax.broadcasted_iota(jnp.int32, (cap, per_tile), 0).astype(jnp.float32)
+    for t in range(n_tiles):
+        chosen = jnp.where(rank[t : t + 1] == place, 1.0, 0.0).astype(jnp.bfloat16)
+        sel_ref[t] = chosen
+        cols_ref[t * cap : (t + 1) * cap, :] = split_dot(chosen, all_ref[t, :per_tile, :])
     w = w_ref[...]
     mapped = dot(w, cols_ref[...], ((1,), (1,)))
     forcing = mapped[0:ZP]
@@ -262,7 +267,11 @@
         mean1, sq1 = sums
         dev.append(jnp.concatenate([mean1 - mean0, (sq1 - mean1 * mean1) - (sq0 - mean0 * mean0)], axis=0))
     x = jnp.concatenate(dev, axis=1)
-    tend_ref[...] = dot(x, w, ((0,), (0,)))
+    tend = dot(x, w, ((0,), (0,)))
+    for t in range(n_tiles):
+        tend_ref[t * per_tile : (t + 1) * per_tile, :] = split_dot(
+            sel_ref[t], tend[t * cap : (t + 1) * cap], ((0,), (0,))
+        )
 
 
 def store_kernel(y_ref, crm_hbm, crm_ref, sems):
@@ -292,9 +301,9 @@
         copy.wait()
 
 
-def finish_kernel(moved_ref, take_ref, back_ref, out_ref):
+def finish_kernel(moved_ref, back_ref, out_ref):
     out_ref[:, 2 * L :] = moved_ref[:, 2 * L :]
-    out_ref[:, : 2 * L] = moved_ref[:, : 2 * L] + split_dot(take_ref[...], back_ref[...])
+    out_ref[:, : 2 * L] = moved_ref[:, : 2 * L] + back_ref[...]
 
 
 def cost(us):
@@ -318,12 +327,11 @@
     tile = state[0]
     low = from_behind(tile[per_tile - TW :], "edge", 1)
     high = from_behind(tile[:TW], "edge", -1)
-    near, put, take, flip = call(
-        functools.partial(slots_kernel, cap_slots),
+    near, named, flip = call(
+        load_kernel,
         (
             pltpu.VMEM((per_tile, width), f32),
-            pltpu.VMEM((slots, per_tile), bf16),
-            pltpu.VMEM((per_tile, slots), bf16),
+            pltpu.VMEM((SUB, per_tile), f32),
             pltpu.VMEM((2, TW, LANES), jnp.int32),
         ),
         (far(tile), far(owners.reshape(1, per_tile)), far(orient[0])),
@@ -333,13 +341,11 @@
     )
     moved, outgoing = call(
         edge_kernel,
-        (pltpu.VMEM((per_tile, width), f32), jax.ShapeDtypeStruct((slots, 2 * L), f32)),
-        (near, low, high, flip, put),
+        (pltpu.VMEM((per_tile, width), f32), jax.ShapeDtypeStruct((per_tile + SUB, 2 * L), f32)),
+        (near, low, high, flip, named),
         cost=cost(1),
     )
-    received = lax.all_to_all(
-        outgoing.reshape(n_tiles, cap_slots, 2 * L), "cols", split_axis=0, concat_axis=0, tiled=True
-    ).reshape(slots, 2 * L)
+    received = lax.all_gather(outgoing, "cols")
     prepared = call(
         prepare_kernel,
         (
@@ -362,18 +368,18 @@
     )
     tend, after = call(
         physics_kernel,
-        (jax.ShapeDtypeStruct((slots, 2 * L), f32), pltpu.VMEM((rows_f, slots), bf16)),
+        (jax.ShapeDtypeStruct((n_tiles * per_tile, 2 * L), f32), pltpu.VMEM((rows_f, slots), bf16)),
         (received, *prepared),
         scratch=(
             pltpu.VMEM((rows_f, slots), f32),
             pltpu.VMEM((5, ZP, slots), f32),
             pltpu.VMEM((2, ZP * SUB, LANES), f32),
+            pltpu.VMEM((n_tiles, cap_slots, per_tile), bf16),
+            pltpu.VMEM((slots, 2 * L), f32),
         ),
         cost=cost(5),
     )
-    returned = lax.all_to_all(
-        tend.reshape(n_tiles, cap_slots, 2 * L), "cols", split_axis=0, concat_axis=0, tiled=True
-    ).reshape(slots, 2 * L)
+    returned = lax.psum_scatter(tend, "cols", scatter_dimension=0, tiled=True)
     crm_new = call(
         store_kernel,
         jax.ShapeDtypeStruct((CZ, CX * slots), bf16),
@@ -385,7 +391,7 @@
     new_state = call(
         finish_kernel,
         jax.ShapeDtypeStruct((per_tile, width), f32),
-        (moved, take, returned),
+        (moved, returned),
         cost=cost(0.7),
     )
     return (new_state[None], crm_new[None, None])

time: 38.6 us -> 122 us (3.16)
  waiting for transfers between devices: 10.9 us -> 60.8 us
  blocking collectives: 0 us -> 31.8 us
  between operations: 0.68 us -> 14.1 us
  starting transfers between devices: 11.6 us -> 2.45 us
  local copies, waits for them, and re-layouts: 3.51 us -> 1.58 us
    reduce_scatter x0 -> x1, waiting for transfers between devices: none -> 60.8 us  [shards(): returned = lax.psum_scatter(tend, 'cols', scatter_dimension=0, tiled=True)]
    all_gather x0 -> x1, blocking collectives: none -> 31.8 us  [shards(): received = lax.all_gather(outgoing, 'cols')]
    all_to_all x2 -> x0, starting transfers between devices: 9.18 us -> none  [the longest x1 5.81 us: shards(): lax.all_to_all(outgoing.reshape(n_tiles, cap_slots, 2 * L), 'cols', split...]
    all_to_all x2 -> x0, waiting for transfers between devices: 8.74 us -> none  [the longest x1 4.87 us: shards(): lax.all_to_all(outgoing.reshape(n_tiles, cap_slots, 2 * L), 'cols', split...]
    ppermute x2, waiting for transfers between devices: 2.12 us -> 0.01 us  [from_behind(): return lax.ppermute(value, axis, pairs)]
    unnamed x4 -> x2, local copies, waits for them, and re-layouts: 2.77 us -> 0.84 us
  transfers between devices with their start and end apart: 4 -> 3, of which waited for: 4 -> 1; matrix products, arithmetic and copies ran while one was open for 0% -> 0% of each run, Pallas kernels for 14% -> 4%
where the time goes in v3:
time: 122 us
  waiting for transfers between devices  60.8 us (50%)
  blocking collectives  31.8 us (26%)
  between operations  14.1 us (12%)
  Pallas kernels  11.1 us (9%)
  starting transfers between devices  2.45 us (2%)
  local copies, waits for them, and re-layouts  1.58 us (1%)
    reduce_scatter x1, waiting for transfers between devices, shards(): returned = lax.psum_scatter(tend, 'cols', scatter_dimension=0, tiled=True)  60.8 us
    all_gather x1, blocking collectives, shards(): received = lax.all_gather(outgoing, 'cols')  31.8 us
    pallas_call x6, Pallas kernels, call(): pl.pallas_call(body, out_shape=outs, scratch_shapes=list(scratch), compil...  11.1 us
  transfers between devices with their start and end apart: 3, of which 1 were waited for; matrix products, arithmetic and copies ran while one was open for 0% of the time, Pallas kernels for 4%

profile of v3, /device:TPU:0, one launch (start us, length us, event | category | flops | bytes accessed | tf_op | source)
XLA Modules:
  0.0 121.9 jit_solution(5744838581390778756)
XLA Ops:
  7.2 0.0 reduce-scatter.2.cloned.1.call-start
  7.2 0.7 slice_bitcast_fusion
  8.0 2.4 %collective-permute-start.1 = (f32[8,512]{1,0:T(8,128)S(1)}, f32[8,512]{1,0:T(8,128)S(1)}, u32[]{:S(2)}, u32[]{:S(2)}) collective-permute-start(f32[8,512]{1,0:T(8,128)S(1)} %get-tuple-element.26), channel_id=1, source_target_pairs={{0,3},{1,0},{2,1},{3,2},{4,7},{5,4},{6,5},{7,6},{8,11},{9,8},{10,9... | collective-permute-start | bytes 49160 | tf_op jit(solution)/shard_map/ppermute | solution.py:52
  10.4 0.0 collective-permute-start
  10.4 1.0 shard_map.86
  11.4 2.5 %shard_map.88 = (bf16[3712,256]{1,0:T(8,128)(2,1)S(1)}, f32[64,256]{1,0:T(8,128)S(1)}, f32[64,256]{1,0:T(8,128)S(1)}, f32[6,64,256]{2,1,0:T(8,128)S(1)}, f32[128,128]{1,0:T(8,128)S(1)}) custom-call(bf16[58,16384]{1,0:T(8,128)(2,1)} %bitcast.13, s32[1,256]{1,0:T(1,128)} %bitcast.17, f32[57]{0:T(128)} %diff_hbm.1, f32[58,64]{1,0:T(8,128)} %vm_hbm.1), custom_call_target="tpu_custom_call" | custom-call | bytes 12000000 | tf_op jit(solution)/shard_map/pallas_call | solution.py:34
  13.8 0.0 collective-permute-done.1.high_ref
  13.9 0.0 collective-permute-done.low_ref
  13.9 0.1 shard_map.87
  13.9 31.8 %all-gather = f32[1088,128]{1,0:T(8,128)S(1)} all-gather(f32[136,128]{1,0:T(8,128)S(1)} %get-tuple-element.18), channel_id=2, replica_groups=mesh['cols'=8,'edge'=4] {'cols'}, dimensions={0}, use_global_device_ids=true | all-gather | bytes 626688 | tf_op jit(solution)/shard_map/all_gather | solution.py:348
  45.8 5.0 %shard_map.89 = (f32[1024,128]{1,0:T(8,128)}, bf16[3712,256]{1,0:T(8,128)(2,1)S(1)}) custom-call(f32[8,136,128]{2,1,0:T(8,128)S(1)} %bitcast.12, bf16[3712,256]{1,0:T(8,128)(2,1)S(1)} %get-tuple-element.19.f_ref, f32[64,256]{1,0:T(8,128)S(1)} %get-tuple-element.20.mean_ref, f32[64,256]{1,0:T(8,128)S(1)} %get-tuple-element.21.sq_ref, ...), custom_call_target="tpu_custom_call" | custom-call | bytes 15000000 | tf_op jit(solution)/shard_map/pallas_call | solution.py:34
  50.8 0.0 reduce-scatter.2.cloned.1.call-update
  50.8 1.9 %shard_map.91 = bf16[58,16384]{1,0:T(8,128)(2,1)} custom-call(bf16[3712,256]{1,0:T(8,128)(2,1)S(1)} %get-tuple-element.25.y_ref), custom_call_target="tpu_custom_call" | custom-call | bytes 9000000 | tf_op jit(solution)/shard_map/pallas_call | solution.py:34
  52.7 60.8 %reduce-scatter.2.cloned.1.call-done.back_ref = f32[128,128]{1,0:T(8,128)} async-done(((f32[1024,128]{1,0:T(8,128)}), f32[128,128]{1,0:T(8,128)}) %reduce-scatter.2.cloned.1.call-update) | async-done | bytes 65552 | tf_op jit(solution)/shard_map/reduce_scatter | solution.py:382
  113.5 0.0 copy-start
  113.5 0.8 copy-done
  114.3 0.7 shard_map.90
Async XLA Ops:
  7.2 106.3 %reduce-scatter.2.cloned.1.call-start = ((), (), s32[]{:S(2)}) async-start(), calls=%async_computation.1 | async-start | bytes 589824 | tf_op jit(solution)/shard_map/reduce_scatter | solution.py:382
  8.0 5.9 %collective-permute-start.1 = (f32[8,512]{1,0:T(8,128)S(1)}, f32[8,512]{1,0:T(8,128)S(1)}, u32[]{:S(2)}, u32[]{:S(2)}) collective-permute-start(f32[8,512]{1,0:T(8,128)S(1)} %get-tuple-element.26), channel_id=1, source_target_pairs={{0,3},{1,0},{2,1},{3,2},{4,7},{5,4},{6,5},{7,6},{8,11},{9,8},{10,9... | collective-permute-start | bytes 49160 | tf_op jit(solution)/shard_map/ppermute | solution.py:52
  10.4 3.5 %collective-permute-start = (f32[8,512]{1,0:T(8,128)S(1)}, f32[8,512]{1,0:T(8,128)S(1)}, u32[]{:S(2)}, u32[]{:S(2)}) collective-permute-start(f32[8,512]{1,0:T(8,128)S(1)} %get-tuple-element.27), channel_id=1, source_target_pairs={{0,1},{1,2},{2,3},{3,0},{4,5},{5,6},{6,7},{7,4},{8,9},{9,10},{10,1... | collective-permute-start | bytes 49160 | tf_op jit(solution)/shard_map/ppermute | solution.py:52
  113.5 0.8 copy-start
Sparse Core Ops, SparseCore 0:
  50.9 62.5 reduce-scatter.1

commit v4 on v2

--- a/solution.py
+++ b/solution.py
@@ -21,8 +21,6 @@
 kappa_edge = 0.25
 max_courant = 0.9
 relax_rate = 0.5
-
-HI = lax.Precision.HIGHEST
 
 
 def call(body, outs, args, scratch=(), in_specs=None, out_specs=None, cost=None, limit=32 << 20, aliases=None):
@@ -42,10 +40,6 @@
     )(*args)
 
 
-def dot(a, b, dims):
-    return lax.dot_general(a, b, (dims, ((), ())), precision=HI, preferred_element_type=jnp.float32)
-
-
 def from_behind(value, axis, steps):
     count = lax.axis_size(axis)
     pairs = [(source, (source + steps) % count) for source in range(count)]
@@ -53,10 +47,26 @@
 
 
 def split_dot(chosen, value):
-    high = value.astype(jnp.bfloat16)
-    low = (value - high.astype(jnp.float32)).astype(jnp.bfloat16)
+    high, low = parts_of(value)
     pick = lambda part: lax.dot_general(chosen, part, (((1,), (0,)), ((), ())), preferred_element_type=jnp.float32)
     return pick(high) + pick(low)
+
+
+def parts_of(value):
+    high = value.astype(jnp.bfloat16)
+    return high, (value - high.astype(jnp.float32)).astype(jnp.bfloat16)
+
+
+def rows_kernel(state_hbm, upper_ref, lower_ref, sems):
+    per_tile = state_hbm.shape[0]
+    copies = [
+        pltpu.make_async_copy(state_hbm.at[per_tile - TW :], upper_ref, sems.at[0]),
+        pltpu.make_async_copy(state_hbm.at[:TW], lower_ref, sems.at[1]),
+    ]
+    for copy in copies:
+        copy.start()
+    for copy in copies:
+        copy.wait()
 
 
 def slots_kernel(cap, state_hbm, owners_hbm, orient_hbm, tile_ref, put_ref, take_ref, flip_ref, own_ref, turn_ref, sems):
@@ -119,7 +129,7 @@
 
 
 def prepare_kernel(
-    crm_hbm, active_hbm, diff_hbm, vm_hbm, f_ref, mean_ref, sq_ref, coef_ref, w_ref, crm_ref, act_ref, diff_ref, vm_ref, sems
+    crm_hbm, active_hbm, diff_hbm, vm_hbm, f_ref, mean_ref, sq_ref, coef_ref, wa_ref, wb_ref, crm_ref, act_ref, diff_ref, vm_ref, sems
 ):
     slots = active_hbm.shape[1]
     copies = [
@@ -132,7 +142,6 @@
         copy.start()
     order = rows_from_levels(False)
     coef_ref[...] = jnp.zeros_like(coef_ref)
-    w_ref[...] = jnp.zeros_like(w_ref)
     copies[0].wait()
     copies[1].wait()
     active = act_ref[...]
@@ -158,8 +167,11 @@
         coef_ref[5, y : y + 1, :] = lower * down
     copies[2].wait()
     pad = jnp.zeros((CZ, L), jnp.float32)
-    w_ref[0:CZ, :] = jnp.concatenate([vm_ref[...], pad], axis=1)
-    w_ref[ZP : ZP + CZ, :] = jnp.concatenate([pad, vm_ref[...]], axis=1)
+    rest = jnp.zeros((ZP - CZ, 2 * L), jnp.float32)
+    both = [jnp.concatenate([vm_ref[...], pad], axis=1), rest, jnp.concatenate([pad, vm_ref[...]], axis=1), rest]
+    high, low = parts_of(jnp.concatenate(both, axis=0))
+    wa_ref[...] = jnp.concatenate([high, low, high], axis=1)
+    wb_ref[...] = jnp.concatenate([high, high, low], axis=0)
 
     copies[3].wait()
     for t in range(ZP // TZ):
@@ -189,25 +201,34 @@
         sq_ref[t * TZ : (t + 1) * TZ, :] = square * (1.0 / CX)
 
 
-def physics_kernel(cols_ref, f_ref, mean_ref, sq_ref, coef_ref, w_ref, tend_ref, y_ref, g_ref, adv_ref, acc_ref):
+def physics_kernel(
+    cols_ref, f_ref, mean_ref, sq_ref, coef_ref, wa_ref, wb_ref, tend_ref, y_ref, g_ref, adv_ref, sum_ref
+):
     slots = cols_ref.shape[0]
     halves = slots // LANES
-    w = w_ref[...]
-    mapped = dot(w, cols_ref[...], ((1,), (1,)))
-    forcing = mapped[0:ZP]
-    courant = max_courant * jax.nn.sigmoid(mapped[ZP:])
-    inv1 = coef_ref[0]
-    inv2 = coef_ref[3]
-    adv_ref[0] = inv1 * (1.0 - courant)
-    adv_ref[1] = inv1 * courant
-    adv_ref[2] = inv2 * (1.0 - courant)
-    adv_ref[3] = inv2 * courant
-    adv_ref[4] = inv1 * (relax_rate * (forcing - mean_ref[...]))
+    for h in range(halves):
+        lane = slice(h * LANES, (h + 1) * LANES)
+        high, low = parts_of(cols_ref[lane, :])
+        mapped = lax.dot_general(
+            wa_ref[...],
+            jnp.concatenate([high, high, low], axis=1),
+            (((1,), (1,)), ((), ())),
+            preferred_element_type=jnp.float32,
+        )
+        forcing = mapped[0:ZP]
+        courant = max_courant * jax.nn.sigmoid(mapped[ZP:])
+        inv1 = coef_ref[0, :, lane]
+        inv2 = coef_ref[3, :, lane]
+        adv_ref[0, :, lane] = inv1 * (1.0 - courant)
+        adv_ref[1, :, lane] = inv1 * courant
+        adv_ref[2, :, lane] = inv2 * (1.0 - courant)
+        adv_ref[3, :, lane] = inv2 * courant
+        adv_ref[4, :, lane] = inv1 * (relax_rate * (forcing - mean_ref[:, lane]))
+    sum_ref[:, CZ:, :] = jnp.zeros((2, ZP - CZ, slots), jnp.float32)
 
     def spread(ref, k, z, lane):
         return jnp.broadcast_to(ref[k, z : z + 1, lane], (SUB, LANES))
 
-    dev = []
     for h in range(halves):
         lane = slice(h * LANES, (h + 1) * LANES)
 
@@ -225,7 +246,7 @@
                 pair = f_ref[at(z, i, 2), lane].astype(jnp.float32)
                 f += [pair[:SUB], pair[SUB:]]
             behind = [pltpu.roll(f[NI - 1], 1, axis=0)] + f[: NI - 1]
-            prev = [(a * f[i] + b * behind[i]) + (d + e * prev[i]) for i in range(NI)]
+            prev = [((a * f[i] + d) + b * behind[i]) + e * prev[i] for i in range(NI)]
             for i in range(NI):
                 g_ref[at(z, i), lane] = prev[i]
         after = [zero] * NI
@@ -243,26 +264,22 @@
         for z in range(CZ):
             g = spread(coef_ref, 5, z, lane)
             after = [g_ref[at(z, i), lane] + g * after[i] for i in range(NI)]
-            total, square = after[0], after[0] * after[0]
-            for i in range(1, NI):
-                total = total + after[i]
-                square = square + after[i] * after[i]
+            total = [after[i] + after[i + 1] for i in range(0, NI, 2)]
+            square = [after[i] * after[i] + after[i + 1] * after[i + 1] for i in range(0, NI, 2)]
             for i in range(0, NI, 2):
                 y_ref[at(z, i, 2), lane] = jnp.concatenate(after[i : i + 2], axis=0).astype(jnp.bfloat16)
-            acc_ref[0, z * SUB : (z + 1) * SUB, :] = total
-            acc_ref[1, z * SUB : (z + 1) * SUB, :] = square
-        acc_ref[:, CZ * SUB :, :] = jnp.zeros((2, (ZP - CZ) * SUB, LANES), jnp.float32)
-        sums = []
-        for k in range(2):
-            part = acc_ref[k, pl.ds(0, ZP, stride=SUB), :]
-            for s in range(1, SUB):
-                part = part + acc_ref[k, pl.ds(s, ZP, stride=SUB), :]
-            sums.append(part * (1.0 / CX))
+            sum_ref[0, z : z + 1, lane] = jnp.sum((total[0] + total[1]) + (total[2] + total[3]), axis=0, keepdims=True)
+            sum_ref[1, z : z + 1, lane] = jnp.sum((square[0] + square[1]) + (square[2] + square[3]), axis=0, keepdims=True)
         mean0, sq0 = mean_ref[:, lane], sq_ref[:, lane]
-        mean1, sq1 = sums
-        dev.append(jnp.concatenate([mean1 - mean0, (sq1 - mean1 * mean1) - (sq0 - mean0 * mean0)], axis=0))
-    x = jnp.concatenate(dev, axis=1)
-    tend_ref[...] = dot(x, w, ((0,), (0,)))
+        mean1, sq1 = sum_ref[0, :, lane] * (1.0 / CX), sum_ref[1, :, lane] * (1.0 / CX)
+        change = jnp.concatenate([mean1 - mean0, (sq1 - mean1 * mean1) - (sq0 - mean0 * mean0)], axis=0)
+        high, low = parts_of(change)
+        tend_ref[lane, :] = lax.dot_general(
+            jnp.concatenate([high, low, high], axis=0),
+            wb_ref[...],
+            (((0,), (0,)), ((), ())),
+            preferred_element_type=jnp.float32,
+        )
 
 
 def store_kernel(y_ref, crm_hbm, crm_ref, sems):
@@ -292,9 +309,14 @@
         copy.wait()
 
 
-def finish_kernel(moved_ref, take_ref, back_ref, out_ref):
-    out_ref[:, 2 * L :] = moved_ref[:, 2 * L :]
-    out_ref[:, : 2 * L] = moved_ref[:, : 2 * L] + split_dot(take_ref[...], back_ref[...])
+def finish_kernel(moved_ref, take_ref, back_ref, out_hbm, part_ref, sems):
+    rest = pltpu.make_async_copy(moved_ref.at[:, 2 * L :], out_hbm.at[:, 2 * L :], sems.at[0])
+    rest.start()
+    part_ref[...] = moved_ref[:, : 2 * L] + split_dot(take_ref[...], back_ref[...])
+    first = pltpu.make_async_copy(part_ref, out_hbm.at[:, : 2 * L], sems.at[1])
+    first.start()
+    rest.wait()
+    first.wait()
 
 
 def cost(us):
@@ -316,8 +338,16 @@
     hbm = pl.BlockSpec(memory_space=pltpu.HBM)
     dma = pltpu.SemaphoreType.DMA
     tile = state[0]
-    low = from_behind(tile[per_tile - TW :], "edge", 1)
-    high = from_behind(tile[:TW], "edge", -1)
+    upper, lower = call(
+        rows_kernel,
+        (pltpu.VMEM((TW, width), f32), pltpu.VMEM((TW, width), f32)),
+        (far(tile),),
+        in_specs=[hbm],
+        scratch=(dma((2,)),),
+        cost=cost(0.5),
+    )
+    low = from_behind(upper, "edge", 1)
+    high = from_behind(lower, "edge", -1)
     near, put, take, flip = call(
         functools.partial(slots_kernel, cap_slots),
         (
@@ -347,7 +377,8 @@
             pltpu.VMEM((ZP, slots), f32),
             pltpu.VMEM((ZP, slots), f32),
             pltpu.VMEM((6, ZP, slots), f32),
-            pltpu.VMEM((2 * ZP, 2 * L), f32),
+            pltpu.VMEM((2 * ZP, 6 * L), bf16),
+            pltpu.VMEM((6 * ZP, 2 * L), bf16),
         ),
         (far(crm_state[0, 0]), far(active_levels[0]), far(diffusion), far(vertical_map)),
         in_specs=[hbm] * 4,
@@ -367,8 +398,9 @@
         scratch=(
             pltpu.VMEM((rows_f, slots), f32),
             pltpu.VMEM((5, ZP, slots), f32),
-            pltpu.VMEM((2, ZP * SUB, LANES), f32),
+            pltpu.VMEM((2, ZP, slots), f32),
         ),
+        aliases={1: 1},
         cost=cost(5),
     )
     returned = lax.all_to_all(
@@ -386,6 +418,8 @@
         finish_kernel,
         jax.ShapeDtypeStruct((per_tile, width), f32),
         (moved, take, returned),
+        scratch=(pltpu.VMEM((per_tile, 2 * L), f32), dma((2,))),
+        out_specs=hbm,
         cost=cost(0.7),
     )
     return (new_state[None], crm_new[None, None])

time: 38.6 us -> 37.2 us (0.964)
  local copies, waits for them, and re-layouts: 3.51 us -> 0 us
  starting transfers between devices: 11.6 us -> 12.4 us
  waiting for transfers between devices: 10.9 us -> 11.6 us
  Pallas kernels: 11.4 us -> 11.9 us
    unnamed x4 -> x0, local copies, waits for them, and re-layouts: 2.77 us -> none
    all_to_all x1, waiting for transfers between devices: 3.88 us -> 5.75 us  [shards(): lax.all_to_all(tend.reshape(n_tiles, cap_slots, 2 * L), 'cols', split_axi...]
    ppermute x2, waiting for transfers between devices: 2.12 us -> 0.41 us  [from_behind(): return lax.ppermute(value, axis, pairs)]
    slice x1 -> x0, local copies, waits for them, and re-layouts: 0.74 us -> none  [shards(): high = from_behind(tile[:TW], 'edge', -1)]
    all_to_all x1, starting transfers between devices: 5.81 us -> 6.53 us  [shards(): lax.all_to_all(outgoing.reshape(n_tiles, cap_slots, 2 * L), 'cols', split...]
    all_to_all x1, waiting for transfers between devices: 4.87 us -> 5.49 us  [shards(): lax.all_to_all(outgoing.reshape(n_tiles, cap_slots, 2 * L), 'cols', split...]
    pallas_call x6 -> x7, Pallas kernels: 11.4 us -> 11.9 us  [call(): pl.pallas_call(body, out_shape=outs, scratch_shapes=list(scratch), compil...]
  transfers between devices with their start and end apart: 4 -> 4, of which waited for: 4 -> 4; matrix products, arithmetic and copies ran while one was open for 0% -> 0% of each run, Pallas kernels for 14% -> 15%
where the time goes in v4:
time: 37.2 us; the launch traced here: 36.6 us
  starting transfers between devices  12.4 us (33%)
  Pallas kernels  11.9 us (32%)
  waiting for transfers between devices  11.6 us (31%)
  between operations  0.67 us (2%)
    pallas_call x7, Pallas kernels, call(): pl.pallas_call(body, out_shape=outs, scratch_shapes=list(scratch), compil...  11.9 us
    all_to_all x1, starting transfers between devices, shards(): lax.all_to_all(outgoing.reshape(n_tiles, cap_slots, 2 * L), 'cols', split...  6.53 us
    all_to_all x1, waiting for transfers between devices, shards(): lax.all_to_all(tend.reshape(n_tiles, cap_slots, 2 * L), 'cols', split_axi...  5.75 us
    all_to_all x1, waiting for transfers between devices, shards(): lax.all_to_all(outgoing.reshape(n_tiles, cap_slots, 2 * L), 'cols', split...  5.49 us
    all_to_all x1, starting transfers between devices, shards(): lax.all_to_all(tend.reshape(n_tiles, cap_slots, 2 * L), 'cols', split_axi...  3.37 us
    ppermute x2, starting transfers between devices, from_behind(): return lax.ppermute(value, axis, pairs)  2.52 us
  transfers between devices with their start and end apart: 4, of which 4 were waited for; matrix products, arithmetic and copies ran while one was open for 0% of the time, Pallas kernels for 15%

profile of v4, /device:TPU:0, one launch (start us, length us, event | category | flops | bytes accessed | tf_op | source)
XLA Modules:
  0.0 36.6 jit_solution(429159766976503902)
XLA Ops:
  0.6 0.8 %shard_map.87 = (f32[8,512]{1,0:T(8,128)S(1)}, f32[8,512]{1,0:T(8,128)S(1)}) custom-call(f32[128,512]{1,0:T(8,128)} %bitcast.15), custom_call_target="tpu_custom_call" | custom-call | bytes 1500000 | tf_op jit(solution)/shard_map/pallas_call | solution.py:32
  1.4 0.5 %collective-permute-start = (f32[8,512]{1,0:T(8,128)S(1)}, f32[8,512]{1,0:T(8,128)S(1)}, u32[]{:S(2)}, u32[]{:S(2)}) collective-permute-start(f32[8,512]{1,0:T(8,128)S(1)} %get-tuple-element.19), channel_id=1, source_target_pairs={{0,1},{1,2},{2,3},{3,0},{4,5},{5,6},{6,7},{7,4},{8,9},{9,10},{10,1... | collective-permute-start | bytes 49160 | tf_op jit(solution)/shard_map/ppermute | solution.py:46
  1.9 2.0 %collective-permute-start.1 = (f32[8,512]{1,0:T(8,128)S(1)}, f32[8,512]{1,0:T(8,128)S(1)}, u32[]{:S(2)}, u32[]{:S(2)}) collective-permute-start(f32[8,512]{1,0:T(8,128)S(1)} %get-tuple-element.20), channel_id=1, source_target_pairs={{0,3},{1,0},{2,1},{3,2},{4,7},{5,4},{6,5},{7,6},{8,11},{9,8},{10,9... | collective-permute-start | bytes 49160 | tf_op jit(solution)/shard_map/ppermute | solution.py:46
  3.9 1.0 %shard_map.86 = (f32[128,512]{1,0:T(8,128)S(1)}, bf16[256,128]{1,0:T(8,128)(2,1)S(1)}, bf16[128,256]{1,0:T(8,128)(2,1)S(1)}, s32[2,8,128]{2,1,0:T(8,128)S(1)}) custom-call(f32[128,512]{1,0:T(8,128)} %bitcast.16, s32[1,128]{1,0:T(1,128)} %bitcast.19, s32[1,2]{1,0:T(1,128)} %bitcast.20), custom_call_target="tpu_custom_call" | custom-call | bytes 3000000 | tf_op jit(solution)/shard_map/pallas_call | solution.py:32
  5.0 0.3 collective-permute-done.low_ref
  5.3 0.1 collective-permute-done.1.high_ref
  5.4 0.9 %shard_map.88 = (f32[128,512]{1,0:T(8,128)S(1)}, f32[256,128]{1,0:T(8,128)}) custom-call(f32[128,512]{1,0:T(8,128)S(1)} %get-tuple-element.18.tile_ref, f32[8,512]{1,0:T(8,128)S(1)} %collective-permute-done.low_ref, f32[8,512]{1,0:T(8,128)S(1)} %collective-permute-done.1.high_ref, s32[2,8,128]{2,1,0:T(8,128)S(1)} %get-tuple-element.21.flip_ref, ...), custom_call_target="tpu_custom_call" | custom-call | bytes 3000000 | tf_op jit(solution)/shard_map/pallas_call | solution.py:32
  6.2 6.5 %all-to-all-start = ((f32[8,32,128]{2,1,0:T(8,128)}), f32[8,32,128]{2,1,0:T(8,128)S(1)}, u32[]{:S(2)}, u32[]{:S(2)}) async-start(f32[8,32,128]{2,1,0:T(8,128)} %bitcast.3), calls=%async_computation | async-start | bytes 262144 | tf_op jit(solution)/shard_map/all_to_all | solution.py:370
  12.8 2.5 %shard_map.89 = (bf16[3712,256]{1,0:T(8,128)(2,1)S(1)}, f32[64,256]{1,0:T(8,128)S(1)}, f32[64,256]{1,0:T(8,128)S(1)}, f32[6,64,256]{2,1,0:T(8,128)S(1)}, bf16[12...) custom-call(bf16[58,16384]{1,0:T(8,128)(2,1)} %bitcast.13, s32[1,256]{1,0:T(1,128)} %bitcast.18, f32[57]{0:T(128)} %diff_hbm.1, ...), custom_call_target="tpu_custom_call" | custom-call | bytes 12000000 | tf_op jit(solution)/shard_map/pallas_call | solution.py:32
  15.2 5.5 %all-to-all-done = f32[8,32,128]{2,1,0:T(8,128)S(1)} async-done(((f32[8,32,128]{2,1,0:T(8,128)}), f32[8,32,128]{2,1,0:T(8,128)S(1)}, u32[]{:S(2)}, u32[]{:S(2)}) %all-to-all-start) | async-done | bytes 131104 | tf_op jit(solution)/shard_map/all_to_all | solution.py:370
  20.7 4.1 %shard_map.90 = (f32[256,128]{1,0:T(8,128)}, bf16[3712,256]{1,0:T(8,128)(2,1)S(1)}) custom-call(f32[256,128]{1,0:T(8,128)S(1)} %bitcast.12, bf16[3712,256]{1,0:T(8,128)(2,1)S(1)} %get-tuple-element.26.f_ref, f32[64,256]{1,0:T(8,128)S(1)} %get-tuple-element.27.mean_ref, f32[64,256]{1,0:T(8,128)S(1)} %get-tuple-element.28.sq_ref, ...), custom_call_target="tpu_custom_call", output_to_operand_aliasing={{1}: (1, {})} | custom-call | bytes 15000000 | tf_op jit(solution)/shard_map/pallas_call | solution.py:32
  24.8 3.4 %all-to-all-start.1 = ((f32[8,32,128]{2,1,0:T(8,128)}), f32[8,32,128]{2,1,0:T(8,128)S(1)}, u32[]{:S(2)}, u32[]{:S(2)}) async-start(f32[8,32,128]{2,1,0:T(8,128)} %bitcast.7), calls=%async_computation.1 | async-start | bytes 262144 | tf_op jit(solution)/shard_map/all_to_all | solution.py:406
  28.2 1.9 %shard_map.92 = bf16[58,16384]{1,0:T(8,128)(2,1)} custom-call(bf16[3712,256]{1,0:T(8,128)(2,1)S(1)} %get-tuple-element.33.y_ref), custom_call_target="tpu_custom_call" | custom-call | bytes 9000000 | tf_op jit(solution)/shard_map/pallas_call | solution.py:32
  30.0 5.7 %all-to-all-done.1 = f32[8,32,128]{2,1,0:T(8,128)S(1)} async-done(((f32[8,32,128]{2,1,0:T(8,128)}), f32[8,32,128]{2,1,0:T(8,128)S(1)}, u32[]{:S(2)}, u32[]{:S(2)}) %all-to-all-start.1) | async-done | bytes 131104 | tf_op jit(solution)/shard_map/all_to_all | solution.py:406
  35.8 0.8 %shard_map.91 = f32[128,512]{1,0:T(8,128)} custom-call(f32[128,512]{1,0:T(8,128)S(1)} %get-tuple-element.23.moved_ref, bf16[128,256]{1,0:T(8,128)(2,1)S(1)} %get-tuple-element.24.take_ref, f32[256,128]{1,0:T(8,128)S(1)} %bitcast.11), custom_call_target="tpu_custom_call" | custom-call | bytes 2100000 | tf_op jit(solution)/shard_map/pallas_call | solution.py:32
Async XLA Ops:
  1.4 3.9 %collective-permute-start = (f32[8,512]{1,0:T(8,128)S(1)}, f32[8,512]{1,0:T(8,128)S(1)}, u32[]{:S(2)}, u32[]{:S(2)}) collective-permute-start(f32[8,512]{1,0:T(8,128)S(1)} %get-tuple-element.19), channel_id=1, source_target_pairs={{0,1},{1,2},{2,3},{3,0},{4,5},{5,6},{6,7},{7,4},{8,9},{9,10},{10,1... | collective-permute-start | bytes 49160 | tf_op jit(solution)/shard_map/ppermute | solution.py:46
  1.9 3.5 %collective-permute-start.1 = (f32[8,512]{1,0:T(8,128)S(1)}, f32[8,512]{1,0:T(8,128)S(1)}, u32[]{:S(2)}, u32[]{:S(2)}) collective-permute-start(f32[8,512]{1,0:T(8,128)S(1)} %get-tuple-element.20), channel_id=1, source_target_pairs={{0,3},{1,0},{2,1},{3,2},{4,7},{5,4},{6,5},{7,6},{8,11},{9,8},{10,9... | collective-permute-start | bytes 49160 | tf_op jit(solution)/shard_map/ppermute | solution.py:46
  6.2 14.5 %all-to-all-start = ((f32[8,32,128]{2,1,0:T(8,128)}), f32[8,32,128]{2,1,0:T(8,128)S(1)}, u32[]{:S(2)}, u32[]{:S(2)}) async-start(f32[8,32,128]{2,1,0:T(8,128)} %bitcast.3), calls=%async_computation | async-start | bytes 262144 | tf_op jit(solution)/shard_map/all_to_all | solution.py:370
  24.8 11.0 %all-to-all-start.1 = ((f32[8,32,128]{2,1,0:T(8,128)}), f32[8,32,128]{2,1,0:T(8,128)S(1)}, u32[]{:S(2)}, u32[]{:S(2)}) async-start(f32[8,32,128]{2,1,0:T(8,128)} %bitcast.7), calls=%async_computation.1 | async-start | bytes 262144 | tf_op jit(solution)/shard_map/all_to_all | solution.py:406

commit v5 on v4

--- a/solution.py
+++ b/solution.py
@@ -226,50 +226,78 @@
         adv_ref[4, :, lane] = inv1 * (relax_rate * (forcing - mean_ref[:, lane]))
     sum_ref[:, CZ:, :] = jnp.zeros((2, ZP - CZ, slots), jnp.float32)
 
-    def spread(ref, k, z, lane):
-        return jnp.broadcast_to(ref[k, z : z + 1, lane], (SUB, LANES))
-
-    for h in range(halves):
-        lane = slice(h * LANES, (h + 1) * LANES)
-
-        def at(z, i, n=1):
-            base = z * CX + i * SUB
-            return slice(base, base + n * SUB)
-
-        zero = jnp.zeros((SUB, LANES), jnp.float32)
-        prev = [zero] * NI
-        for z in range(CZ):
-            a, b = spread(adv_ref, 0, z, lane), spread(adv_ref, 1, z, lane)
-            d, e = spread(adv_ref, 4, z, lane), spread(coef_ref, 1, z, lane)
-            f = []
-            for i in range(0, NI, 2):
-                pair = f_ref[at(z, i, 2), lane].astype(jnp.float32)
-                f += [pair[:SUB], pair[SUB:]]
-            behind = [pltpu.roll(f[NI - 1], 1, axis=0)] + f[: NI - 1]
-            prev = [((a * f[i] + d) + b * behind[i]) + e * prev[i] for i in range(NI)]
-            for i in range(NI):
-                g_ref[at(z, i), lane] = prev[i]
-        after = [zero] * NI
-        prev = [zero] * NI
-        for z in range(CZ - 1, -1, -1):
-            g = spread(coef_ref, 2, z, lane)
-            a, b = spread(adv_ref, 2, z, lane), spread(adv_ref, 3, z, lane)
-            e = spread(coef_ref, 4, z, lane)
-            after = [g_ref[at(z, i), lane] + g * after[i] for i in range(NI)]
-            behind = [pltpu.roll(after[NI - 1], 1, axis=0)] + after[: NI - 1]
-            prev = [(a * after[i] + b * behind[i]) + e * prev[i] for i in range(NI)]
-            for i in range(NI):
-                g_ref[at(z, i), lane] = prev[i]
-        after = [zero] * NI
-        for z in range(CZ):
-            g = spread(coef_ref, 5, z, lane)
-            after = [g_ref[at(z, i), lane] + g * after[i] for i in range(NI)]
-            total = [after[i] + after[i + 1] for i in range(0, NI, 2)]
-            square = [after[i] * after[i] + after[i + 1] * after[i + 1] for i in range(0, NI, 2)]
-            for i in range(0, NI, 2):
-                y_ref[at(z, i, 2), lane] = jnp.concatenate(after[i : i + 2], axis=0).astype(jnp.bfloat16)
-            sum_ref[0, z : z + 1, lane] = jnp.sum((total[0] + total[1]) + (total[2] + total[3]), axis=0, keepdims=True)
-            sum_ref[1, z : z + 1, lane] = jnp.sum((square[0] + square[1]) + (square[2] + square[3]), axis=0, keepdims=True)
+    lanes = [slice(h * LANES, (h + 1) * LANES) for h in range(halves)]
+    whole = CZ // SUB
+    zero = jnp.zeros((SUB, LANES), jnp.float32)
+    still = tuple(tuple(zero for _ in range(NI)) for _ in range(halves))
+
+    def group(ref, k, base):
+        return ref.at[k, pl.ds(base, SUB), :]
+
+    def spread(rows, u, lane):
+        return jnp.broadcast_to(rows[u : u + 1, lane], (SUB, LANES))
+
+    def at(base, u, i, n=1):
+        return pl.ds(pl.multiple_of(base * CX + (u * CX + i * SUB), n * SUB), n * SUB)
+
+    def rise(base, levels, carry):
+        prev = list(carry)
+        rows = [group(adv_ref, 0, base), group(adv_ref, 1, base), group(adv_ref, 4, base), group(coef_ref, 1, base)]
+        for u in levels:
+            for h, lane in enumerate(lanes):
+                a, b, d, e = [spread(r, u, lane) for r in rows]
+                f = []
+                for i in range(0, NI, 2):
+                    pair = f_ref[at(base, u, i, 2), lane].astype(jnp.float32)
+                    f += [pair[:SUB], pair[SUB:]]
+                behind = [pltpu.roll(f[NI - 1], 1, axis=0)] + f[: NI - 1]
+                prev[h] = tuple(((a * f[i] + d) + b * behind[i]) + e * prev[h][i] for i in range(NI))
+                for i in range(NI):
+                    g_ref[at(base, u, i), lane] = prev[h][i]
+        return tuple(prev)
+
+    def fall(base, levels, carry):
+        after, prev = list(carry[0]), list(carry[1])
+        rows = [group(coef_ref, 2, base), group(adv_ref, 2, base), group(adv_ref, 3, base), group(coef_ref, 4, base)]
+        for u in levels:
+            for h, lane in enumerate(lanes):
+                g, a, b, e = [spread(r, u, lane) for r in rows]
+                y = tuple(g_ref[at(base, u, i), lane] + g * after[h][i] for i in range(NI))
+                behind = (pltpu.roll(y[NI - 1], 1, axis=0),) + y[: NI - 1]
+                after[h] = y
+                prev[h] = tuple((a * y[i] + b * behind[i]) + e * prev[h][i] for i in range(NI))
+                for i in range(NI):
+                    g_ref[at(base, u, i), lane] = prev[h][i]
+        return tuple(after), tuple(prev)
+
+    def settle(base, levels, carry):
+        after = list(carry)
+        rows = group(coef_ref, 5, base)
+        sums = [group(sum_ref, q, base) for q in range(2)]
+        for u in levels:
+            for h, lane in enumerate(lanes):
+                g = spread(rows, u, lane)
+                y = tuple(g_ref[at(base, u, i), lane] + g * after[h][i] for i in range(NI))
+                after[h] = y
+                for i in range(0, NI, 2):
+                    y_ref[at(base, u, i, 2), lane] = jnp.concatenate(y[i : i + 2], axis=0).astype(jnp.bfloat16)
+                for q in range(2):
+                    part = [v * v for v in y] if q else list(y)
+                    while len(part) > 1:
+                        part = [part[i] + part[i + 1] for i in range(0, len(part), 2)]
+                    sums[q][u : u + 1, lane] = jnp.sum(part[0], axis=0, keepdims=True)
+        return tuple(after)
+
+    every, some = range(SUB), range(CZ - whole * SUB)
+    base_of = lambda k: pl.multiple_of(k * SUB, SUB)
+    last = whole * SUB
+    carry = lax.fori_loop(0, whole, lambda k, c: rise(base_of(k), every, c), still)
+    rise(last, some, carry)
+    carry = fall(last, some[::-1], (still, still))
+    lax.fori_loop(0, whole, lambda k, c: fall(base_of(whole - 1 - k), every[::-1], c), carry)
+    carry = lax.fori_loop(0, whole, lambda k, c: settle(base_of(k), every, c), still)
+    settle(last, some, carry)
+    for lane in lanes:
         mean0, sq0 = mean_ref[:, lane], sq_ref[:, lane]
         mean1, sq1 = sum_ref[0, :, lane] * (1.0 / CX), sum_ref[1, :, lane] * (1.0 / CX)
         change = jnp.concatenate([mean1 - mean0, (sq1 - mean1 * mean1) - (sq0 - mean0 * mean0)], axis=0)
@@ -363,7 +391,7 @@
     )
     moved, outgoing = call(
         edge_kernel,
-        (pltpu.VMEM((per_tile, width), f32), jax.ShapeDtypeStruct((slots, 2 * L), f32)),
+        (pltpu.VMEM((per_tile, width), f32), pltpu.VMEM((slots, 2 * L), f32)),
         (near, low, high, flip, put),
         cost=cost(1),
     )
@@ -393,7 +421,7 @@
     )
     tend, after = call(
         physics_kernel,
-        (jax.ShapeDtypeStruct((slots, 2 * L), f32), pltpu.VMEM((rows_f, slots), bf16)),
+        (pltpu.VMEM((slots, 2 * L), f32), pltpu.VMEM((rows_f, slots), bf16)),
         (received, *prepared),
         scratch=(
             pltpu.VMEM((rows_f, slots), f32),

time: 37.2 us -> 38.2 us (1.027)
  Pallas kernels: 11.9 us -> 12.9 us
    pallas_call x7, Pallas kernels: 11.9 us -> 12.9 us  [call(): pl.pallas_call(body, out_shape=outs, scratch_shapes=list(scratch), compil...]
  transfers between devices with their start and end apart: 4 -> 4, of which waited for: 4 -> 4; matrix products, arithmetic and copies ran while one was open for 0% -> 0% of each run, Pallas kernels for 15% -> 14%
where the time goes in v5:
time: 38.2 us; the launch traced here: 37.6 us
  Pallas kernels  12.9 us (34%)
  starting transfers between devices  12.4 us (32%)
  waiting for transfers between devices  11.6 us (30%)
  between operations  0.67 us (2%)
    pallas_call x7, Pallas kernels, call(): pl.pallas_call(body, out_shape=outs, scratch_shapes=list(scratch), compil...  12.9 us
    all_to_all x1, starting transfers between devices, shards(): lax.all_to_all(outgoing.reshape(n_tiles, cap_slots, 2 * L), 'cols', split...  6.53 us
    all_to_all x1, waiting for transfers between devices, shards(): lax.all_to_all(tend.reshape(n_tiles, cap_slots, 2 * L), 'cols', split_axi...  5.75 us
    all_to_all x1, waiting for transfers between devices, shards(): lax.all_to_all(outgoing.reshape(n_tiles, cap_slots, 2 * L), 'cols', split...  5.49 us
    all_to_all x1, starting transfers between devices, shards(): lax.all_to_all(tend.reshape(n_tiles, cap_slots, 2 * L), 'cols', split_axi...  3.37 us
    ppermute x2, starting transfers between devices, from_behind(): return lax.ppermute(value, axis, pairs)  2.52 us
  transfers between devices with their start and end apart: 4, of which 4 were waited for; matrix products, arithmetic and copies ran while one was open for 0% of the time, Pallas kernels for 14%

profile of v5, /device:TPU:0, one launch (start us, length us, event | category | flops | bytes accessed | tf_op | source)
XLA Modules:
  0.0 37.6 jit_solution(14678787681087113808)
XLA Ops:
  0.6 0.8 %shard_map.87 = (f32[8,512]{1,0:T(8,128)S(1)}, f32[8,512]{1,0:T(8,128)S(1)}) custom-call(f32[128,512]{1,0:T(8,128)} %bitcast.15), custom_call_target="tpu_custom_call" | custom-call | bytes 1500000 | tf_op jit(solution)/shard_map/pallas_call | solution.py:32
  1.4 0.5 %collective-permute-start = (f32[8,512]{1,0:T(8,128)S(1)}, f32[8,512]{1,0:T(8,128)S(1)}, u32[]{:S(2)}, u32[]{:S(2)}) collective-permute-start(f32[8,512]{1,0:T(8,128)S(1)} %get-tuple-element.19), channel_id=1, source_target_pairs={{0,1},{1,2},{2,3},{3,0},{4,5},{5,6},{6,7},{7,4},{8,9},{9,10},{10,1... | collective-permute-start | bytes 49160 | tf_op jit(solution)/shard_map/ppermute | solution.py:46
  1.9 2.0 %collective-permute-start.1 = (f32[8,512]{1,0:T(8,128)S(1)}, f32[8,512]{1,0:T(8,128)S(1)}, u32[]{:S(2)}, u32[]{:S(2)}) collective-permute-start(f32[8,512]{1,0:T(8,128)S(1)} %get-tuple-element.20), channel_id=1, source_target_pairs={{0,3},{1,0},{2,1},{3,2},{4,7},{5,4},{6,5},{7,6},{8,11},{9,8},{10,9... | collective-permute-start | bytes 49160 | tf_op jit(solution)/shard_map/ppermute | solution.py:46
  3.9 1.0 %shard_map.86 = (f32[128,512]{1,0:T(8,128)S(1)}, bf16[256,128]{1,0:T(8,128)(2,1)S(1)}, bf16[128,256]{1,0:T(8,128)(2,1)S(1)}, s32[2,8,128]{2,1,0:T(8,128)S(1)}) custom-call(f32[128,512]{1,0:T(8,128)} %bitcast.16, s32[1,128]{1,0:T(1,128)} %bitcast.19, s32[1,2]{1,0:T(1,128)} %bitcast.20), custom_call_target="tpu_custom_call" | custom-call | bytes 3000000 | tf_op jit(solution)/shard_map/pallas_call | solution.py:32
  5.0 0.3 collective-permute-done.low_ref
  5.3 0.1 collective-permute-done.1.high_ref
  5.4 0.9 %shard_map.88 = (f32[128,512]{1,0:T(8,128)S(1)}, f32[256,128]{1,0:T(8,128)}) custom-call(f32[128,512]{1,0:T(8,128)S(1)} %get-tuple-element.18.tile_ref, f32[8,512]{1,0:T(8,128)S(1)} %collective-permute-done.low_ref, f32[8,512]{1,0:T(8,128)S(1)} %collective-permute-done.1.high_ref, s32[2,8,128]{2,1,0:T(8,128)S(1)} %get-tuple-element.21.flip_ref, ...), custom_call_target="tpu_custom_call" | custom-call | bytes 3000000 | tf_op jit(solution)/shard_map/pallas_call | solution.py:32
  6.2 6.5 %all-to-all-start = ((f32[8,32,128]{2,1,0:T(8,128)}), f32[8,32,128]{2,1,0:T(8,128)S(1)}, u32[]{:S(2)}, u32[]{:S(2)}) async-start(f32[8,32,128]{2,1,0:T(8,128)} %bitcast.3), calls=%async_computation | async-start | bytes 262144 | tf_op jit(solution)/shard_map/all_to_all | solution.py:398
  12.8 2.5 %shard_map.89 = (bf16[3712,256]{1,0:T(8,128)(2,1)S(1)}, f32[64,256]{1,0:T(8,128)S(1)}, f32[64,256]{1,0:T(8,128)S(1)}, f32[6,64,256]{2,1,0:T(8,128)S(1)}, bf16[12...) custom-call(bf16[58,16384]{1,0:T(8,128)(2,1)} %bitcast.13, s32[1,256]{1,0:T(1,128)} %bitcast.18, f32[57]{0:T(128)} %diff_hbm.1, ...), custom_call_target="tpu_custom_call" | custom-call | bytes 12000000 | tf_op jit(solution)/shard_map/pallas_call | solution.py:32
  15.2 5.5 %all-to-all-done = f32[8,32,128]{2,1,0:T(8,128)S(1)} async-done(((f32[8,32,128]{2,1,0:T(8,128)}), f32[8,32,128]{2,1,0:T(8,128)S(1)}, u32[]{:S(2)}, u32[]{:S(2)}) %all-to-all-start) | async-done | bytes 131104 | tf_op jit(solution)/shard_map/all_to_all | solution.py:398
  20.7 5.0 %shard_map.90 = (f32[256,128]{1,0:T(8,128)}, bf16[3712,256]{1,0:T(8,128)(2,1)S(1)}) custom-call(f32[256,128]{1,0:T(8,128)S(1)} %bitcast.12, bf16[3712,256]{1,0:T(8,128)(2,1)S(1)} %get-tuple-element.26.f_ref, f32[64,256]{1,0:T(8,128)S(1)} %get-tuple-element.27.mean_ref, f32[64,256]{1,0:T(8,128)S(1)} %get-tuple-element.28.sq_ref, ...), custom_call_target="tpu_custom_call", output_to_operand_aliasing={{1}: (1, {})} | custom-call | bytes 15000000 | tf_op jit(solution)/shard_map/pallas_call | solution.py:32
  25.8 3.4 %all-to-all-start.1 = ((f32[8,32,128]{2,1,0:T(8,128)}), f32[8,32,128]{2,1,0:T(8,128)S(1)}, u32[]{:S(2)}, u32[]{:S(2)}) async-start(f32[8,32,128]{2,1,0:T(8,128)} %bitcast.7), calls=%async_computation.1 | async-start | bytes 262144 | tf_op jit(solution)/shard_map/all_to_all | solution.py:434
  29.1 1.9 %shard_map.92 = bf16[58,16384]{1,0:T(8,128)(2,1)} custom-call(bf16[3712,256]{1,0:T(8,128)(2,1)S(1)} %get-tuple-element.33.y_ref), custom_call_target="tpu_custom_call" | custom-call | bytes 9000000 | tf_op jit(solution)/shard_map/pallas_call | solution.py:32
  31.0 5.8 %all-to-all-done.1 = f32[8,32,128]{2,1,0:T(8,128)S(1)} async-done(((f32[8,32,128]{2,1,0:T(8,128)}), f32[8,32,128]{2,1,0:T(8,128)S(1)}, u32[]{:S(2)}, u32[]{:S(2)}) %all-to-all-start.1) | async-done | bytes 131104 | tf_op jit(solution)/shard_map/all_to_all | solution.py:434
  36.8 0.8 %shard_map.91 = f32[128,512]{1,0:T(8,128)} custom-call(f32[128,512]{1,0:T(8,128)S(1)} %get-tuple-element.23.moved_ref, bf16[128,256]{1,0:T(8,128)(2,1)S(1)} %get-tuple-element.24.take_ref, f32[256,128]{1,0:T(8,128)S(1)} %bitcast.11), custom_call_target="tpu_custom_call" | custom-call | bytes 2100000 | tf_op jit(solution)/shard_map/pallas_call | solution.py:32
Async XLA Ops:
  1.4 3.9 %collective-permute-start = (f32[8,512]{1,0:T(8,128)S(1)}, f32[8,512]{1,0:T(8,128)S(1)}, u32[]{:S(2)}, u32[]{:S(2)}) collective-permute-start(f32[8,512]{1,0:T(8,128)S(1)} %get-tuple-element.19), channel_id=1, source_target_pairs={{0,1},{1,2},{2,3},{3,0},{4,5},{5,6},{6,7},{7,4},{8,9},{9,10},{10,1... | collective-permute-start | bytes 49160 | tf_op jit(solution)/shard_map/ppermute | solution.py:46
  1.9 3.5 %collective-permute-start.1 = (f32[8,512]{1,0:T(8,128)S(1)}, f32[8,512]{1,0:T(8,128)S(1)}, u32[]{:S(2)}, u32[]{:S(2)}) collective-permute-start(f32[8,512]{1,0:T(8,128)S(1)} %get-tuple-element.20), channel_id=1, source_target_pairs={{0,3},{1,0},{2,1},{3,2},{4,7},{5,4},{6,5},{7,6},{8,11},{9,8},{10,9... | collective-permute-start | bytes 49160 | tf_op jit(solution)/shard_map/ppermute | solution.py:46
  6.2 14.5 %all-to-all-start = ((f32[8,32,128]{2,1,0:T(8,128)}), f32[8,32,128]{2,1,0:T(8,128)S(1)}, u32[]{:S(2)}, u32[]{:S(2)}) async-start(f32[8,32,128]{2,1,0:T(8,128)} %bitcast.3), calls=%async_computation | async-start | bytes 262144 | tf_op jit(solution)/shard_map/all_to_all | solution.py:398
  25.8 11.0 %all-to-all-start.1 = ((f32[8,32,128]{2,1,0:T(8,128)}), f32[8,32,128]{2,1,0:T(8,128)S(1)}, u32[]{:S(2)}, u32[]{:S(2)}) async-start(f32[8,32,128]{2,1,0:T(8,128)} %bitcast.7), calls=%async_computation.1 | async-start | bytes 262144 | tf_op jit(solution)/shard_map/all_to_all | solution.py:434

commit v6 on v4

--- a/solution.py
+++ b/solution.py
@@ -46,6 +46,23 @@
     return lax.ppermute(value, axis, pairs)
 
 
+def exchange(pieces):
+    count = lax.axis_size("cols")
+    if len(pieces) == 1:
+        whole = pieces[0].reshape(count, -1, pieces[0].shape[1])
+        return [lax.all_to_all(whole, "cols", split_axis=0, concat_axis=0, tiled=True).reshape(pieces[0].shape)]
+    out = list(pieces)
+    for k in sorted(range(1, count), reverse=True):
+        out[k] = lax.ppermute(pieces[k], "cols", [(c, c ^ k) for c in range(count)])
+    return out
+
+
+def place_of(k, pieces, rows):
+    if pieces == 1:
+        return 0
+    return pl.multiple_of((lax.axis_index("cols") ^ k) * rows, SUB)
+
+
 def split_dot(chosen, value):
     high, low = parts_of(value)
     pick = lambda part: lax.dot_general(chosen, part, (((1,), (0,)), ((), ())), preferred_element_type=jnp.float32)
@@ -69,7 +86,7 @@
         copy.wait()
 
 
-def slots_kernel(cap, state_hbm, owners_hbm, orient_hbm, tile_ref, put_ref, take_ref, flip_ref, own_ref, turn_ref, sems):
+def slots_kernel(cap, pieces, state_hbm, owners_hbm, orient_hbm, tile_ref, put_ref, take_ref, flip_ref, own_ref, turn_ref, sems):
     per_tile = owners_hbm.shape[1]
     n_slots = put_ref.shape[0]
     copies = [
@@ -84,7 +101,10 @@
     q_down = lax.broadcasted_iota(jnp.int32, (n_slots, per_tile), 0)
     q_across = lax.broadcasted_iota(jnp.int32, (per_tile, n_slots), 1)
     copies[0].wait()
-    across = jnp.broadcast_to(own_ref[...], (per_tile, per_tile))
+    named = own_ref[...]
+    if pieces > 1:
+        named = named ^ lax.axis_index("cols")
+    across = jnp.broadcast_to(named, (per_tile, per_tile))
     down = across.T
     same = down == across
     before_col = jnp.where(same & (row < col), 1.0, 0.0)
@@ -101,7 +121,7 @@
     copies[2].wait()
 
 
-def edge_kernel(tile_ref, low_ref, high_ref, flip_ref, put_ref, moved_ref, out_ref):
+def edge_kernel(tile_ref, low_ref, high_ref, flip_ref, put_ref, moved_ref, *out_refs):
     per_tile, width = tile_ref.shape
 
     def turned(ref, k):
@@ -116,7 +136,10 @@
     below = jnp.concatenate([low, tiles[: per_tile - TW]], axis=0)
     above = jnp.concatenate([tiles[TW:], high], axis=0)
     moved = tiles + kappa_edge * ((above + below) - 2.0 * tiles)
-    out_ref[...] = split_dot(put_ref[...], moved[:, : 2 * L])
+    picked = split_dot(put_ref[...], moved[:, : 2 * L])
+    for k, ref in enumerate(out_refs):
+        rows = ref.shape[0]
+        ref[...] = picked[k * rows : (k + 1) * rows]
     moved_ref[...] = moved
 
 
@@ -201,9 +224,14 @@
         sq_ref[t * TZ : (t + 1) * TZ, :] = square * (1.0 / CX)
 
 
-def physics_kernel(
-    cols_ref, f_ref, mean_ref, sq_ref, coef_ref, wa_ref, wb_ref, tend_ref, y_ref, g_ref, adv_ref, sum_ref
-):
+def physics_kernel(pieces, *refs):
+    sent_refs, refs = refs[:pieces], refs[pieces:]
+    f_ref, mean_ref, sq_ref, coef_ref, wa_ref, wb_ref, y_ref = refs[:7]
+    back_refs = refs[7 : 7 + pieces]
+    g_ref, adv_ref, sum_ref, cols_ref, tend_ref = refs[7 + pieces :]
+    rows = sent_refs[0].shape[0]
+    for k, ref in enumerate(sent_refs):
+        cols_ref[pl.ds(place_of(k, pieces, rows), rows), :] = ref[...]
     slots = cols_ref.shape[0]
     halves = slots // LANES
     for h in range(halves):
@@ -280,6 +308,8 @@
             (((0,), (0,)), ((), ())),
             preferred_element_type=jnp.float32,
         )
+    for k, ref in enumerate(back_refs):
+        ref[...] = tend_ref[pl.ds(place_of(k, pieces, rows), rows), :]
 
 
 def store_kernel(y_ref, crm_hbm, crm_ref, sems):
@@ -309,10 +339,13 @@
         copy.wait()
 
 
-def finish_kernel(moved_ref, take_ref, back_ref, out_hbm, part_ref, sems):
+def finish_kernel(pieces, moved_ref, take_ref, *refs):
+    back_refs = refs[:pieces]
+    out_hbm, part_ref, sems = refs[pieces:]
+    back = jnp.concatenate([ref[...] for ref in back_refs], axis=0)
     rest = pltpu.make_async_copy(moved_ref.at[:, 2 * L :], out_hbm.at[:, 2 * L :], sems.at[0])
     rest.start()
-    part_ref[...] = moved_ref[:, : 2 * L] + split_dot(take_ref[...], back_ref[...])
+    part_ref[...] = moved_ref[:, : 2 * L] + split_dot(take_ref[...], back)
     first = pltpu.make_async_copy(part_ref, out_hbm.at[:, : 2 * L], sems.at[1])
     first.start()
     rest.wait()
@@ -335,6 +368,9 @@
     cap_slots = max(2, 2 * per_tile // n_tiles)
     slots = n_tiles * cap_slots
     rows_f = CZ * CX
+    pieces = n_tiles if n_tiles <= 8 else 1
+    piece = (slots // pieces, 2 * L)
+    near_by = pltpu.VMEM(piece, f32) if pieces > 1 else jax.ShapeDtypeStruct(piece, f32)
     hbm = pl.BlockSpec(memory_space=pltpu.HBM)
     dma = pltpu.SemaphoreType.DMA
     tile = state[0]
@@ -349,7 +385,7 @@
     low = from_behind(upper, "edge", 1)
     high = from_behind(lower, "edge", -1)
     near, put, take, flip = call(
-        functools.partial(slots_kernel, cap_slots),
+        functools.partial(slots_kernel, cap_slots, pieces),
         (
             pltpu.VMEM((per_tile, width), f32),
             pltpu.VMEM((slots, per_tile), bf16),
@@ -361,15 +397,13 @@
         scratch=(pltpu.VMEM((1, per_tile), jnp.int32), pltpu.VMEM((1, 2), jnp.int32), dma((3,))),
         cost=cost(1),
     )
-    moved, outgoing = call(
+    moved, *outgoing = call(
         edge_kernel,
-        (pltpu.VMEM((per_tile, width), f32), jax.ShapeDtypeStruct((slots, 2 * L), f32)),
+        (pltpu.VMEM((per_tile, width), f32), *[near_by] * pieces),
         (near, low, high, flip, put),
         cost=cost(1),
     )
-    received = lax.all_to_all(
-        outgoing.reshape(n_tiles, cap_slots, 2 * L), "cols", split_axis=0, concat_axis=0, tiled=True
-    ).reshape(slots, 2 * L)
+    received = exchange(outgoing)
     prepared = call(
         prepare_kernel,
         (
@@ -391,21 +425,21 @@
         ),
         cost=cost(4),
     )
-    tend, after = call(
-        physics_kernel,
-        (jax.ShapeDtypeStruct((slots, 2 * L), f32), pltpu.VMEM((rows_f, slots), bf16)),
-        (received, *prepared),
+    after, *tend = call(
+        functools.partial(physics_kernel, pieces),
+        (pltpu.VMEM((rows_f, slots), bf16), *[near_by] * pieces),
+        (*received, *prepared),
         scratch=(
             pltpu.VMEM((rows_f, slots), f32),
             pltpu.VMEM((5, ZP, slots), f32),
             pltpu.VMEM((2, ZP, slots), f32),
+            pltpu.VMEM((slots, 2 * L), f32),
+            pltpu.VMEM((slots, 2 * L), f32),
         ),
-        aliases={1: 1},
+        aliases={pieces: 0},
         cost=cost(5),
     )
-    returned = lax.all_to_all(
-        tend.reshape(n_tiles, cap_slots, 2 * L), "cols", split_axis=0, concat_axis=0, tiled=True
-    ).reshape(slots, 2 * L)
+    returned = exchange(tend)
     crm_new = call(
         store_kernel,
         jax.ShapeDtypeStruct((CZ, CX * slots), bf16),
@@ -415,9 +449,9 @@
         cost=cost(3),
     )
     new_state = call(
-        finish_kernel,
+        functools.partial(finish_kernel, pieces),
         jax.ShapeDtypeStruct((per_tile, width), f32),
-        (moved, take, returned),
+        (moved, take, *returned),
         scratch=(pltpu.VMEM((per_tile, 2 * L), f32), dma((2,))),
         out_specs=hbm,
         cost=cost(0.7),

time: 37.2 us -> 42.1 us (1.13)
  starting transfers between devices: 12.4 us -> 25.5 us
  waiting for transfers between devices: 11.6 us -> 4.96 us
  Pallas kernels: 11.9 us -> 10.5 us
    ppermute x0 -> x14, starting transfers between devices: none -> 23 us  [exchange(): out[k] = lax.ppermute(pieces[k], 'cols', [(c, c ^ k) for c in range(count)])]
    all_to_all x2 -> x0, waiting for transfers between devices: 11.2 us -> none  [the longest x1 5.75 us: shards(): lax.all_to_all(tend.reshape(n_tiles, cap_slots, 2 * L), 'cols', split_axi...]
    all_to_all x2 -> x0, starting transfers between devices: 9.9 us -> none  [the longest x1 6.53 us: shards(): lax.all_to_all(outgoing.reshape(n_tiles, cap_slots, 2 * L), 'cols', split...]
    ppermute x0 -> x14, waiting for transfers between devices: none -> 4.53 us  [exchange(): out[k] = lax.ppermute(pieces[k], 'cols', [(c, c ^ k) for c in range(count)])]
    pallas_call x7, Pallas kernels: 11.9 us -> 10.5 us  [call(): pl.pallas_call(body, out_shape=outs, scratch_shapes=list(scratch), compil...]
  transfers between devices with their start and end apart: 4 -> 16, of which waited for: 4 -> 4; matrix products, arithmetic and copies ran while one was open for 0% -> 0% of each run, Pallas kernels for 15% -> 13%
where the time goes in v6:
time: 42.1 us; the launch traced here: 41.8 us
  starting transfers between devices  25.5 us (61%)
  Pallas kernels  10.5 us (25%)
  waiting for transfers between devices  4.96 us (12%)
  between operations  0.75 us (2%)
    ppermute x14, starting transfers between devices, exchange(): out[k] = lax.ppermute(pieces[k], 'cols', [(c, c ^ k) for c in range(count)])  23 us
    pallas_call x7, Pallas kernels, call(): pl.pallas_call(body, out_shape=outs, scratch_shapes=list(scratch), compil...  10.5 us
    ppermute x14, waiting for transfers between devices, exchange(): out[k] = lax.ppermute(pieces[k], 'cols', [(c, c ^ k) for c in range(count)])  4.53 us
    ppermute x2, starting transfers between devices, from_behind(): return lax.ppermute(value, axis, pairs)  2.52 us
  transfers between devices with their start and end apart: 16, of which 4 were waited for; matrix products, arithmetic and copies ran while one was open for 0% of the time, Pallas kernels for 13%

profile of v6, /device:TPU:0, one launch (start us, length us, event | category | flops | bytes accessed | tf_op | source)
XLA Modules:
  0.0 41.8 jit_solution(208719947795884595)
XLA Ops:
  0.6 0.8 %shard_map.87 = (f32[8,512]{1,0:T(8,128)S(1)}, f32[8,512]{1,0:T(8,128)S(1)}) custom-call(f32[128,512]{1,0:T(8,128)} %bitcast.9), custom_call_target="tpu_custom_call" | custom-call | bytes 1500000 | tf_op jit(solution)/shard_map/pallas_call | solution.py:32
  1.4 0.5 %collective-permute-start = (f32[8,512]{1,0:T(8,128)S(1)}, f32[8,512]{1,0:T(8,128)S(1)}, u32[]{:S(2)}, u32[]{:S(2)}) collective-permute-start(f32[8,512]{1,0:T(8,128)S(1)} %get-tuple-element.33), channel_id=1, source_target_pairs={{0,1},{1,2},{2,3},{3,0},{4,5},{5,6},{6,7},{7,4},{8,9},{9,10},{10,1... | collective-permute-start | bytes 49160 | tf_op jit(solution)/shard_map/ppermute | solution.py:46
  1.9 2.0 %collective-permute-start.1 = (f32[8,512]{1,0:T(8,128)S(1)}, f32[8,512]{1,0:T(8,128)S(1)}, u32[]{:S(2)}, u32[]{:S(2)}) collective-permute-start(f32[8,512]{1,0:T(8,128)S(1)} %get-tuple-element.34), channel_id=1, source_target_pairs={{0,3},{1,0},{2,1},{3,2},{4,7},{5,4},{6,5},{7,6},{8,11},{9,8},{10,9... | collective-permute-start | bytes 49160 | tf_op jit(solution)/shard_map/ppermute | solution.py:46
  3.9 1.0 %shard_map.86 = (f32[128,512]{1,0:T(8,128)S(1)}, bf16[256,128]{1,0:T(8,128)(2,1)S(1)}, bf16[128,256]{1,0:T(8,128)(2,1)S(1)}, s32[2,8,128]{2,1,0:T(8,128)S(1)}) custom-call(f32[128,512]{1,0:T(8,128)} %bitcast.10, s32[1,128]{1,0:T(1,128)} %bitcast.13, s32[1,2]{1,0:T(1,128)} %bitcast.14), custom_call_target="tpu_custom_call" | custom-call | bytes 3000000 | tf_op jit(solution)/shard_map/pallas_call | solution.py:32
  4.9 0.3 collective-permute-done.low_ref
  5.3 0.1 collective-permute-done.1.high_ref
  5.4 0.2 shard_map.88
  5.6 2.3 %collective-permute-start.2 = (f32[32,128]{1,0:T(8,128)S(1)}, f32[32,128]{1,0:T(8,128)S(1)}, u32[]{:S(2)}, u32[]{:S(2)}) collective-permute-start(f32[32,128]{1,0:T(8,128)S(1)} %get-tuple-element.40), channel_id=1, source_target_pairs={{0,4},{4,0},{8,12},{12,8},{16,20},{20,16},{24,28},{28,24},{1,5},{5... | collective-permute-start | bytes 49160 | tf_op jit(solution)/shard_map/ppermute | solution.py:56
  7.9 1.6 %collective-permute-start.3 = (f32[32,128]{1,0:T(8,128)S(1)}, f32[32,128]{1,0:T(8,128)S(1)}, u32[]{:S(2)}, u32[]{:S(2)}) collective-permute-start(f32[32,128]{1,0:T(8,128)S(1)} %get-tuple-element.41), channel_id=1, source_target_pairs={{0,8},{4,12},{8,0},{12,4},{16,24},{20,28},{24,16},{28,20},{1,9},{5... | collective-permute-start | bytes 49160 | tf_op jit(solution)/shard_map/ppermute | solution.py:56
  9.4 3.0 %collective-permute-start.5 = (f32[32,128]{1,0:T(8,128)S(1)}, f32[32,128]{1,0:T(8,128)S(1)}, u32[]{:S(2)}, u32[]{:S(2)}) collective-permute-start(f32[32,128]{1,0:T(8,128)S(1)} %get-tuple-element.43), channel_id=1, source_target_pairs={{0,16},{4,20},{8,24},{12,28},{16,0},{20,4},{24,8},{28,12},{1,17},{... | collective-permute-start | bytes 49160 | tf_op jit(solution)/shard_map/ppermute | solution.py:56
  12.5 1.3 %collective-permute-start.6 = (f32[32,128]{1,0:T(8,128)S(1)}, f32[32,128]{1,0:T(8,128)S(1)}, u32[]{:S(2)}, u32[]{:S(2)}) collective-permute-start(f32[32,128]{1,0:T(8,128)S(1)} %get-tuple-element.44), channel_id=1, source_target_pairs={{0,20},{4,16},{8,28},{12,24},{16,4},{20,0},{24,12},{28,8},{1,21},{... | collective-permute-start | bytes 49160 | tf_op jit(solution)/shard_map/ppermute | solution.py:56
  13.7 3.6 %collective-permute-start.7 = (f32[32,128]{1,0:T(8,128)S(1)}, f32[32,128]{1,0:T(8,128)S(1)}, u32[]{:S(2)}, u32[]{:S(2)}) collective-permute-start(f32[32,128]{1,0:T(8,128)S(1)} %get-tuple-element.45), channel_id=1, source_target_pairs={{0,24},{4,28},{8,16},{12,20},{16,8},{20,12},{24,0},{28,4},{1,25},{... | collective-permute-start | bytes 49160 | tf_op jit(solution)/shard_map/ppermute | solution.py:56
  17.3 0.0 collective-permute-start.8
  17.4 2.5 %shard_map.89 = (bf16[3712,256]{1,0:T(8,128)(2,1)S(1)}, f32[64,256]{1,0:T(8,128)S(1)}, f32[64,256]{1,0:T(8,128)S(1)}, f32[6,64,256]{2,1,0:T(8,128)S(1)}, bf16[12...) custom-call(bf16[58,16384]{1,0:T(8,128)(2,1)} %bitcast.7, s32[1,256]{1,0:T(1,128)} %bitcast.12, f32[57]{0:T(128)} %diff_hbm.1, ...), custom_call_target="tpu_custom_call" | custom-call | bytes 12000000 | tf_op jit(solution)/shard_map/pallas_call | solution.py:32
  19.9 3.9 %collective-permute-done.8.refs_7_ = f32[32,128]{1,0:T(8,128)S(1)} collective-permute-done((f32[32,128]{1,0:T(8,128)S(1)}, f32[32,128]{1,0:T(8,128)S(1)}, u32[]{:S(2)}, u32[]{:S(2)}) %collective-permute-start.8) | collective-permute-done | bytes 16416 | tf_op jit(solution)/shard_map/ppermute | solution.py:56
  23.8 3.4 %shard_map.90 = (bf16[3712,256]{1,0:T(8,128)(2,1)S(1)}, f32[32,128]{1,0:T(8,128)S(1)}, f32[32,128]{1,0:T(8,128)S(1)}, f32[32,128]{1,0:T(8,128)S(1)}, f32[32,128]...) custom-call(f32[32,128]{1,0:T(8,128)S(1)} %get-tuple-element.39.refs, ...), custom_call_target="tpu_custom_call", output_to_operand_aliasing={{0}: (8, {})} | custom-call | bytes 15000000 | tf_op jit(solution)/shard_map/pallas_call | solution.py:32
  27.2 0.6 %collective-permute-start.9 = (f32[32,128]{1,0:T(8,128)S(1)}, f32[32,128]{1,0:T(8,128)S(1)}, u32[]{:S(2)}, u32[]{:S(2)}) collective-permute-start(f32[32,128]{1,0:T(8,128)S(1)} %get-tuple-element.54), channel_id=1, source_target_pairs={{0,4},{4,0},{8,12},{12,8},{16,20},{20,16},{24,28},{28,24},{1,5},{5... | collective-permute-start | bytes 49160 | tf_op jit(solution)/shard_map/ppermute | solution.py:56
  27.8 2.9 %collective-permute-start.11 = (f32[32,128]{1,0:T(8,128)S(1)}, f32[32,128]{1,0:T(8,128)S(1)}, u32[]{:S(2)}, u32[]{:S(2)}) collective-permute-start(f32[32,128]{1,0:T(8,128)S(1)} %get-tuple-element.56), channel_id=1, source_target_pairs={{0,12},{4,8},{8,4},{12,0},{16,28},{20,24},{24,20},{28,16},{1,13},{... | collective-permute-start | bytes 49160 | tf_op jit(solution)/shard_map/ppermute | solution.py:56
  30.7 2.9 %collective-permute-start.13 = (f32[32,128]{1,0:T(8,128)S(1)}, f32[32,128]{1,0:T(8,128)S(1)}, u32[]{:S(2)}, u32[]{:S(2)}) collective-permute-start(f32[32,128]{1,0:T(8,128)S(1)} %get-tuple-element.58), channel_id=1, source_target_pairs={{0,20},{4,16},{8,28},{12,24},{16,4},{20,0},{24,12},{28,8},{1,21},{... | collective-permute-start | bytes 49160 | tf_op jit(solution)/shard_map/ppermute | solution.py:56
  33.6 0.8 %collective-permute-start.14 = (f32[32,128]{1,0:T(8,128)S(1)}, f32[32,128]{1,0:T(8,128)S(1)}, u32[]{:S(2)}, u32[]{:S(2)}) collective-permute-start(f32[32,128]{1,0:T(8,128)S(1)} %get-tuple-element.59), channel_id=1, source_target_pairs={{0,24},{4,28},{8,16},{12,20},{16,8},{20,12},{24,0},{28,4},{1,25},{... | collective-permute-start | bytes 49160 | tf_op jit(solution)/shard_map/ppermute | solution.py:56
  34.5 3.9 %collective-permute-start.15 = (f32[32,128]{1,0:T(8,128)S(1)}, f32[32,128]{1,0:T(8,128)S(1)}, u32[]{:S(2)}, u32[]{:S(2)}) collective-permute-start(f32[32,128]{1,0:T(8,128)S(1)} %get-tuple-element.60), channel_id=1, source_target_pairs={{0,28},{4,24},{8,20},{12,16},{16,12},{20,8},{24,4},{28,0},{1,29},{... | collective-permute-start | bytes 49160 | tf_op jit(solution)/shard_map/ppermute | solution.py:56
  38.4 1.9 %shard_map.92 = bf16[58,16384]{1,0:T(8,128)(2,1)} custom-call(bf16[3712,256]{1,0:T(8,128)(2,1)S(1)} %get-tuple-element.61.y_ref), custom_call_target="tpu_custom_call" | custom-call | bytes 9000000 | tf_op jit(solution)/shard_map/pallas_call | solution.py:32
  40.3 0.6 %collective-permute-done.15.refs_7_ = f32[32,128]{1,0:T(8,128)S(1)} collective-permute-done((f32[32,128]{1,0:T(8,128)S(1)}, f32[32,128]{1,0:T(8,128)S(1)}, u32[]{:S(2)}, u32[]{:S(2)}) %collective-permute-start.15) | collective-permute-done | bytes 16416 | tf_op jit(solution)/shard_map/ppermute | solution.py:56
  40.9 0.8 %shard_map.91 = f32[128,512]{1,0:T(8,128)} custom-call(f32[128,512]{1,0:T(8,128)S(1)} %get-tuple-element.37.moved_ref, bf16[128,256]{1,0:T(8,128)(2,1)S(1)} %get-tuple-element.38.take_ref, f32[32,128]{1,0:T(8,128)S(1)} %get-tuple-element.53.refs_0_, f32[32,128]{1,0:T(8,128)S(1)} %collective-permute-done.9.refs_1_, ...), custom_call_target="tpu_custom_call" | custom-call | bytes 2100000 | tf_op jit(solution)/shard_map/pallas_call | solution.py:32
  (15 shorter events, 0.0 us)
Async XLA Ops:
  1.4 3.9 %collective-permute-start = (f32[8,512]{1,0:T(8,128)S(1)}, f32[8,512]{1,0:T(8,128)S(1)}, u32[]{:S(2)}, u32[]{:S(2)}) collective-permute-start(f32[8,512]{1,0:T(8,128)S(1)} %get-tuple-element.33), channel_id=1, source_target_pairs={{0,1},{1,2},{2,3},{3,0},{4,5},{5,6},{6,7},{7,4},{8,9},{9,10},{10,1... | collective-permute-start | bytes 49160 | tf_op jit(solution)/shard_map/ppermute | solution.py:46
  1.9 3.5 %collective-permute-start.1 = (f32[8,512]{1,0:T(8,128)S(1)}, f32[8,512]{1,0:T(8,128)S(1)}, u32[]{:S(2)}, u32[]{:S(2)}) collective-permute-start(f32[8,512]{1,0:T(8,128)S(1)} %get-tuple-element.34), channel_id=1, source_target_pairs={{0,3},{1,0},{2,1},{3,2},{4,7},{5,4},{6,5},{7,6},{8,11},{9,8},{10,9... | collective-permute-start | bytes 49160 | tf_op jit(solution)/shard_map/ppermute | solution.py:46
  5.6 8.1 %collective-permute-start.2 = (f32[32,128]{1,0:T(8,128)S(1)}, f32[32,128]{1,0:T(8,128)S(1)}, u32[]{:S(2)}, u32[]{:S(2)}) collective-permute-start(f32[32,128]{1,0:T(8,128)S(1)} %get-tuple-element.40), channel_id=1, source_target_pairs={{0,4},{4,0},{8,12},{12,8},{16,20},{20,16},{24,28},{28,24},{1,5},{5... | collective-permute-start | bytes 49160 | tf_op jit(solution)/shard_map/ppermute | solution.py:56
  7.9 9.5 %collective-permute-start.3 = (f32[32,128]{1,0:T(8,128)S(1)}, f32[32,128]{1,0:T(8,128)S(1)}, u32[]{:S(2)}, u32[]{:S(2)}) collective-permute-start(f32[32,128]{1,0:T(8,128)S(1)} %get-tuple-element.41), channel_id=1, source_target_pairs={{0,8},{4,12},{8,0},{12,4},{16,24},{20,28},{24,16},{28,20},{1,9},{5... | collective-permute-start | bytes 49160 | tf_op jit(solution)/shard_map/ppermute | solution.py:56
  9.4 10.4 %collective-permute-start.4 = (f32[32,128]{1,0:T(8,128)S(1)}, f32[32,128]{1,0:T(8,128)S(1)}, u32[]{:S(2)}, u32[]{:S(2)}) collective-permute-start(f32[32,128]{1,0:T(8,128)S(1)} %get-tuple-element.42), channel_id=1, source_target_pairs={{0,12},{4,8},{8,4},{12,0},{16,28},{20,24},{24,20},{28,16},{1,13},{... | collective-permute-start | bytes 49160 | tf_op jit(solution)/shard_map/ppermute | solution.py:56
  9.4 10.4 %collective-permute-start.5 = (f32[32,128]{1,0:T(8,128)S(1)}, f32[32,128]{1,0:T(8,128)S(1)}, u32[]{:S(2)}, u32[]{:S(2)}) collective-permute-start(f32[32,128]{1,0:T(8,128)S(1)} %get-tuple-element.43), channel_id=1, source_target_pairs={{0,16},{4,20},{8,24},{12,28},{16,0},{20,4},{24,8},{28,12},{1,17},{... | collective-permute-start | bytes 49160 | tf_op jit(solution)/shard_map/ppermute | solution.py:56
  12.5 7.4 %collective-permute-start.6 = (f32[32,128]{1,0:T(8,128)S(1)}, f32[32,128]{1,0:T(8,128)S(1)}, u32[]{:S(2)}, u32[]{:S(2)}) collective-permute-start(f32[32,128]{1,0:T(8,128)S(1)} %get-tuple-element.44), channel_id=1, source_target_pairs={{0,20},{4,16},{8,28},{12,24},{16,4},{20,0},{24,12},{28,8},{1,21},{... | collective-permute-start | bytes 49160 | tf_op jit(solution)/shard_map/ppermute | solution.py:56
  13.7 6.1 %collective-permute-start.7 = (f32[32,128]{1,0:T(8,128)S(1)}, f32[32,128]{1,0:T(8,128)S(1)}, u32[]{:S(2)}, u32[]{:S(2)}) collective-permute-start(f32[32,128]{1,0:T(8,128)S(1)} %get-tuple-element.45), channel_id=1, source_target_pairs={{0,24},{4,28},{8,16},{12,20},{16,8},{20,12},{24,0},{28,4},{1,25},{... | collective-permute-start | bytes 49160 | tf_op jit(solution)/shard_map/ppermute | solution.py:56
  17.3 6.4 %collective-permute-start.8 = (f32[32,128]{1,0:T(8,128)S(1)}, f32[32,128]{1,0:T(8,128)S(1)}, u32[]{:S(2)}, u32[]{:S(2)}) collective-permute-start(f32[32,128]{1,0:T(8,128)S(1)} %get-tuple-element.46), channel_id=1, source_target_pairs={{0,28},{4,24},{8,20},{12,16},{16,12},{20,8},{24,4},{28,0},{1,29},{... | collective-permute-start | bytes 49160 | tf_op jit(solution)/shard_map/ppermute | solution.py:56
  27.2 6.5 %collective-permute-start.9 = (f32[32,128]{1,0:T(8,128)S(1)}, f32[32,128]{1,0:T(8,128)S(1)}, u32[]{:S(2)}, u32[]{:S(2)}) collective-permute-start(f32[32,128]{1,0:T(8,128)S(1)} %get-tuple-element.54), channel_id=1, source_target_pairs={{0,4},{4,0},{8,12},{12,8},{16,20},{20,16},{24,28},{28,24},{1,5},{5... | collective-permute-start | bytes 49160 | tf_op jit(solution)/shard_map/ppermute | solution.py:56
  27.8 6.7 %collective-permute-start.10 = (f32[32,128]{1,0:T(8,128)S(1)}, f32[32,128]{1,0:T(8,128)S(1)}, u32[]{:S(2)}, u32[]{:S(2)}) collective-permute-start(f32[32,128]{1,0:T(8,128)S(1)} %get-tuple-element.55), channel_id=1, source_target_pairs={{0,8},{4,12},{8,0},{12,4},{16,24},{20,28},{24,16},{28,20},{1,9},{5... | collective-permute-start | bytes 49160 | tf_op jit(solution)/shard_map/ppermute | solution.py:56
  27.8 12.5 %collective-permute-start.11 = (f32[32,128]{1,0:T(8,128)S(1)}, f32[32,128]{1,0:T(8,128)S(1)}, u32[]{:S(2)}, u32[]{:S(2)}) collective-permute-start(f32[32,128]{1,0:T(8,128)S(1)} %get-tuple-element.56), channel_id=1, source_target_pairs={{0,12},{4,8},{8,4},{12,0},{16,28},{20,24},{24,20},{28,16},{1,13},{... | collective-permute-start | bytes 49160 | tf_op jit(solution)/shard_map/ppermute | solution.py:56
  30.7 9.5 %collective-permute-start.12 = (f32[32,128]{1,0:T(8,128)S(1)}, f32[32,128]{1,0:T(8,128)S(1)}, u32[]{:S(2)}, u32[]{:S(2)}) collective-permute-start(f32[32,128]{1,0:T(8,128)S(1)} %get-tuple-element.57), channel_id=1, source_target_pairs={{0,16},{4,20},{8,24},{12,28},{16,0},{20,4},{24,8},{28,12},{1,17},{... | collective-permute-start | bytes 49160 | tf_op jit(solution)/shard_map/ppermute | solution.py:56
  30.7 9.6 %collective-permute-start.13 = (f32[32,128]{1,0:T(8,128)S(1)}, f32[32,128]{1,0:T(8,128)S(1)}, u32[]{:S(2)}, u32[]{:S(2)}) collective-permute-start(f32[32,128]{1,0:T(8,128)S(1)} %get-tuple-element.58), channel_id=1, source_target_pairs={{0,20},{4,16},{8,28},{12,24},{16,4},{20,0},{24,12},{28,8},{1,21},{... | collective-permute-start | bytes 49160 | tf_op jit(solution)/shard_map/ppermute | solution.py:56
  33.6 6.7 %collective-permute-start.14 = (f32[32,128]{1,0:T(8,128)S(1)}, f32[32,128]{1,0:T(8,128)S(1)}, u32[]{:S(2)}, u32[]{:S(2)}) collective-permute-start(f32[32,128]{1,0:T(8,128)S(1)} %get-tuple-element.59), channel_id=1, source_target_pairs={{0,24},{4,28},{8,16},{12,20},{16,8},{20,12},{24,0},{28,4},{1,25},{... | collective-permute-start | bytes 49160 | tf_op jit(solution)/shard_map/ppermute | solution.py:56
  34.5 6.4 %collective-permute-start.15 = (f32[32,128]{1,0:T(8,128)S(1)}, f32[32,128]{1,0:T(8,128)S(1)}, u32[]{:S(2)}, u32[]{:S(2)}) collective-permute-start(f32[32,128]{1,0:T(8,128)S(1)} %get-tuple-element.60), channel_id=1, source_target_pairs={{0,28},{4,24},{8,20},{12,16},{16,12},{20,8},{24,4},{28,0},{1,29},{... | collective-permute-start | bytes 49160 | tf_op jit(solution)/shard_map/ppermute | solution.py:56

commit v7 on v4

--- a/solution.py
+++ b/solution.py
@@ -40,10 +40,17 @@
     )(*args)
 
 
-def from_behind(value, axis, steps):
+def swap(value, axis, first):
     count = lax.axis_size(axis)
-    pairs = [(source, (source + steps) % count) for source in range(count)]
+    pairs = []
+    for one in range(first, count, 2):
+        other = (one + 1) % count
+        pairs += [(one, other), (other, one)]
     return lax.ppermute(value, axis, pairs)
+
+
+def odd_strip():
+    return lax.rem(lax.axis_index("edge"), 2)
 
 
 def split_dot(chosen, value):
@@ -57,11 +64,13 @@
     return high, (value - high.astype(jnp.float32)).astype(jnp.bfloat16)
 
 
-def rows_kernel(state_hbm, upper_ref, lower_ref, sems):
-    per_tile = state_hbm.shape[0]
+def rows_kernel(state_hbm, outer_ref, inner_ref, sems):
+    last = state_hbm.shape[0] - TW
+    outer = pl.multiple_of(odd_strip() * last, TW)
+    inner = pl.multiple_of((1 - odd_strip()) * last, TW)
     copies = [
-        pltpu.make_async_copy(state_hbm.at[per_tile - TW :], upper_ref, sems.at[0]),
-        pltpu.make_async_copy(state_hbm.at[:TW], lower_ref, sems.at[1]),
+        pltpu.make_async_copy(state_hbm.at[pl.ds(outer, TW)], outer_ref, sems.at[0]),
+        pltpu.make_async_copy(state_hbm.at[pl.ds(inner, TW)], inner_ref, sems.at[1]),
     ]
     for copy in copies:
         copy.start()
@@ -101,17 +110,19 @@
     copies[2].wait()
 
 
-def edge_kernel(tile_ref, low_ref, high_ref, flip_ref, put_ref, moved_ref, out_ref):
+def edge_kernel(tile_ref, outer_ref, inner_ref, flip_ref, put_ref, moved_ref, out_ref):
     per_tile, width = tile_ref.shape
 
-    def turned(ref, k):
-        value = ref[...]
+    odd = odd_strip() == 1
+
+    def turned(value, k):
         back = jnp.concatenate([value[TW - 1 - w : TW - w] for w in range(TW)], axis=0)
         flip = jnp.concatenate([flip_ref[k]] * (width // LANES), axis=1)
         return jnp.where(flip == 1, back, value)
 
-    low = turned(low_ref, 0)
-    high = turned(high_ref, 1)
+    outer, inner = outer_ref[...], inner_ref[...]
+    low = turned(jnp.where(odd, inner, outer), 0)
+    high = turned(jnp.where(odd, outer, inner), 1)
     tiles = tile_ref[...]
     below = jnp.concatenate([low, tiles[: per_tile - TW]], axis=0)
     above = jnp.concatenate([tiles[TW:], high], axis=0)
@@ -338,7 +349,7 @@
     hbm = pl.BlockSpec(memory_space=pltpu.HBM)
     dma = pltpu.SemaphoreType.DMA
     tile = state[0]
-    upper, lower = call(
+    outer, inner = call(
         rows_kernel,
         (pltpu.VMEM((TW, width), f32), pltpu.VMEM((TW, width), f32)),
         (far(tile),),
@@ -346,8 +357,8 @@
         scratch=(dma((2,)),),
         cost=cost(0.5),
     )
-    low = from_behind(upper, "edge", 1)
-    high = from_behind(lower, "edge", -1)
+    outer = swap(outer, "edge", 1)
+    inner = swap(inner, "edge", 0)
     near, put, take, flip = call(
         functools.partial(slots_kernel, cap_slots),
         (
@@ -364,7 +375,7 @@
     moved, outgoing = call(
         edge_kernel,
         (pltpu.VMEM((per_tile, width), f32), jax.ShapeDtypeStruct((slots, 2 * L), f32)),
-        (near, low, high, flip, put),
+        (near, outer, inner, flip, put),
         cost=cost(1),
     )
     received = lax.all_to_all(

time: 37.2 us -> 36.4 us (0.978)
  waiting for transfers between devices: 11.6 us -> 10.3 us
  starting transfers between devices: 12.4 us -> 12.9 us
    ppermute x2, starting transfers between devices: 2.52 us -> 3.15 us  [swap(): return lax.ppermute(value, axis, pairs)]
    all_to_all x1, waiting for transfers between devices: 5.49 us -> 4.89 us  [shards(): lax.all_to_all(outgoing.reshape(n_tiles, cap_slots, 2 * L), 'cols', split...]
    ppermute x2, waiting for transfers between devices: 0.41 us -> 0.01 us  [swap(): return lax.ppermute(value, axis, pairs)]
  transfers between devices with their start and end apart: 4 -> 4, of which waited for: 4 -> 2; matrix products, arithmetic and copies ran while one was open for 0% -> 0% of each run, Pallas kernels for 15% -> 15%
where the time goes in v7:
time: 36.4 us; the launch traced here: 35.8 us
  starting transfers between devices  12.9 us (35%)
  Pallas kernels  11.9 us (33%)
  waiting for transfers between devices  10.3 us (28%)
  between operations  0.69 us (2%)
    pallas_call x7, Pallas kernels, call(): pl.pallas_call(body, out_shape=outs, scratch_shapes=list(scratch), compil...  11.9 us
    all_to_all x1, starting transfers between devices, shards(): lax.all_to_all(outgoing.reshape(n_tiles, cap_slots, 2 * L), 'cols', split...  6.38 us
    all_to_all x1, waiting for transfers between devices, shards(): lax.all_to_all(tend.reshape(n_tiles, cap_slots, 2 * L), 'cols', split_axi...  5.4 us
    all_to_all x1, waiting for transfers between devices, shards(): lax.all_to_all(outgoing.reshape(n_tiles, cap_slots, 2 * L), 'cols', split...  4.89 us
    all_to_all x1, starting transfers between devices, shards(): lax.all_to_all(tend.reshape(n_tiles, cap_slots, 2 * L), 'cols', split_axi...  3.37 us
    ppermute x2, starting transfers between devices, swap(): return lax.ppermute(value, axis, pairs)  3.15 us
  transfers between devices with their start and end apart: 4, of which 2 were waited for; matrix products, arithmetic and copies ran while one was open for 0% of the time, Pallas kernels for 15%

profile of v7, /device:TPU:0, one launch (start us, length us, event | category | flops | bytes accessed | tf_op | source)
XLA Modules:
  0.0 35.8 jit_solution(7313000350800852557)
XLA Ops:
  0.6 0.8 %shard_map.87 = (f32[8,512]{1,0:T(8,128)S(1)}, f32[8,512]{1,0:T(8,128)S(1)}) custom-call(f32[128,512]{1,0:T(8,128)} %bitcast.15), custom_call_target="tpu_custom_call" | custom-call | bytes 1500000 | tf_op jit(solution)/shard_map/pallas_call | solution.py:32
  1.4 2.5 %collective-permute-start = (f32[8,512]{1,0:T(8,128)S(1)}, f32[8,512]{1,0:T(8,128)S(1)}, u32[]{:S(2)}, u32[]{:S(2)}) collective-permute-start(f32[8,512]{1,0:T(8,128)S(1)} %get-tuple-element.19), channel_id=1, source_target_pairs={{1,2},{2,1},{3,0},{0,3},{5,6},{6,5},{7,4},{4,7},{9,10},{10,9},{11,... | collective-permute-start | bytes 49160 | tf_op jit(solution)/shard_map/ppermute | solution.py:49
  3.9 0.7 %collective-permute-start.1 = (f32[8,512]{1,0:T(8,128)S(1)}, f32[8,512]{1,0:T(8,128)S(1)}, u32[]{:S(2)}, u32[]{:S(2)}) collective-permute-start(f32[8,512]{1,0:T(8,128)S(1)} %get-tuple-element.20), channel_id=1, source_target_pairs={{0,1},{1,0},{2,3},{3,2},{4,5},{5,4},{6,7},{7,6},{8,9},{9,8},{10,11... | collective-permute-start | bytes 49160 | tf_op jit(solution)/shard_map/ppermute | solution.py:49
  4.5 1.0 %shard_map.86 = (f32[128,512]{1,0:T(8,128)S(1)}, bf16[256,128]{1,0:T(8,128)(2,1)S(1)}, bf16[128,256]{1,0:T(8,128)(2,1)S(1)}, s32[2,8,128]{2,1,0:T(8,128)S(1)}) custom-call(f32[128,512]{1,0:T(8,128)} %bitcast.16, s32[1,128]{1,0:T(1,128)} %bitcast.19, s32[1,2]{1,0:T(1,128)} %bitcast.20), custom_call_target="tpu_custom_call" | custom-call | bytes 3000000 | tf_op jit(solution)/shard_map/pallas_call | solution.py:32
  5.6 0.0 collective-permute-done.outer_ref
  5.6 0.0 collective-permute-done.1.inner_ref
  5.6 0.9 %shard_map.88 = (f32[128,512]{1,0:T(8,128)S(1)}, f32[256,128]{1,0:T(8,128)}) custom-call(f32[128,512]{1,0:T(8,128)S(1)} %get-tuple-element.18.tile_ref, f32[8,512]{1,0:T(8,128)S(1)} %collective-permute-done.outer_ref, f32[8,512]{1,0:T(8,128)S(1)} %collective-permute-done.1.inner_ref, s32[2,8,128]{2,1,0:T(8,128)S(1)} %get-tuple-element.21.flip_ref, ...), custom_call_target="tpu_custom_call" | custom-call | bytes 3000000 | tf_op jit(solution)/shard_map/pallas_call | solution.py:32
  6.5 6.4 %all-to-all-start = ((f32[8,32,128]{2,1,0:T(8,128)}), f32[8,32,128]{2,1,0:T(8,128)S(1)}, u32[]{:S(2)}, u32[]{:S(2)}) async-start(f32[8,32,128]{2,1,0:T(8,128)} %bitcast.3), calls=%async_computation | async-start | bytes 262144 | tf_op jit(solution)/shard_map/all_to_all | solution.py:381
  12.9 2.4 %shard_map.89 = (bf16[3712,256]{1,0:T(8,128)(2,1)S(1)}, f32[64,256]{1,0:T(8,128)S(1)}, f32[64,256]{1,0:T(8,128)S(1)}, f32[6,64,256]{2,1,0:T(8,128)S(1)}, bf16[12...) custom-call(bf16[58,16384]{1,0:T(8,128)(2,1)} %bitcast.13, s32[1,256]{1,0:T(1,128)} %bitcast.18, f32[57]{0:T(128)} %diff_hbm.1, ...), custom_call_target="tpu_custom_call" | custom-call | bytes 12000000 | tf_op jit(solution)/shard_map/pallas_call | solution.py:32
  15.3 4.9 %all-to-all-done = f32[8,32,128]{2,1,0:T(8,128)S(1)} async-done(((f32[8,32,128]{2,1,0:T(8,128)}), f32[8,32,128]{2,1,0:T(8,128)S(1)}, u32[]{:S(2)}, u32[]{:S(2)}) %all-to-all-start) | async-done | bytes 131104 | tf_op jit(solution)/shard_map/all_to_all | solution.py:381
  20.2 4.1 %shard_map.90 = (f32[256,128]{1,0:T(8,128)}, bf16[3712,256]{1,0:T(8,128)(2,1)S(1)}) custom-call(f32[256,128]{1,0:T(8,128)S(1)} %bitcast.12, bf16[3712,256]{1,0:T(8,128)(2,1)S(1)} %get-tuple-element.26.f_ref, f32[64,256]{1,0:T(8,128)S(1)} %get-tuple-element.27.mean_ref, f32[64,256]{1,0:T(8,128)S(1)} %get-tuple-element.28.sq_ref, ...), custom_call_target="tpu_custom_call", output_to_operand_aliasing={{1}: (1, {})} | custom-call | bytes 15000000 | tf_op jit(solution)/shard_map/pallas_call | solution.py:32
  24.3 3.4 %all-to-all-start.1 = ((f32[8,32,128]{2,1,0:T(8,128)}), f32[8,32,128]{2,1,0:T(8,128)S(1)}, u32[]{:S(2)}, u32[]{:S(2)}) async-start(f32[8,32,128]{2,1,0:T(8,128)} %bitcast.7), calls=%async_computation.1 | async-start | bytes 262144 | tf_op jit(solution)/shard_map/all_to_all | solution.py:417
  27.7 1.9 %shard_map.92 = bf16[58,16384]{1,0:T(8,128)(2,1)} custom-call(bf16[3712,256]{1,0:T(8,128)(2,1)S(1)} %get-tuple-element.33.y_ref), custom_call_target="tpu_custom_call" | custom-call | bytes 9000000 | tf_op jit(solution)/shard_map/pallas_call | solution.py:32
  29.5 5.4 %all-to-all-done.1 = f32[8,32,128]{2,1,0:T(8,128)S(1)} async-done(((f32[8,32,128]{2,1,0:T(8,128)}), f32[8,32,128]{2,1,0:T(8,128)S(1)}, u32[]{:S(2)}, u32[]{:S(2)}) %all-to-all-start.1) | async-done | bytes 131104 | tf_op jit(solution)/shard_map/all_to_all | solution.py:417
  34.9 0.8 %shard_map.91 = f32[128,512]{1,0:T(8,128)} custom-call(f32[128,512]{1,0:T(8,128)S(1)} %get-tuple-element.23.moved_ref, bf16[128,256]{1,0:T(8,128)(2,1)S(1)} %get-tuple-element.24.take_ref, f32[256,128]{1,0:T(8,128)S(1)} %bitcast.11), custom_call_target="tpu_custom_call" | custom-call | bytes 2100000 | tf_op jit(solution)/shard_map/pallas_call | solution.py:32
Async XLA Ops:
  1.4 4.2 %collective-permute-start = (f32[8,512]{1,0:T(8,128)S(1)}, f32[8,512]{1,0:T(8,128)S(1)}, u32[]{:S(2)}, u32[]{:S(2)}) collective-permute-start(f32[8,512]{1,0:T(8,128)S(1)} %get-tuple-element.19), channel_id=1, source_target_pairs={{1,2},{2,1},{3,0},{0,3},{5,6},{6,5},{7,4},{4,7},{9,10},{10,9},{11,... | collective-permute-start | bytes 49160 | tf_op jit(solution)/shard_map/ppermute | solution.py:49
  3.9 1.7 %collective-permute-start.1 = (f32[8,512]{1,0:T(8,128)S(1)}, f32[8,512]{1,0:T(8,128)S(1)}, u32[]{:S(2)}, u32[]{:S(2)}) collective-permute-start(f32[8,512]{1,0:T(8,128)S(1)} %get-tuple-element.20), channel_id=1, source_target_pairs={{0,1},{1,0},{2,3},{3,2},{4,5},{5,4},{6,7},{7,6},{8,9},{9,8},{10,11... | collective-permute-start | bytes 49160 | tf_op jit(solution)/shard_map/ppermute | solution.py:49
  6.5 13.7 %all-to-all-start = ((f32[8,32,128]{2,1,0:T(8,128)}), f32[8,32,128]{2,1,0:T(8,128)S(1)}, u32[]{:S(2)}, u32[]{:S(2)}) async-start(f32[8,32,128]{2,1,0:T(8,128)} %bitcast.3), calls=%async_computation | async-start | bytes 262144 | tf_op jit(solution)/shard_map/all_to_all | solution.py:381
  24.3 10.7 %all-to-all-start.1 = ((f32[8,32,128]{2,1,0:T(8,128)}), f32[8,32,128]{2,1,0:T(8,128)S(1)}, u32[]{:S(2)}, u32[]{:S(2)}) async-start(f32[8,32,128]{2,1,0:T(8,128)} %bitcast.7), calls=%async_computation.1 | async-start | bytes 262144 | tf_op jit(solution)/shard_map/all_to_all | solution.py:417

commit v8 on v7

--- a/solution.py
+++ b/solution.py
@@ -16,6 +16,7 @@
 LANES = 128
 SUB = 8
 NI = CX // SUB
+STAGED = 8
 TZ = 16
 
 kappa_edge = 0.25
@@ -49,6 +50,46 @@
     return lax.ppermute(value, axis, pairs)
 
 
+def pair_kernel(own_ref, got_ref, *pair_refs):
+    rows = pair_refs[0].shape[0] // 2
+    for k, ref in enumerate(pair_refs):
+        here = slice((k + 1) * rows, (k + 2) * rows)
+        ref[:rows, :] = own_ref[here, :]
+        ref[rows:, :] = got_ref[here, :]
+
+
+def exchange(sent):
+    count = lax.axis_size("cols")
+    if len(sent) == 1:
+        whole = sent[0].reshape(count, -1, sent[0].shape[1])
+        return [lax.all_to_all(whole, "cols", split_axis=0, concat_axis=0, tiled=True).reshape(sent[0].shape)]
+
+    def trade(value, k):
+        return lax.ppermute(value, "cols", [(c, c ^ k) for c in range(count)])
+
+    own, other = sent
+    got = trade(other, 1)
+    far_ones = count // 2 - 1
+    pairs = call(
+        pair_kernel,
+        tuple(pltpu.VMEM((2 * own.shape[0] // (count // 2), own.shape[1]), jnp.float32) for _ in range(far_ones)),
+        (own, got),
+        cost=cost(0.2),
+    )
+    return [own, got, *[trade(pair, 2 * (k + 1)) for k, pair in enumerate(pairs)]]
+
+
+def arrived(refs, rows):
+    out = [(0, refs[0][:rows, :]), (1, refs[1][:rows, :])]
+    for k, ref in enumerate(refs[2:]):
+        out += [(2 * (k + 1), ref[:rows, :]), (2 * (k + 1) + 1, ref[rows:, :])]
+    return out
+
+
+def tile_rows(distance, rows):
+    return pl.ds(pl.multiple_of((lax.axis_index("cols") ^ distance) * rows, SUB), rows)
+
+
 def odd_strip():
     return lax.rem(lax.axis_index("edge"), 2)
 
@@ -78,7 +119,7 @@
         copy.wait()
 
 
-def slots_kernel(cap, state_hbm, owners_hbm, orient_hbm, tile_ref, put_ref, take_ref, flip_ref, own_ref, turn_ref, sems):
+def slots_kernel(cap, staged, state_hbm, owners_hbm, orient_hbm, tile_ref, put_ref, take_ref, flip_ref, own_ref, turn_ref, sems):
     per_tile = owners_hbm.shape[1]
     n_slots = put_ref.shape[0]
     copies = [
@@ -93,7 +134,11 @@
     q_down = lax.broadcasted_iota(jnp.int32, (n_slots, per_tile), 0)
     q_across = lax.broadcasted_iota(jnp.int32, (per_tile, n_slots), 1)
     copies[0].wait()
-    across = jnp.broadcast_to(own_ref[...], (per_tile, per_tile))
+    named = own_ref[...]
+    if staged:
+        named = named ^ lax.axis_index("cols")
+        named = (named & 1) * (staged // 2) + (named >> 1)
+    across = jnp.broadcast_to(named, (per_tile, per_tile))
     down = across.T
     same = down == across
     before_col = jnp.where(same & (row < col), 1.0, 0.0)
@@ -110,7 +155,7 @@
     copies[2].wait()
 
 
-def edge_kernel(tile_ref, outer_ref, inner_ref, flip_ref, put_ref, moved_ref, out_ref):
+def edge_kernel(tile_ref, outer_ref, inner_ref, flip_ref, put_ref, moved_ref, *out_refs):
     per_tile, width = tile_ref.shape
 
     odd = odd_strip() == 1
@@ -127,7 +172,10 @@
     below = jnp.concatenate([low, tiles[: per_tile - TW]], axis=0)
     above = jnp.concatenate([tiles[TW:], high], axis=0)
     moved = tiles + kappa_edge * ((above + below) - 2.0 * tiles)
-    out_ref[...] = split_dot(put_ref[...], moved[:, : 2 * L])
+    picked = split_dot(put_ref[...], moved[:, : 2 * L])
+    for k, ref in enumerate(out_refs):
+        rows = ref.shape[0]
+        ref[...] = picked[k * rows : (k + 1) * rows]
     moved_ref[...] = moved
 
 
@@ -212,10 +260,19 @@
         sq_ref[t * TZ : (t + 1) * TZ, :] = square * (1.0 / CX)
 
 
-def physics_kernel(
-    cols_ref, f_ref, mean_ref, sq_ref, coef_ref, wa_ref, wb_ref, tend_ref, y_ref, g_ref, adv_ref, sum_ref
-):
+def physics_kernel(staged, *refs):
+    n_in = staged // 2 + 1 if staged else 1
+    sent_refs, refs = refs[:n_in], refs[n_in:]
+    f_ref, mean_ref, sq_ref, coef_ref, wa_ref, wb_ref, y_ref = refs[:7]
+    back_refs = refs[7:-5]
+    g_ref, adv_ref, sum_ref, cols_ref, tend_ref = refs[-5:]
     slots = cols_ref.shape[0]
+    if staged:
+        rows = slots // staged
+        for distance, value in arrived(sent_refs, rows):
+            cols_ref[tile_rows(distance, rows), :] = value
+    else:
+        cols_ref[...] = sent_refs[0][...]
     halves = slots // LANES
     for h in range(halves):
         lane = slice(h * LANES, (h + 1) * LANES)
@@ -291,6 +348,12 @@
             (((0,), (0,)), ((), ())),
             preferred_element_type=jnp.float32,
         )
+    if staged:
+        for distance in range(staged):
+            place = distance // 2 * rows
+            back_refs[distance % 2][place : place + rows, :] = tend_ref[tile_rows(distance, rows), :]
+    else:
+        back_refs[0][...] = tend_ref[...]
 
 
 def store_kernel(y_ref, crm_hbm, crm_ref, sems):
@@ -320,10 +383,17 @@
         copy.wait()
 
 
-def finish_kernel(moved_ref, take_ref, back_ref, out_hbm, part_ref, sems):
+def finish_kernel(staged, moved_ref, take_ref, *refs):
+    back_refs = refs[:-3]
+    out_hbm, part_ref, sems = refs[-3:]
     rest = pltpu.make_async_copy(moved_ref.at[:, 2 * L :], out_hbm.at[:, 2 * L :], sems.at[0])
     rest.start()
-    part_ref[...] = moved_ref[:, : 2 * L] + split_dot(take_ref[...], back_ref[...])
+    if staged:
+        parts = arrived(back_refs, take_ref.shape[1] // staged)
+        back = jnp.concatenate([part for _, part in parts[0::2] + parts[1::2]], axis=0)
+    else:
+        back = back_refs[0][...]
+    part_ref[...] = moved_ref[:, : 2 * L] + split_dot(take_ref[...], back)
     first = pltpu.make_async_copy(part_ref, out_hbm.at[:, : 2 * L], sems.at[1])
     first.start()
     rest.wait()
@@ -346,6 +416,11 @@
     cap_slots = max(2, 2 * per_tile // n_tiles)
     slots = n_tiles * cap_slots
     rows_f = CZ * CX
+    staged = n_tiles if n_tiles == STAGED else 0
+    if staged:
+        sent = (pltpu.VMEM((slots // 2, 2 * L), f32),) * 2
+    else:
+        sent = (jax.ShapeDtypeStruct((slots, 2 * L), f32),)
     hbm = pl.BlockSpec(memory_space=pltpu.HBM)
     dma = pltpu.SemaphoreType.DMA
     tile = state[0]
@@ -360,7 +435,7 @@
     outer = swap(outer, "edge", 1)
     inner = swap(inner, "edge", 0)
     near, put, take, flip = call(
-        functools.partial(slots_kernel, cap_slots),
+        functools.partial(slots_kernel, cap_slots, staged),
         (
             pltpu.VMEM((per_tile, width), f32),
             pltpu.VMEM((slots, per_tile), bf16),
@@ -372,15 +447,13 @@
         scratch=(pltpu.VMEM((1, per_tile), jnp.int32), pltpu.VMEM((1, 2), jnp.int32), dma((3,))),
         cost=cost(1),
     )
-    moved, outgoing = call(
+    moved, *outgoing = call(
         edge_kernel,
-        (pltpu.VMEM((per_tile, width), f32), jax.ShapeDtypeStruct((slots, 2 * L), f32)),
+        (pltpu.VMEM((per_tile, width), f32), *sent),
         (near, outer, inner, flip, put),
         cost=cost(1),
     )
-    received = lax.all_to_all(
-        outgoing.reshape(n_tiles, cap_slots, 2 * L), "cols", split_axis=0, concat_axis=0, tiled=True
-    ).reshape(slots, 2 * L)
+    received = exchange(outgoing)
     prepared = call(
         prepare_kernel,
         (
@@ -402,21 +475,21 @@
         ),
         cost=cost(4),
     )
-    tend, after = call(
-        physics_kernel,
-        (jax.ShapeDtypeStruct((slots, 2 * L), f32), pltpu.VMEM((rows_f, slots), bf16)),
-        (received, *prepared),
+    after, *tend = call(
+        functools.partial(physics_kernel, staged),
+        (pltpu.VMEM((rows_f, slots), bf16), *sent),
+        (*received, *prepared),
         scratch=(
             pltpu.VMEM((rows_f, slots), f32),
             pltpu.VMEM((5, ZP, slots), f32),
             pltpu.VMEM((2, ZP, slots), f32),
+            pltpu.VMEM((slots, 2 * L), f32),
+            pltpu.VMEM((slots, 2 * L), f32),
         ),
-        aliases={1: 1},
+        aliases={len(received): 0},
         cost=cost(5),
     )
-    returned = lax.all_to_all(
-        tend.reshape(n_tiles, cap_slots, 2 * L), "cols", split_axis=0, concat_axis=0, tiled=True
-    ).reshape(slots, 2 * L)
+    returned = exchange(tend)
     crm_new = call(
         store_kernel,
         jax.ShapeDtypeStruct((CZ, CX * slots), bf16),
@@ -426,9 +499,9 @@
         cost=cost(3),
     )
     new_state = call(
-        finish_kernel,
+        functools.partial(finish_kernel, staged),
         jax.ShapeDtypeStruct((per_tile, width), f32),
-        (moved, take, returned),
+        (moved, take, *returned),
         scratch=(pltpu.VMEM((per_tile, 2 * L), f32), dma((2,))),
         out_specs=hbm,
         cost=cost(0.7),

time: 36.4 us -> 36.6 us (level)
  starting transfers between devices: 12.9 us -> 15.9 us
  Pallas kernels: 11.9 us -> 10.6 us
  waiting for transfers between devices: 10.3 us -> 9 us
    ppermute x0 -> x8, starting transfers between devices: none -> 12.8 us  [trade(): return lax.ppermute(value, 'cols', [(c, c ^ k) for c in range(count)])]
    all_to_all x2 -> x0, waiting for transfers between devices: 10.3 us -> none  [the longest x1 5.4 us: shards(): lax.all_to_all(tend.reshape(n_tiles, cap_slots, 2 * L), 'cols', split_axi...]
    all_to_all x2 -> x0, starting transfers between devices: 9.75 us -> none  [the longest x1 6.38 us: shards(): lax.all_to_all(outgoing.reshape(n_tiles, cap_slots, 2 * L), 'cols', split...]
    ppermute x0 -> x8, waiting for transfers between devices: none -> 8.99 us  [trade(): return lax.ppermute(value, 'cols', [(c, c ^ k) for c in range(count)])]
    pallas_call x7 -> x9, Pallas kernels: 11.9 us -> 10.6 us  [call(): pl.pallas_call(body, out_shape=outs, scratch_shapes=list(scratch), compil...]
  transfers between devices with their start and end apart: 4 -> 10, of which waited for: 2 -> 4; matrix products, arithmetic and copies ran while one was open for 0% -> 0% of each run, Pallas kernels for 15% -> 15%
where the time goes in v8:
time: 36.6 us; the launch traced here: 36.2 us
  starting transfers between devices  15.9 us (43%)
  Pallas kernels  10.6 us (29%)
  waiting for transfers between devices  9 us (25%)
  between operations  0.74 us (2%)
    ppermute x8, starting transfers between devices, trade(): return lax.ppermute(value, 'cols', [(c, c ^ k) for c in range(count)])  12.8 us
    pallas_call x9, Pallas kernels, call(): pl.pallas_call(body, out_shape=outs, scratch_shapes=list(scratch), compil...  10.6 us
    ppermute x8, waiting for transfers between devices, trade(): return lax.ppermute(value, 'cols', [(c, c ^ k) for c in range(count)])  8.99 us
    ppermute x2, starting transfers between devices, swap(): return lax.ppermute(value, axis, pairs)  3.15 us
  transfers between devices with their start and end apart: 10, of which 4 were waited for; matrix products, arithmetic and copies ran while one was open for 0% of the time, Pallas kernels for 15%

profile of v8, /device:TPU:0, one launch (start us, length us, event | category | flops | bytes accessed | tf_op | source)
XLA Modules:
  0.0 36.2 jit_solution(10322829602436297358)
XLA Ops:
  0.6 0.8 %shard_map.87 = (f32[8,512]{1,0:T(8,128)S(1)}, f32[8,512]{1,0:T(8,128)S(1)}) custom-call(f32[128,512]{1,0:T(8,128)} %bitcast.9), custom_call_target="tpu_custom_call" | custom-call | bytes 1500000 | tf_op jit(solution)/shard_map/pallas_call | solution.py:33
  1.4 2.5 %collective-permute-start = (f32[8,512]{1,0:T(8,128)S(1)}, f32[8,512]{1,0:T(8,128)S(1)}, u32[]{:S(2)}, u32[]{:S(2)}) collective-permute-start(f32[8,512]{1,0:T(8,128)S(1)} %get-tuple-element.27), channel_id=1, source_target_pairs={{1,2},{2,1},{3,0},{0,3},{5,6},{6,5},{7,4},{4,7},{9,10},{10,9},{11,... | collective-permute-start | bytes 49160 | tf_op jit(solution)/shard_map/ppermute | solution.py:50
  3.9 0.7 %collective-permute-start.1 = (f32[8,512]{1,0:T(8,128)S(1)}, f32[8,512]{1,0:T(8,128)S(1)}, u32[]{:S(2)}, u32[]{:S(2)}) collective-permute-start(f32[8,512]{1,0:T(8,128)S(1)} %get-tuple-element.28), channel_id=1, source_target_pairs={{0,1},{1,0},{2,3},{3,2},{4,5},{5,4},{6,7},{7,6},{8,9},{9,8},{10,11... | collective-permute-start | bytes 49160 | tf_op jit(solution)/shard_map/ppermute | solution.py:50
  4.5 1.0 %shard_map.86 = (f32[128,512]{1,0:T(8,128)S(1)}, bf16[256,128]{1,0:T(8,128)(2,1)S(1)}, bf16[128,256]{1,0:T(8,128)(2,1)S(1)}, s32[2,8,128]{2,1,0:T(8,128)S(1)}) custom-call(f32[128,512]{1,0:T(8,128)} %bitcast.10, s32[1,128]{1,0:T(1,128)} %bitcast.13, s32[1,2]{1,0:T(1,128)} %bitcast.14), custom_call_target="tpu_custom_call" | custom-call | bytes 3000000 | tf_op jit(solution)/shard_map/pallas_call | solution.py:33
  5.6 0.0 collective-permute-done.1.inner_ref
  5.6 0.2 shard_map.88
  5.8 2.1 %collective-permute-start.2 = (f32[128,128]{1,0:T(8,128)S(1)}, f32[128,128]{1,0:T(8,128)S(1)}, u32[]{:S(2)}, u32[]{:S(2)}) collective-permute-start(f32[128,128]{1,0:T(8,128)S(1)} %get-tuple-element.34), channel_id=1, source_target_pairs={{0,4},{4,0},{8,12},{12,8},{16,20},{20,16},{24,28},{28,24},{1,5},{5... | collective-permute-start | bytes 196616 | tf_op jit(solution)/shard_map/ppermute | solution.py:68
  8.0 2.4 %collective-permute-done.2.got_ref.refs_1_ = f32[128,128]{1,0:T(8,128)S(1)} collective-permute-done((f32[128,128]{1,0:T(8,128)S(1)}, f32[128,128]{1,0:T(8,128)S(1)}, u32[]{:S(2)}, u32[]{:S(2)}) %collective-permute-start.2) | collective-permute-done | bytes 65568 | tf_op jit(solution)/shard_map/ppermute | solution.py:68
  10.4 2.0 %collective-permute-start.3 = (f32[64,128]{1,0:T(8,128)S(1)}, f32[64,128]{1,0:T(8,128)S(1)}, u32[]{:S(2)}, u32[]{:S(2)}) collective-permute-start(f32[64,128]{1,0:T(8,128)S(1)} %get-tuple-element.35), channel_id=1, source_target_pairs={{0,8},{4,12},{8,0},{12,4},{16,24},{20,28},{24,16},{28,20},{1,9},{5... | collective-permute-start | bytes 98312 | tf_op jit(solution)/shard_map/ppermute | solution.py:68
  12.4 2.6 %collective-permute-start.4 = (f32[64,128]{1,0:T(8,128)S(1)}, f32[64,128]{1,0:T(8,128)S(1)}, u32[]{:S(2)}, u32[]{:S(2)}) collective-permute-start(f32[64,128]{1,0:T(8,128)S(1)} %get-tuple-element.36), channel_id=1, source_target_pairs={{0,16},{4,20},{8,24},{12,28},{16,0},{20,4},{24,8},{28,12},{1,17},{... | collective-permute-start | bytes 98312 | tf_op jit(solution)/shard_map/ppermute | solution.py:68
  15.0 0.0 collective-permute-start.5
  15.0 2.5 %shard_map.90 = (bf16[3712,256]{1,0:T(8,128)(2,1)S(1)}, f32[64,256]{1,0:T(8,128)S(1)}, f32[64,256]{1,0:T(8,128)S(1)}, f32[6,64,256]{2,1,0:T(8,128)S(1)}, bf16[12...) custom-call(bf16[58,16384]{1,0:T(8,128)(2,1)} %bitcast.7, s32[1,256]{1,0:T(1,128)} %bitcast.12, f32[57]{0:T(128)} %diff_hbm.1, ...), custom_call_target="tpu_custom_call" | custom-call | bytes 12000000 | tf_op jit(solution)/shard_map/pallas_call | solution.py:33
  17.5 0.0 collective-permute-done.4.refs_3_
  17.5 3.2 %collective-permute-done.5.refs_4_ = f32[64,128]{1,0:T(8,128)S(1)} collective-permute-done((f32[64,128]{1,0:T(8,128)S(1)}, f32[64,128]{1,0:T(8,128)S(1)}, u32[]{:S(2)}, u32[]{:S(2)}) %collective-permute-start.5) | collective-permute-done | bytes 32800 | tf_op jit(solution)/shard_map/ppermute | solution.py:68
  20.7 3.4 %shard_map.91 = (bf16[3712,256]{1,0:T(8,128)(2,1)S(1)}, f32[128,128]{1,0:T(8,128)S(1)}, f32[128,128]{1,0:T(8,128)S(1)}) custom-call(f32[128,128]{1,0:T(8,128)S(1)} %get-tuple-element.33.own_ref.refs_0_, f32[128,128]{1,0:T(8,128)S(1)} %collective-permute-done.2.got_ref.refs_1_, ...), custom_call_target="tpu_custom_call", output_to_operand_aliasing={{0}: (5, {})} | custom-call | bytes 15000000 | tf_op jit(solution)/shard_map/pallas_call | solution.py:33
  24.1 1.6 %collective-permute-start.6 = (f32[128,128]{1,0:T(8,128)S(1)}, f32[128,128]{1,0:T(8,128)S(1)}, u32[]{:S(2)}, u32[]{:S(2)}) collective-permute-start(f32[128,128]{1,0:T(8,128)S(1)} %get-tuple-element.45), channel_id=1, source_target_pairs={{0,4},{4,0},{8,12},{12,8},{16,20},{20,16},{24,28},{28,24},{1,5},{5... | collective-permute-start | bytes 196616 | tf_op jit(solution)/shard_map/ppermute | solution.py:68
  25.7 2.8 %collective-permute-done.6.got_ref.refs_1_ = f32[128,128]{1,0:T(8,128)S(1)} collective-permute-done((f32[128,128]{1,0:T(8,128)S(1)}, f32[128,128]{1,0:T(8,128)S(1)}, u32[]{:S(2)}, u32[]{:S(2)}) %collective-permute-start.6) | collective-permute-done | bytes 65568 | tf_op jit(solution)/shard_map/ppermute | solution.py:68
  28.5 0.1 collective-permute-start.7
  28.5 1.2 %collective-permute-start.8 = (f32[64,128]{1,0:T(8,128)S(1)}, f32[64,128]{1,0:T(8,128)S(1)}, u32[]{:S(2)}, u32[]{:S(2)}) collective-permute-start(f32[64,128]{1,0:T(8,128)S(1)} %get-tuple-element.47), channel_id=1, source_target_pairs={{0,16},{4,20},{8,24},{12,28},{16,0},{20,4},{24,8},{28,12},{1,17},{... | collective-permute-start | bytes 98312 | tf_op jit(solution)/shard_map/ppermute | solution.py:68
  29.7 3.2 %collective-permute-start.9 = (f32[64,128]{1,0:T(8,128)S(1)}, f32[64,128]{1,0:T(8,128)S(1)}, u32[]{:S(2)}, u32[]{:S(2)}) collective-permute-start(f32[64,128]{1,0:T(8,128)S(1)} %get-tuple-element.48), channel_id=1, source_target_pairs={{0,24},{4,28},{8,16},{12,20},{16,8},{20,12},{24,0},{28,4},{1,25},{... | collective-permute-start | bytes 98312 | tf_op jit(solution)/shard_map/ppermute | solution.py:68
  32.9 1.9 %shard_map.94 = bf16[58,16384]{1,0:T(8,128)(2,1)} custom-call(bf16[3712,256]{1,0:T(8,128)(2,1)S(1)} %get-tuple-element.49.y_ref), custom_call_target="tpu_custom_call" | custom-call | bytes 9000000 | tf_op jit(solution)/shard_map/pallas_call | solution.py:33
  34.8 0.0 collective-permute-done.8.refs_3_
  34.8 0.6 %collective-permute-done.9.refs_4_ = f32[64,128]{1,0:T(8,128)S(1)} collective-permute-done((f32[64,128]{1,0:T(8,128)S(1)}, f32[64,128]{1,0:T(8,128)S(1)}, u32[]{:S(2)}, u32[]{:S(2)}) %collective-permute-start.9) | collective-permute-done | bytes 32800 | tf_op jit(solution)/shard_map/ppermute | solution.py:68
  35.4 0.8 %shard_map.93 = f32[128,512]{1,0:T(8,128)} custom-call(f32[128,512]{1,0:T(8,128)S(1)} %get-tuple-element.31.moved_ref, bf16[128,256]{1,0:T(8,128)(2,1)S(1)} %get-tuple-element.32.take_ref, f32[128,128]{1,0:T(8,128)S(1)} %get-tuple-element.44.own_ref.refs_0_, f32[128,128]{1,0:T(8,128)S(1)} %collective-permute-done.6.got_ref.refs_1_, ...), custom_call_target="tpu_custom_call" | custom-call | bytes 2100000 | tf_op jit(solution)/shard_map/pallas_call | solution.py:33
  (5 shorter events, 0.0 us)
Async XLA Ops:
  1.4 4.2 %collective-permute-start = (f32[8,512]{1,0:T(8,128)S(1)}, f32[8,512]{1,0:T(8,128)S(1)}, u32[]{:S(2)}, u32[]{:S(2)}) collective-permute-start(f32[8,512]{1,0:T(8,128)S(1)} %get-tuple-element.27), channel_id=1, source_target_pairs={{1,2},{2,1},{3,0},{0,3},{5,6},{6,5},{7,4},{4,7},{9,10},{10,9},{11,... | collective-permute-start | bytes 49160 | tf_op jit(solution)/shard_map/ppermute | solution.py:50
  3.9 1.7 %collective-permute-start.1 = (f32[8,512]{1,0:T(8,128)S(1)}, f32[8,512]{1,0:T(8,128)S(1)}, u32[]{:S(2)}, u32[]{:S(2)}) collective-permute-start(f32[8,512]{1,0:T(8,128)S(1)} %get-tuple-element.28), channel_id=1, source_target_pairs={{0,1},{1,0},{2,3},{3,2},{4,5},{5,4},{6,7},{7,6},{8,9},{9,8},{10,11... | collective-permute-start | bytes 49160 | tf_op jit(solution)/shard_map/ppermute | solution.py:50
  5.8 4.5 %collective-permute-start.2 = (f32[128,128]{1,0:T(8,128)S(1)}, f32[128,128]{1,0:T(8,128)S(1)}, u32[]{:S(2)}, u32[]{:S(2)}) collective-permute-start(f32[128,128]{1,0:T(8,128)S(1)} %get-tuple-element.34), channel_id=1, source_target_pairs={{0,4},{4,0},{8,12},{12,8},{16,20},{20,16},{24,28},{28,24},{1,5},{5... | collective-permute-start | bytes 196616 | tf_op jit(solution)/shard_map/ppermute | solution.py:68
  10.4 7.1 %collective-permute-start.3 = (f32[64,128]{1,0:T(8,128)S(1)}, f32[64,128]{1,0:T(8,128)S(1)}, u32[]{:S(2)}, u32[]{:S(2)}) collective-permute-start(f32[64,128]{1,0:T(8,128)S(1)} %get-tuple-element.35), channel_id=1, source_target_pairs={{0,8},{4,12},{8,0},{12,4},{16,24},{20,28},{24,16},{28,20},{1,9},{5... | collective-permute-start | bytes 98312 | tf_op jit(solution)/shard_map/ppermute | solution.py:68
  12.4 5.1 %collective-permute-start.4 = (f32[64,128]{1,0:T(8,128)S(1)}, f32[64,128]{1,0:T(8,128)S(1)}, u32[]{:S(2)}, u32[]{:S(2)}) collective-permute-start(f32[64,128]{1,0:T(8,128)S(1)} %get-tuple-element.36), channel_id=1, source_target_pairs={{0,16},{4,20},{8,24},{12,28},{16,0},{20,4},{24,8},{28,12},{1,17},{... | collective-permute-start | bytes 98312 | tf_op jit(solution)/shard_map/ppermute | solution.py:68
  15.0 5.7 %collective-permute-start.5 = (f32[64,128]{1,0:T(8,128)S(1)}, f32[64,128]{1,0:T(8,128)S(1)}, u32[]{:S(2)}, u32[]{:S(2)}) collective-permute-start(f32[64,128]{1,0:T(8,128)S(1)} %get-tuple-element.37), channel_id=1, source_target_pairs={{0,24},{4,28},{8,16},{12,20},{16,8},{20,12},{24,0},{28,4},{1,25},{... | collective-permute-start | bytes 98312 | tf_op jit(solution)/shard_map/ppermute | solution.py:68
  24.1 4.3 %collective-permute-start.6 = (f32[128,128]{1,0:T(8,128)S(1)}, f32[128,128]{1,0:T(8,128)S(1)}, u32[]{:S(2)}, u32[]{:S(2)}) collective-permute-start(f32[128,128]{1,0:T(8,128)S(1)} %get-tuple-element.45), channel_id=1, source_target_pairs={{0,4},{4,0},{8,12},{12,8},{16,20},{20,16},{24,28},{28,24},{1,5},{5... | collective-permute-start | bytes 196616 | tf_op jit(solution)/shard_map/ppermute | solution.py:68
  28.5 6.3 %collective-permute-start.7 = (f32[64,128]{1,0:T(8,128)S(1)}, f32[64,128]{1,0:T(8,128)S(1)}, u32[]{:S(2)}, u32[]{:S(2)}) collective-permute-start(f32[64,128]{1,0:T(8,128)S(1)} %get-tuple-element.46), channel_id=1, source_target_pairs={{0,8},{4,12},{8,0},{12,4},{16,24},{20,28},{24,16},{28,20},{1,9},{5... | collective-permute-start | bytes 98312 | tf_op jit(solution)/shard_map/ppermute | solution.py:68
  28.5 6.3 %collective-permute-start.8 = (f32[64,128]{1,0:T(8,128)S(1)}, f32[64,128]{1,0:T(8,128)S(1)}, u32[]{:S(2)}, u32[]{:S(2)}) collective-permute-start(f32[64,128]{1,0:T(8,128)S(1)} %get-tuple-element.47), channel_id=1, source_target_pairs={{0,16},{4,20},{8,24},{12,28},{16,0},{20,4},{24,8},{28,12},{1,17},{... | collective-permute-start | bytes 98312 | tf_op jit(solution)/shard_map/ppermute | solution.py:68
  29.7 5.7 %collective-permute-start.9 = (f32[64,128]{1,0:T(8,128)S(1)}, f32[64,128]{1,0:T(8,128)S(1)}, u32[]{:S(2)}, u32[]{:S(2)}) collective-permute-start(f32[64,128]{1,0:T(8,128)S(1)} %get-tuple-element.48), channel_id=1, source_target_pairs={{0,24},{4,28},{8,16},{12,20},{16,8},{20,12},{24,0},{28,4},{1,25},{... | collective-permute-start | bytes 98312 | tf_op jit(solution)/shard_map/ppermute | solution.py:68

commit v9 on v8

--- a/solution.py
+++ b/solution.py
@@ -53,7 +53,8 @@
 def pair_kernel(own_ref, got_ref, *pair_refs):
     rows = pair_refs[0].shape[0] // 2
     for k, ref in enumerate(pair_refs):
-        here = slice((k + 1) * rows, (k + 2) * rows)
+        far = len(pair_refs) - k
+        here = slice(far * rows, (far + 1) * rows)
         ref[:rows, :] = own_ref[here, :]
         ref[rows:, :] = got_ref[here, :]
 
@@ -76,12 +77,12 @@
         (own, got),
         cost=cost(0.2),
     )
-    return [own, got, *[trade(pair, 2 * (k + 1)) for k, pair in enumerate(pairs)]]
+    return [own, got, *[trade(pair, 2 * (far_ones - k)) for k, pair in enumerate(pairs)]]
 
 
 def arrived(refs, rows):
     out = [(0, refs[0][:rows, :]), (1, refs[1][:rows, :])]
-    for k, ref in enumerate(refs[2:]):
+    for k, ref in enumerate(refs[:1:-1]):
         out += [(2 * (k + 1), ref[:rows, :]), (2 * (k + 1) + 1, ref[rows:, :])]
     return out
 

time: 36.6 us -> 35.5 us (0.970)
  waiting for transfers between devices: 9 us -> 7.78 us
    ppermute x8, waiting for transfers between devices: 8.99 us -> 7.78 us  [trade(): return lax.ppermute(value, 'cols', [(c, c ^ k) for c in range(count)])]
where the time goes in v9:
time: 35.5 us; the launch traced here: 35.1 us
  starting transfers between devices  16 us (45%)
  Pallas kernels  10.6 us (30%)
  waiting for transfers between devices  7.78 us (22%)
  between operations  0.72 us (2%)
    ppermute x8, starting transfers between devices, trade(): return lax.ppermute(value, 'cols', [(c, c ^ k) for c in range(count)])  12.9 us
    pallas_call x9, Pallas kernels, call(): pl.pallas_call(body, out_shape=outs, scratch_shapes=list(scratch), compil...  10.6 us
    ppermute x8, waiting for transfers between devices, trade(): return lax.ppermute(value, 'cols', [(c, c ^ k) for c in range(count)])  7.78 us
    ppermute x2, starting transfers between devices, swap(): return lax.ppermute(value, axis, pairs)  3.15 us
  transfers between devices with their start and end apart: 10, of which 4 were waited for; matrix products, arithmetic and copies ran while one was open for 0% of the time, Pallas kernels for 15%

profile of v9, /device:TPU:0, one launch (start us, length us, event | category | flops | bytes accessed | tf_op | source)
XLA Modules:
  0.0 35.1 jit_solution(15265648023082001533)
XLA Ops:
  0.6 0.8 %shard_map.87 = (f32[8,512]{1,0:T(8,128)S(1)}, f32[8,512]{1,0:T(8,128)S(1)}) custom-call(f32[128,512]{1,0:T(8,128)} %bitcast.9), custom_call_target="tpu_custom_call" | custom-call | bytes 1500000 | tf_op jit(solution)/shard_map/pallas_call | solution.py:33
  1.4 2.5 %collective-permute-start = (f32[8,512]{1,0:T(8,128)S(1)}, f32[8,512]{1,0:T(8,128)S(1)}, u32[]{:S(2)}, u32[]{:S(2)}) collective-permute-start(f32[8,512]{1,0:T(8,128)S(1)} %get-tuple-element.27), channel_id=1, source_target_pairs={{1,2},{2,1},{3,0},{0,3},{5,6},{6,5},{7,4},{4,7},{9,10},{10,9},{11,... | collective-permute-start | bytes 49160 | tf_op jit(solution)/shard_map/ppermute | solution.py:50
  3.9 0.7 %collective-permute-start.1 = (f32[8,512]{1,0:T(8,128)S(1)}, f32[8,512]{1,0:T(8,128)S(1)}, u32[]{:S(2)}, u32[]{:S(2)}) collective-permute-start(f32[8,512]{1,0:T(8,128)S(1)} %get-tuple-element.28), channel_id=1, source_target_pairs={{0,1},{1,0},{2,3},{3,2},{4,5},{5,4},{6,7},{7,6},{8,9},{9,8},{10,11... | collective-permute-start | bytes 49160 | tf_op jit(solution)/shard_map/ppermute | solution.py:50
  4.5 1.0 %shard_map.86 = (f32[128,512]{1,0:T(8,128)S(1)}, bf16[256,128]{1,0:T(8,128)(2,1)S(1)}, bf16[128,256]{1,0:T(8,128)(2,1)S(1)}, s32[2,8,128]{2,1,0:T(8,128)S(1)}) custom-call(f32[128,512]{1,0:T(8,128)} %bitcast.10, s32[1,128]{1,0:T(1,128)} %bitcast.13, s32[1,2]{1,0:T(1,128)} %bitcast.14), custom_call_target="tpu_custom_call" | custom-call | bytes 3000000 | tf_op jit(solution)/shard_map/pallas_call | solution.py:33
  5.6 0.0 collective-permute-done.outer_ref
  5.6 0.0 collective-permute-done.1.inner_ref
  5.6 0.2 shard_map.88
  5.8 2.1 %collective-permute-start.2 = (f32[128,128]{1,0:T(8,128)S(1)}, f32[128,128]{1,0:T(8,128)S(1)}, u32[]{:S(2)}, u32[]{:S(2)}) collective-permute-start(f32[128,128]{1,0:T(8,128)S(1)} %get-tuple-element.34), channel_id=1, source_target_pairs={{0,4},{4,0},{8,12},{12,8},{16,20},{20,16},{24,28},{28,24},{1,5},{5... | collective-permute-start | bytes 196616 | tf_op jit(solution)/shard_map/ppermute | solution.py:69
  8.0 2.4 %collective-permute-done.2.got_ref.refs_1_ = f32[128,128]{1,0:T(8,128)S(1)} collective-permute-done((f32[128,128]{1,0:T(8,128)S(1)}, f32[128,128]{1,0:T(8,128)S(1)}, u32[]{:S(2)}, u32[]{:S(2)}) %collective-permute-start.2) | collective-permute-done | bytes 65568 | tf_op jit(solution)/shard_map/ppermute | solution.py:69
  10.4 4.1 %collective-permute-start.3 = (f32[64,128]{1,0:T(8,128)S(1)}, f32[64,128]{1,0:T(8,128)S(1)}, u32[]{:S(2)}, u32[]{:S(2)}) collective-permute-start(f32[64,128]{1,0:T(8,128)S(1)} %get-tuple-element.35), channel_id=1, source_target_pairs={{0,24},{4,28},{8,16},{12,20},{16,8},{20,12},{24,0},{28,4},{1,25},{... | collective-permute-start | bytes 98312 | tf_op jit(solution)/shard_map/ppermute | solution.py:69
  14.4 0.6 %collective-permute-start.5 = (f32[64,128]{1,0:T(8,128)S(1)}, f32[64,128]{1,0:T(8,128)S(1)}, u32[]{:S(2)}, u32[]{:S(2)}) collective-permute-start(f32[64,128]{1,0:T(8,128)S(1)} %get-tuple-element.37), channel_id=1, source_target_pairs={{0,8},{4,12},{8,0},{12,4},{16,24},{20,28},{24,16},{28,20},{1,9},{5... | collective-permute-start | bytes 98312 | tf_op jit(solution)/shard_map/ppermute | solution.py:69
  15.1 2.4 %shard_map.90 = (bf16[3712,256]{1,0:T(8,128)(2,1)S(1)}, f32[64,256]{1,0:T(8,128)S(1)}, f32[64,256]{1,0:T(8,128)S(1)}, f32[6,64,256]{2,1,0:T(8,128)S(1)}, bf16[12...) custom-call(bf16[58,16384]{1,0:T(8,128)(2,1)} %bitcast.7, s32[1,256]{1,0:T(1,128)} %bitcast.12, f32[57]{0:T(128)} %diff_hbm.1, ...), custom_call_target="tpu_custom_call" | custom-call | bytes 12000000 | tf_op jit(solution)/shard_map/pallas_call | solution.py:33
  17.5 1.7 %collective-permute-done.4.refs_3_ = f32[64,128]{1,0:T(8,128)S(1)} collective-permute-done((f32[64,128]{1,0:T(8,128)S(1)}, f32[64,128]{1,0:T(8,128)S(1)}, u32[]{:S(2)}, u32[]{:S(2)}) %collective-permute-start.4) | collective-permute-done | bytes 32800 | tf_op jit(solution)/shard_map/ppermute | solution.py:69
  19.2 0.0 collective-permute-done.5.refs_4_
  19.2 3.4 %shard_map.91 = (bf16[3712,256]{1,0:T(8,128)(2,1)S(1)}, f32[128,128]{1,0:T(8,128)S(1)}, f32[128,128]{1,0:T(8,128)S(1)}) custom-call(f32[128,128]{1,0:T(8,128)S(1)} %get-tuple-element.33.own_ref.refs_0_, f32[128,128]{1,0:T(8,128)S(1)} %collective-permute-done.2.got_ref.refs_1_, ...), custom_call_target="tpu_custom_call", output_to_operand_aliasing={{0}: (5, {})} | custom-call | bytes 15000000 | tf_op jit(solution)/shard_map/pallas_call | solution.py:33
  22.7 1.6 %collective-permute-start.6 = (f32[128,128]{1,0:T(8,128)S(1)}, f32[128,128]{1,0:T(8,128)S(1)}, u32[]{:S(2)}, u32[]{:S(2)}) collective-permute-start(f32[128,128]{1,0:T(8,128)S(1)} %get-tuple-element.45), channel_id=1, source_target_pairs={{0,4},{4,0},{8,12},{12,8},{16,20},{20,16},{24,28},{28,24},{1,5},{5... | collective-permute-start | bytes 196616 | tf_op jit(solution)/shard_map/ppermute | solution.py:69
  24.2 2.8 %collective-permute-done.6.got_ref.refs_1_ = f32[128,128]{1,0:T(8,128)S(1)} collective-permute-done((f32[128,128]{1,0:T(8,128)S(1)}, f32[128,128]{1,0:T(8,128)S(1)}, u32[]{:S(2)}, u32[]{:S(2)}) %collective-permute-start.6) | collective-permute-done | bytes 65568 | tf_op jit(solution)/shard_map/ppermute | solution.py:69
  27.0 2.1 %collective-permute-start.7 = (f32[64,128]{1,0:T(8,128)S(1)}, f32[64,128]{1,0:T(8,128)S(1)}, u32[]{:S(2)}, u32[]{:S(2)}) collective-permute-start(f32[64,128]{1,0:T(8,128)S(1)} %get-tuple-element.46), channel_id=1, source_target_pairs={{0,24},{4,28},{8,16},{12,20},{16,8},{20,12},{24,0},{28,4},{1,25},{... | collective-permute-start | bytes 98312 | tf_op jit(solution)/shard_map/ppermute | solution.py:69
  29.1 0.0 collective-permute-start.8
  29.2 2.3 %collective-permute-start.9 = (f32[64,128]{1,0:T(8,128)S(1)}, f32[64,128]{1,0:T(8,128)S(1)}, u32[]{:S(2)}, u32[]{:S(2)}) collective-permute-start(f32[64,128]{1,0:T(8,128)S(1)} %get-tuple-element.48), channel_id=1, source_target_pairs={{0,8},{4,12},{8,0},{12,4},{16,24},{20,28},{24,16},{28,20},{1,9},{5... | collective-permute-start | bytes 98312 | tf_op jit(solution)/shard_map/ppermute | solution.py:69
  31.5 1.9 %shard_map.94 = bf16[58,16384]{1,0:T(8,128)(2,1)} custom-call(bf16[3712,256]{1,0:T(8,128)(2,1)S(1)} %get-tuple-element.49.y_ref), custom_call_target="tpu_custom_call" | custom-call | bytes 9000000 | tf_op jit(solution)/shard_map/pallas_call | solution.py:33
  33.3 0.0 collective-permute-done.7.refs_2_
  33.4 0.9 %collective-permute-done.8.refs_3_ = f32[64,128]{1,0:T(8,128)S(1)} collective-permute-done((f32[64,128]{1,0:T(8,128)S(1)}, f32[64,128]{1,0:T(8,128)S(1)}, u32[]{:S(2)}, u32[]{:S(2)}) %collective-permute-start.8) | collective-permute-done | bytes 32800 | tf_op jit(solution)/shard_map/ppermute | solution.py:69
  34.3 0.8 %shard_map.93 = f32[128,512]{1,0:T(8,128)} custom-call(f32[128,512]{1,0:T(8,128)S(1)} %get-tuple-element.31.moved_ref, bf16[128,256]{1,0:T(8,128)(2,1)S(1)} %get-tuple-element.32.take_ref, f32[128,128]{1,0:T(8,128)S(1)} %get-tuple-element.44.own_ref.refs_0_, f32[128,128]{1,0:T(8,128)S(1)} %collective-permute-done.6.got_ref.refs_1_, ...), custom_call_target="tpu_custom_call" | custom-call | bytes 2100000 | tf_op jit(solution)/shard_map/pallas_call | solution.py:33
  (5 shorter events, 0.0 us)
Async XLA Ops:
  1.4 4.2 %collective-permute-start = (f32[8,512]{1,0:T(8,128)S(1)}, f32[8,512]{1,0:T(8,128)S(1)}, u32[]{:S(2)}, u32[]{:S(2)}) collective-permute-start(f32[8,512]{1,0:T(8,128)S(1)} %get-tuple-element.27), channel_id=1, source_target_pairs={{1,2},{2,1},{3,0},{0,3},{5,6},{6,5},{7,4},{4,7},{9,10},{10,9},{11,... | collective-permute-start | bytes 49160 | tf_op jit(solution)/shard_map/ppermute | solution.py:50
  3.9 1.7 %collective-permute-start.1 = (f32[8,512]{1,0:T(8,128)S(1)}, f32[8,512]{1,0:T(8,128)S(1)}, u32[]{:S(2)}, u32[]{:S(2)}) collective-permute-start(f32[8,512]{1,0:T(8,128)S(1)} %get-tuple-element.28), channel_id=1, source_target_pairs={{0,1},{1,0},{2,3},{3,2},{4,5},{5,4},{6,7},{7,6},{8,9},{9,8},{10,11... | collective-permute-start | bytes 49160 | tf_op jit(solution)/shard_map/ppermute | solution.py:50
  5.8 4.5 %collective-permute-start.2 = (f32[128,128]{1,0:T(8,128)S(1)}, f32[128,128]{1,0:T(8,128)S(1)}, u32[]{:S(2)}, u32[]{:S(2)}) collective-permute-start(f32[128,128]{1,0:T(8,128)S(1)} %get-tuple-element.34), channel_id=1, source_target_pairs={{0,4},{4,0},{8,12},{12,8},{16,20},{20,16},{24,28},{28,24},{1,5},{5... | collective-permute-start | bytes 196616 | tf_op jit(solution)/shard_map/ppermute | solution.py:69
  10.4 7.2 %collective-permute-start.3 = (f32[64,128]{1,0:T(8,128)S(1)}, f32[64,128]{1,0:T(8,128)S(1)}, u32[]{:S(2)}, u32[]{:S(2)}) collective-permute-start(f32[64,128]{1,0:T(8,128)S(1)} %get-tuple-element.35), channel_id=1, source_target_pairs={{0,24},{4,28},{8,16},{12,20},{16,8},{20,12},{24,0},{28,4},{1,25},{... | collective-permute-start | bytes 98312 | tf_op jit(solution)/shard_map/ppermute | solution.py:69
  14.4 4.8 %collective-permute-start.4 = (f32[64,128]{1,0:T(8,128)S(1)}, f32[64,128]{1,0:T(8,128)S(1)}, u32[]{:S(2)}, u32[]{:S(2)}) collective-permute-start(f32[64,128]{1,0:T(8,128)S(1)} %get-tuple-element.36), channel_id=1, source_target_pairs={{0,16},{4,20},{8,24},{12,28},{16,0},{20,4},{24,8},{28,12},{1,17},{... | collective-permute-start | bytes 98312 | tf_op jit(solution)/shard_map/ppermute | solution.py:69
  14.4 4.8 %collective-permute-start.5 = (f32[64,128]{1,0:T(8,128)S(1)}, f32[64,128]{1,0:T(8,128)S(1)}, u32[]{:S(2)}, u32[]{:S(2)}) collective-permute-start(f32[64,128]{1,0:T(8,128)S(1)} %get-tuple-element.37), channel_id=1, source_target_pairs={{0,8},{4,12},{8,0},{12,4},{16,24},{20,28},{24,16},{28,20},{1,9},{5... | collective-permute-start | bytes 98312 | tf_op jit(solution)/shard_map/ppermute | solution.py:69
  22.7 4.3 %collective-permute-start.6 = (f32[128,128]{1,0:T(8,128)S(1)}, f32[128,128]{1,0:T(8,128)S(1)}, u32[]{:S(2)}, u32[]{:S(2)}) collective-permute-start(f32[128,128]{1,0:T(8,128)S(1)} %get-tuple-element.45), channel_id=1, source_target_pairs={{0,4},{4,0},{8,12},{12,8},{16,20},{20,16},{24,28},{28,24},{1,5},{5... | collective-permute-start | bytes 196616 | tf_op jit(solution)/shard_map/ppermute | solution.py:69
  27.0 6.3 %collective-permute-start.7 = (f32[64,128]{1,0:T(8,128)S(1)}, f32[64,128]{1,0:T(8,128)S(1)}, u32[]{:S(2)}, u32[]{:S(2)}) collective-permute-start(f32[64,128]{1,0:T(8,128)S(1)} %get-tuple-element.46), channel_id=1, source_target_pairs={{0,24},{4,28},{8,16},{12,20},{16,8},{20,12},{24,0},{28,4},{1,25},{... | collective-permute-start | bytes 98312 | tf_op jit(solution)/shard_map/ppermute | solution.py:69
  29.1 5.1 %collective-permute-start.8 = (f32[64,128]{1,0:T(8,128)S(1)}, f32[64,128]{1,0:T(8,128)S(1)}, u32[]{:S(2)}, u32[]{:S(2)}) collective-permute-start(f32[64,128]{1,0:T(8,128)S(1)} %get-tuple-element.47), channel_id=1, source_target_pairs={{0,16},{4,20},{8,24},{12,28},{16,0},{20,4},{24,8},{28,12},{1,17},{... | collective-permute-start | bytes 98312 | tf_op jit(solution)/shard_map/ppermute | solution.py:69
  29.2 5.1 %collective-permute-start.9 = (f32[64,128]{1,0:T(8,128)S(1)}, f32[64,128]{1,0:T(8,128)S(1)}, u32[]{:S(2)}, u32[]{:S(2)}) collective-permute-start(f32[64,128]{1,0:T(8,128)S(1)} %get-tuple-element.48), channel_id=1, source_target_pairs={{0,8},{4,12},{8,0},{12,4},{16,24},{20,28},{24,16},{28,20},{1,9},{5... | collective-permute-start | bytes 98312 | tf_op jit(solution)/shard_map/ppermute | solution.py:69

commit v10 on v9

--- a/solution.py
+++ b/solution.py
@@ -50,7 +50,8 @@
     return lax.ppermute(value, axis, pairs)
 
 
-def pair_kernel(own_ref, got_ref, *pair_refs):
+def pair_kernel(ahead, own_ref, got_ref, *refs):
+    pair_refs = refs[ahead:]
     rows = pair_refs[0].shape[0] // 2
     for k, ref in enumerate(pair_refs):
         far = len(pair_refs) - k
@@ -59,7 +60,7 @@
         ref[rows:, :] = got_ref[here, :]
 
 
-def exchange(sent):
+def exchange(sent, ahead=()):
     count = lax.axis_size("cols")
     if len(sent) == 1:
         whole = sent[0].reshape(count, -1, sent[0].shape[1])
@@ -72,9 +73,10 @@
     got = trade(other, 1)
     far_ones = count // 2 - 1
     pairs = call(
-        pair_kernel,
+        functools.partial(pair_kernel, len(ahead)),
         tuple(pltpu.VMEM((2 * own.shape[0] // (count // 2), own.shape[1]), jnp.float32) for _ in range(far_ones)),
-        (own, got),
+        (own, got, *ahead),
+        in_specs=[pl.BlockSpec(memory_space=pltpu.VMEM)] * 2 + [pl.BlockSpec(memory_space=pl.ANY)] * len(ahead),
         cost=cost(0.2),
     )
     return [own, got, *[trade(pair, 2 * (far_ones - k)) for k, pair in enumerate(pairs)]]
@@ -454,7 +456,6 @@
         (near, outer, inner, flip, put),
         cost=cost(1),
     )
-    received = exchange(outgoing)
     prepared = call(
         prepare_kernel,
         (
@@ -476,6 +477,7 @@
         ),
         cost=cost(4),
     )
+    received = exchange(outgoing, prepared[1:2])
     after, *tend = call(
         functools.partial(physics_kernel, staged),
         (pltpu.VMEM((rows_f, slots), bf16), *sent),

time: 35.5 us -> 34.9 us (0.983)
  waiting for transfers between devices: 7.78 us -> 7.31 us
    ppermute x8, waiting for transfers between devices: 7.78 us -> 7.3 us  [trade(): return lax.ppermute(value, 'cols', [(c, c ^ k) for c in range(count)])]
where the time goes in v10:
time: 34.9 us; the launch traced here: 34.5 us
  starting transfers between devices  15.9 us (46%)
  Pallas kernels  10.6 us (30%)
  waiting for transfers between devices  7.31 us (21%)
  between operations  0.73 us (2%)
    ppermute x8, starting transfers between devices, trade(): return lax.ppermute(value, 'cols', [(c, c ^ k) for c in range(count)])  12.8 us
    pallas_call x9, Pallas kernels, call(): pl.pallas_call(body, out_shape=outs, scratch_shapes=list(scratch), compil...  10.6 us
    ppermute x8, waiting for transfers between devices, trade(): return lax.ppermute(value, 'cols', [(c, c ^ k) for c in range(count)])  7.3 us
    ppermute x2, starting transfers between devices, swap(): return lax.ppermute(value, axis, pairs)  3.15 us
  transfers between devices with their start and end apart: 10, of which 4 were waited for; matrix products, arithmetic and copies ran while one was open for 0% of the time, Pallas kernels for 15%

profile of v10, /device:TPU:0, one launch (start us, length us, event | category | flops | bytes accessed | tf_op | source)
XLA Modules:
  0.0 34.5 jit_solution(14284828090370507317)
XLA Ops:
  0.6 0.8 %shard_map.87 = (f32[8,512]{1,0:T(8,128)S(1)}, f32[8,512]{1,0:T(8,128)S(1)}) custom-call(f32[128,512]{1,0:T(8,128)} %bitcast.9), custom_call_target="tpu_custom_call" | custom-call | bytes 1500000 | tf_op jit(solution)/shard_map/pallas_call | solution.py:33
  1.4 2.5 %collective-permute-start = (f32[8,512]{1,0:T(8,128)S(1)}, f32[8,512]{1,0:T(8,128)S(1)}, u32[]{:S(2)}, u32[]{:S(2)}) collective-permute-start(f32[8,512]{1,0:T(8,128)S(1)} %get-tuple-element.27), channel_id=1, source_target_pairs={{1,2},{2,1},{3,0},{0,3},{5,6},{6,5},{7,4},{4,7},{9,10},{10,9},{11,... | collective-permute-start | bytes 49160 | tf_op jit(solution)/shard_map/ppermute | solution.py:50
  3.9 0.7 %collective-permute-start.1 = (f32[8,512]{1,0:T(8,128)S(1)}, f32[8,512]{1,0:T(8,128)S(1)}, u32[]{:S(2)}, u32[]{:S(2)}) collective-permute-start(f32[8,512]{1,0:T(8,128)S(1)} %get-tuple-element.28), channel_id=1, source_target_pairs={{0,1},{1,0},{2,3},{3,2},{4,5},{5,4},{6,7},{7,6},{8,9},{9,8},{10,11... | collective-permute-start | bytes 49160 | tf_op jit(solution)/shard_map/ppermute | solution.py:50
  4.5 1.0 %shard_map.86 = (f32[128,512]{1,0:T(8,128)S(1)}, bf16[256,128]{1,0:T(8,128)(2,1)S(1)}, bf16[128,256]{1,0:T(8,128)(2,1)S(1)}, s32[2,8,128]{2,1,0:T(8,128)S(1)}) custom-call(f32[128,512]{1,0:T(8,128)} %bitcast.10, s32[1,128]{1,0:T(1,128)} %bitcast.13, s32[1,2]{1,0:T(1,128)} %bitcast.14), custom_call_target="tpu_custom_call" | custom-call | bytes 3000000 | tf_op jit(solution)/shard_map/pallas_call | solution.py:33
  5.6 0.0 collective-permute-done.1.inner_ref
  5.6 0.2 shard_map.88
  5.8 2.1 %collective-permute-start.2 = (f32[128,128]{1,0:T(8,128)S(1)}, f32[128,128]{1,0:T(8,128)S(1)}, u32[]{:S(2)}, u32[]{:S(2)}) collective-permute-start(f32[128,128]{1,0:T(8,128)S(1)} %get-tuple-element.34), channel_id=1, source_target_pairs={{0,4},{4,0},{8,12},{12,8},{16,20},{20,16},{24,28},{28,24},{1,5},{5... | collective-permute-start | bytes 196616 | tf_op jit(solution)/shard_map/ppermute | solution.py:70
  8.0 2.5 %shard_map.89 = (bf16[3712,256]{1,0:T(8,128)(2,1)S(1)}, f32[64,256]{1,0:T(8,128)S(1)}, f32[64,256]{1,0:T(8,128)S(1)}, f32[6,64,256]{2,1,0:T(8,128)S(1)}, bf16[12...) custom-call(bf16[58,16384]{1,0:T(8,128)(2,1)} %bitcast.7, s32[1,256]{1,0:T(1,128)} %bitcast.12, f32[57]{0:T(128)} %diff_hbm.1, ...), custom_call_target="tpu_custom_call" | custom-call | bytes 12000000 | tf_op jit(solution)/shard_map/pallas_call | solution.py:33
  10.5 4.0 %collective-permute-start.3 = (f32[64,128]{1,0:T(8,128)S(1)}, f32[64,128]{1,0:T(8,128)S(1)}, u32[]{:S(2)}, u32[]{:S(2)}) collective-permute-start(f32[64,128]{1,0:T(8,128)S(1)} %get-tuple-element.36), channel_id=1, source_target_pairs={{0,24},{4,28},{8,16},{12,20},{16,8},{20,12},{24,0},{28,4},{1,25},{... | collective-permute-start | bytes 98312 | tf_op jit(solution)/shard_map/ppermute | solution.py:70
  14.4 0.0 collective-permute-start.4
  14.4 0.6 %collective-permute-start.5 = (f32[64,128]{1,0:T(8,128)S(1)}, f32[64,128]{1,0:T(8,128)S(1)}, u32[]{:S(2)}, u32[]{:S(2)}) collective-permute-start(f32[64,128]{1,0:T(8,128)S(1)} %get-tuple-element.38), channel_id=1, source_target_pairs={{0,8},{4,12},{8,0},{12,4},{16,24},{20,28},{24,16},{28,20},{1,9},{5... | collective-permute-start | bytes 98312 | tf_op jit(solution)/shard_map/ppermute | solution.py:70
  15.1 1.4 %collective-permute-done.3.refs_2_ = f32[64,128]{1,0:T(8,128)S(1)} collective-permute-done((f32[64,128]{1,0:T(8,128)S(1)}, f32[64,128]{1,0:T(8,128)S(1)}, u32[]{:S(2)}, u32[]{:S(2)}) %collective-permute-start.3) | collective-permute-done | bytes 32800 | tf_op jit(solution)/shard_map/ppermute | solution.py:70
  16.5 2.8 %collective-permute-done.4.refs_3_ = f32[64,128]{1,0:T(8,128)S(1)} collective-permute-done((f32[64,128]{1,0:T(8,128)S(1)}, f32[64,128]{1,0:T(8,128)S(1)}, u32[]{:S(2)}, u32[]{:S(2)}) %collective-permute-start.4) | collective-permute-done | bytes 32800 | tf_op jit(solution)/shard_map/ppermute | solution.py:70
  19.2 0.0 collective-permute-done.5.refs_4_
  19.2 3.4 %shard_map.91 = (bf16[3712,256]{1,0:T(8,128)(2,1)S(1)}, f32[128,128]{1,0:T(8,128)S(1)}, f32[128,128]{1,0:T(8,128)S(1)}) custom-call(f32[128,128]{1,0:T(8,128)S(1)} %get-tuple-element.33.own_ref.refs_0_, f32[128,128]{1,0:T(8,128)S(1)} %collective-permute-done.2.got_ref.refs_1_, ...), custom_call_target="tpu_custom_call", output_to_operand_aliasing={{0}: (5, {})} | custom-call | bytes 15000000 | tf_op jit(solution)/shard_map/pallas_call | solution.py:33
  22.7 1.6 %collective-permute-start.6 = (f32[128,128]{1,0:T(8,128)S(1)}, f32[128,128]{1,0:T(8,128)S(1)}, u32[]{:S(2)}, u32[]{:S(2)}) collective-permute-start(f32[128,128]{1,0:T(8,128)S(1)} %get-tuple-element.45), channel_id=1, source_target_pairs={{0,4},{4,0},{8,12},{12,8},{16,20},{20,16},{24,28},{28,24},{1,5},{5... | collective-permute-start | bytes 196616 | tf_op jit(solution)/shard_map/ppermute | solution.py:70
  24.2 2.8 %collective-permute-done.6.got_ref.refs_1_ = f32[128,128]{1,0:T(8,128)S(1)} collective-permute-done((f32[128,128]{1,0:T(8,128)S(1)}, f32[128,128]{1,0:T(8,128)S(1)}, u32[]{:S(2)}, u32[]{:S(2)}) %collective-permute-start.6) | collective-permute-done | bytes 65568 | tf_op jit(solution)/shard_map/ppermute | solution.py:70
  27.0 1.5 %collective-permute-start.7 = (f32[64,128]{1,0:T(8,128)S(1)}, f32[64,128]{1,0:T(8,128)S(1)}, u32[]{:S(2)}, u32[]{:S(2)}) collective-permute-start(f32[64,128]{1,0:T(8,128)S(1)} %get-tuple-element.46), channel_id=1, source_target_pairs={{0,24},{4,28},{8,16},{12,20},{16,8},{20,12},{24,0},{28,4},{1,25},{... | collective-permute-start | bytes 98312 | tf_op jit(solution)/shard_map/ppermute | solution.py:70
  28.5 0.6 %collective-permute-start.8 = (f32[64,128]{1,0:T(8,128)S(1)}, f32[64,128]{1,0:T(8,128)S(1)}, u32[]{:S(2)}, u32[]{:S(2)}) collective-permute-start(f32[64,128]{1,0:T(8,128)S(1)} %get-tuple-element.47), channel_id=1, source_target_pairs={{0,16},{4,20},{8,24},{12,28},{16,0},{20,4},{24,8},{28,12},{1,17},{... | collective-permute-start | bytes 98312 | tf_op jit(solution)/shard_map/ppermute | solution.py:70
  29.2 2.3 %collective-permute-start.9 = (f32[64,128]{1,0:T(8,128)S(1)}, f32[64,128]{1,0:T(8,128)S(1)}, u32[]{:S(2)}, u32[]{:S(2)}) collective-permute-start(f32[64,128]{1,0:T(8,128)S(1)} %get-tuple-element.48), channel_id=1, source_target_pairs={{0,8},{4,12},{8,0},{12,4},{16,24},{20,28},{24,16},{28,20},{1,9},{5... | collective-permute-start | bytes 98312 | tf_op jit(solution)/shard_map/ppermute | solution.py:70
  31.5 1.9 %shard_map.94 = bf16[58,16384]{1,0:T(8,128)(2,1)} custom-call(bf16[3712,256]{1,0:T(8,128)(2,1)S(1)} %get-tuple-element.49.y_ref), custom_call_target="tpu_custom_call" | custom-call | bytes 9000000 | tf_op jit(solution)/shard_map/pallas_call | solution.py:33
  33.4 0.0 collective-permute-done.8.refs_3_
  33.4 0.3 collective-permute-done.9.refs_4_
  33.7 0.8 %shard_map.93 = f32[128,512]{1,0:T(8,128)} custom-call(f32[128,512]{1,0:T(8,128)S(1)} %get-tuple-element.31.moved_ref, bf16[128,256]{1,0:T(8,128)(2,1)S(1)} %get-tuple-element.32.take_ref, f32[128,128]{1,0:T(8,128)S(1)} %get-tuple-element.44.own_ref.refs_0_, f32[128,128]{1,0:T(8,128)S(1)} %collective-permute-done.6.got_ref.refs_1_, ...), custom_call_target="tpu_custom_call" | custom-call | bytes 2100000 | tf_op jit(solution)/shard_map/pallas_call | solution.py:33
  (5 shorter events, 0.0 us)
Async XLA Ops:
  1.4 4.2 %collective-permute-start = (f32[8,512]{1,0:T(8,128)S(1)}, f32[8,512]{1,0:T(8,128)S(1)}, u32[]{:S(2)}, u32[]{:S(2)}) collective-permute-start(f32[8,512]{1,0:T(8,128)S(1)} %get-tuple-element.27), channel_id=1, source_target_pairs={{1,2},{2,1},{3,0},{0,3},{5,6},{6,5},{7,4},{4,7},{9,10},{10,9},{11,... | collective-permute-start | bytes 49160 | tf_op jit(solution)/shard_map/ppermute | solution.py:50
  3.9 1.7 %collective-permute-start.1 = (f32[8,512]{1,0:T(8,128)S(1)}, f32[8,512]{1,0:T(8,128)S(1)}, u32[]{:S(2)}, u32[]{:S(2)}) collective-permute-start(f32[8,512]{1,0:T(8,128)S(1)} %get-tuple-element.28), channel_id=1, source_target_pairs={{0,1},{1,0},{2,3},{3,2},{4,5},{5,4},{6,7},{7,6},{8,9},{9,8},{10,11... | collective-permute-start | bytes 49160 | tf_op jit(solution)/shard_map/ppermute | solution.py:50
  5.8 4.6 %collective-permute-start.2 = (f32[128,128]{1,0:T(8,128)S(1)}, f32[128,128]{1,0:T(8,128)S(1)}, u32[]{:S(2)}, u32[]{:S(2)}) collective-permute-start(f32[128,128]{1,0:T(8,128)S(1)} %get-tuple-element.34), channel_id=1, source_target_pairs={{0,4},{4,0},{8,12},{12,8},{16,20},{20,16},{24,28},{28,24},{1,5},{5... | collective-permute-start | bytes 196616 | tf_op jit(solution)/shard_map/ppermute | solution.py:70
  10.5 6.0 %collective-permute-start.3 = (f32[64,128]{1,0:T(8,128)S(1)}, f32[64,128]{1,0:T(8,128)S(1)}, u32[]{:S(2)}, u32[]{:S(2)}) collective-permute-start(f32[64,128]{1,0:T(8,128)S(1)} %get-tuple-element.36), channel_id=1, source_target_pairs={{0,24},{4,28},{8,16},{12,20},{16,8},{20,12},{24,0},{28,4},{1,25},{... | collective-permute-start | bytes 98312 | tf_op jit(solution)/shard_map/ppermute | solution.py:70
  14.4 4.8 %collective-permute-start.4 = (f32[64,128]{1,0:T(8,128)S(1)}, f32[64,128]{1,0:T(8,128)S(1)}, u32[]{:S(2)}, u32[]{:S(2)}) collective-permute-start(f32[64,128]{1,0:T(8,128)S(1)} %get-tuple-element.37), channel_id=1, source_target_pairs={{0,16},{4,20},{8,24},{12,28},{16,0},{20,4},{24,8},{28,12},{1,17},{... | collective-permute-start | bytes 98312 | tf_op jit(solution)/shard_map/ppermute | solution.py:70
  14.4 4.8 %collective-permute-start.5 = (f32[64,128]{1,0:T(8,128)S(1)}, f32[64,128]{1,0:T(8,128)S(1)}, u32[]{:S(2)}, u32[]{:S(2)}) collective-permute-start(f32[64,128]{1,0:T(8,128)S(1)} %get-tuple-element.38), channel_id=1, source_target_pairs={{0,8},{4,12},{8,0},{12,4},{16,24},{20,28},{24,16},{28,20},{1,9},{5... | collective-permute-start | bytes 98312 | tf_op jit(solution)/shard_map/ppermute | solution.py:70
  22.7 4.3 %collective-permute-start.6 = (f32[128,128]{1,0:T(8,128)S(1)}, f32[128,128]{1,0:T(8,128)S(1)}, u32[]{:S(2)}, u32[]{:S(2)}) collective-permute-start(f32[128,128]{1,0:T(8,128)S(1)} %get-tuple-element.45), channel_id=1, source_target_pairs={{0,4},{4,0},{8,12},{12,8},{16,20},{20,16},{24,28},{28,24},{1,5},{5... | collective-permute-start | bytes 196616 | tf_op jit(solution)/shard_map/ppermute | solution.py:70
  27.0 6.3 %collective-permute-start.7 = (f32[64,128]{1,0:T(8,128)S(1)}, f32[64,128]{1,0:T(8,128)S(1)}, u32[]{:S(2)}, u32[]{:S(2)}) collective-permute-start(f32[64,128]{1,0:T(8,128)S(1)} %get-tuple-element.46), channel_id=1, source_target_pairs={{0,24},{4,28},{8,16},{12,20},{16,8},{20,12},{24,0},{28,4},{1,25},{... | collective-permute-start | bytes 98312 | tf_op jit(solution)/shard_map/ppermute | solution.py:70
  28.5 4.8 %collective-permute-start.8 = (f32[64,128]{1,0:T(8,128)S(1)}, f32[64,128]{1,0:T(8,128)S(1)}, u32[]{:S(2)}, u32[]{:S(2)}) collective-permute-start(f32[64,128]{1,0:T(8,128)S(1)} %get-tuple-element.47), channel_id=1, source_target_pairs={{0,16},{4,20},{8,24},{12,28},{16,0},{20,4},{24,8},{28,12},{1,17},{... | collective-permute-start | bytes 98312 | tf_op jit(solution)/shard_map/ppermute | solution.py:70
  29.2 4.5 %collective-permute-start.9 = (f32[64,128]{1,0:T(8,128)S(1)}, f32[64,128]{1,0:T(8,128)S(1)}, u32[]{:S(2)}, u32[]{:S(2)}) collective-permute-start(f32[64,128]{1,0:T(8,128)S(1)} %get-tuple-element.48), channel_id=1, source_target_pairs={{0,8},{4,12},{8,0},{12,4},{16,24},{20,28},{24,16},{28,20},{1,9},{5... | collective-permute-start | bytes 98312 | tf_op jit(solution)/shard_map/ppermute | solution.py:70

commit v11 on v10

--- a/solution.py
+++ b/solution.py
@@ -17,6 +17,8 @@
 SUB = 8
 NI = CX // SUB
 STAGED = 8
+ORDER_OUT = (2, 3, 1)
+ORDER_BACK = (3, 2, 1)
 TZ = 16
 
 kappa_edge = 0.25
@@ -50,17 +52,16 @@
     return lax.ppermute(value, axis, pairs)
 
 
-def pair_kernel(ahead, own_ref, got_ref, *refs):
+def pair_kernel(order, ahead, own_ref, got_ref, *refs):
     pair_refs = refs[ahead:]
     rows = pair_refs[0].shape[0] // 2
-    for k, ref in enumerate(pair_refs):
-        far = len(pair_refs) - k
+    for far, ref in zip(order, pair_refs):
         here = slice(far * rows, (far + 1) * rows)
         ref[:rows, :] = own_ref[here, :]
         ref[rows:, :] = got_ref[here, :]
 
 
-def exchange(sent, ahead=()):
+def exchange(sent, order, ahead=()):
     count = lax.axis_size("cols")
     if len(sent) == 1:
         whole = sent[0].reshape(count, -1, sent[0].shape[1])
@@ -71,21 +72,20 @@
 
     own, other = sent
     got = trade(other, 1)
-    far_ones = count // 2 - 1
     pairs = call(
-        functools.partial(pair_kernel, len(ahead)),
-        tuple(pltpu.VMEM((2 * own.shape[0] // (count // 2), own.shape[1]), jnp.float32) for _ in range(far_ones)),
+        functools.partial(pair_kernel, order, len(ahead)),
+        tuple(pltpu.VMEM((2 * own.shape[0] // (count // 2), own.shape[1]), jnp.float32) for _ in order),
         (own, got, *ahead),
         in_specs=[pl.BlockSpec(memory_space=pltpu.VMEM)] * 2 + [pl.BlockSpec(memory_space=pl.ANY)] * len(ahead),
         cost=cost(0.2),
     )
-    return [own, got, *[trade(pair, 2 * (far_ones - k)) for k, pair in enumerate(pairs)]]
-
-
-def arrived(refs, rows):
+    return [own, got, *[trade(pair, 2 * far) for far, pair in zip(order, pairs)]]
+
+
+def arrived(refs, rows, order):
     out = [(0, refs[0][:rows, :]), (1, refs[1][:rows, :])]
-    for k, ref in enumerate(refs[:1:-1]):
-        out += [(2 * (k + 1), ref[:rows, :]), (2 * (k + 1) + 1, ref[rows:, :])]
+    for far, ref in sorted(zip(order, refs[2:]), key=lambda pair: pair[0]):
+        out += [(2 * far, ref[:rows, :]), (2 * far + 1, ref[rows:, :])]
     return out
 
 
@@ -272,7 +272,7 @@
     slots = cols_ref.shape[0]
     if staged:
         rows = slots // staged
-        for distance, value in arrived(sent_refs, rows):
+        for distance, value in arrived(sent_refs, rows, ORDER_OUT):
             cols_ref[tile_rows(distance, rows), :] = value
     else:
         cols_ref[...] = sent_refs[0][...]
@@ -392,7 +392,7 @@
     rest = pltpu.make_async_copy(moved_ref.at[:, 2 * L :], out_hbm.at[:, 2 * L :], sems.at[0])
     rest.start()
     if staged:
-        parts = arrived(back_refs, take_ref.shape[1] // staged)
+        parts = arrived(back_refs, take_ref.shape[1] // staged, ORDER_BACK)
         back = jnp.concatenate([part for _, part in parts[0::2] + parts[1::2]], axis=0)
     else:
         back = back_refs[0][...]
@@ -477,7 +477,7 @@
         ),
         cost=cost(4),
     )
-    received = exchange(outgoing, prepared[1:2])
+    received = exchange(outgoing, ORDER_OUT, prepared[1:2])
     after, *tend = call(
         functools.partial(physics_kernel, staged),
         (pltpu.VMEM((rows_f, slots), bf16), *sent),
@@ -492,7 +492,7 @@
         aliases={len(received): 0},
         cost=cost(5),
     )
-    returned = exchange(tend)
+    returned = exchange(tend, ORDER_BACK)
     crm_new = call(
         store_kernel,
         jax.ShapeDtypeStruct((CZ, CX * slots), bf16),

time: 34.9 us -> 35 us (level)
  no operation moved by 1% of the time
where the time goes in v11:
time: 35 us; the launch traced here: 34.6 us
  starting transfers between devices  15.8 us (45%)
  Pallas kernels  10.6 us (30%)
  waiting for transfers between devices  7.49 us (21%)
  between operations  0.73 us (2%)
    ppermute x8, starting transfers between devices, trade(): return lax.ppermute(value, 'cols', [(c, c ^ k) for c in range(count)])  12.7 us
    pallas_call x9, Pallas kernels, call(): pl.pallas_call(body, out_shape=outs, scratch_shapes=list(scratch), compil...  10.6 us
    ppermute x8, waiting for transfers between devices, trade(): return lax.ppermute(value, 'cols', [(c, c ^ k) for c in range(count)])  7.48 us
    ppermute x2, starting transfers between devices, swap(): return lax.ppermute(value, axis, pairs)  3.15 us
  transfers between devices with their start and end apart: 10, of which 4 were waited for; matrix products, arithmetic and copies ran while one was open for 0% of the time, Pallas kernels for 15%

profile of v11, /device:TPU:0, one launch (start us, length us, event | category | flops | bytes accessed | tf_op | source)
XLA Modules:
  0.0 34.6 jit_solution(10387766757791410366)
XLA Ops:
  0.6 0.8 %shard_map.87 = (f32[8,512]{1,0:T(8,128)S(1)}, f32[8,512]{1,0:T(8,128)S(1)}) custom-call(f32[128,512]{1,0:T(8,128)} %bitcast.9), custom_call_target="tpu_custom_call" | custom-call | bytes 1500000 | tf_op jit(solution)/shard_map/pallas_call | solution.py:35
  1.4 2.5 %collective-permute-start = (f32[8,512]{1,0:T(8,128)S(1)}, f32[8,512]{1,0:T(8,128)S(1)}, u32[]{:S(2)}, u32[]{:S(2)}) collective-permute-start(f32[8,512]{1,0:T(8,128)S(1)} %get-tuple-element.27), channel_id=1, source_target_pairs={{1,2},{2,1},{3,0},{0,3},{5,6},{6,5},{7,4},{4,7},{9,10},{10,9},{11,... | collective-permute-start | bytes 49160 | tf_op jit(solution)/shard_map/ppermute | solution.py:52
  3.9 0.7 %collective-permute-start.1 = (f32[8,512]{1,0:T(8,128)S(1)}, f32[8,512]{1,0:T(8,128)S(1)}, u32[]{:S(2)}, u32[]{:S(2)}) collective-permute-start(f32[8,512]{1,0:T(8,128)S(1)} %get-tuple-element.28), channel_id=1, source_target_pairs={{0,1},{1,0},{2,3},{3,2},{4,5},{5,4},{6,7},{7,6},{8,9},{9,8},{10,11... | collective-permute-start | bytes 49160 | tf_op jit(solution)/shard_map/ppermute | solution.py:52
  4.5 1.0 %shard_map.86 = (f32[128,512]{1,0:T(8,128)S(1)}, bf16[256,128]{1,0:T(8,128)(2,1)S(1)}, bf16[128,256]{1,0:T(8,128)(2,1)S(1)}, s32[2,8,128]{2,1,0:T(8,128)S(1)}) custom-call(f32[128,512]{1,0:T(8,128)} %bitcast.10, s32[1,128]{1,0:T(1,128)} %bitcast.13, s32[1,2]{1,0:T(1,128)} %bitcast.14), custom_call_target="tpu_custom_call" | custom-call | bytes 3000000 | tf_op jit(solution)/shard_map/pallas_call | solution.py:35
  5.6 0.0 collective-permute-done.1.inner_ref
  5.6 0.2 shard_map.88
  5.8 2.1 %collective-permute-start.2 = (f32[128,128]{1,0:T(8,128)S(1)}, f32[128,128]{1,0:T(8,128)S(1)}, u32[]{:S(2)}, u32[]{:S(2)}) collective-permute-start(f32[128,128]{1,0:T(8,128)S(1)} %get-tuple-element.34), channel_id=1, source_target_pairs={{0,4},{4,0},{8,12},{12,8},{16,20},{20,16},{24,28},{28,24},{1,5},{5... | collective-permute-start | bytes 196616 | tf_op jit(solution)/shard_map/ppermute | solution.py:71
  8.0 2.5 %shard_map.89 = (bf16[3712,256]{1,0:T(8,128)(2,1)S(1)}, f32[64,256]{1,0:T(8,128)S(1)}, f32[64,256]{1,0:T(8,128)S(1)}, f32[6,64,256]{2,1,0:T(8,128)S(1)}, bf16[12...) custom-call(bf16[58,16384]{1,0:T(8,128)(2,1)} %bitcast.7, s32[1,256]{1,0:T(1,128)} %bitcast.12, f32[57]{0:T(128)} %diff_hbm.1, ...), custom_call_target="tpu_custom_call" | custom-call | bytes 12000000 | tf_op jit(solution)/shard_map/pallas_call | solution.py:35
  10.5 2.9 %collective-permute-start.3 = (f32[64,128]{1,0:T(8,128)S(1)}, f32[64,128]{1,0:T(8,128)S(1)}, u32[]{:S(2)}, u32[]{:S(2)}) collective-permute-start(f32[64,128]{1,0:T(8,128)S(1)} %get-tuple-element.36), channel_id=1, source_target_pairs={{0,16},{4,20},{8,24},{12,28},{16,0},{20,4},{24,8},{28,12},{1,17},{... | collective-permute-start | bytes 98312 | tf_op jit(solution)/shard_map/ppermute | solution.py:71
  13.4 1.3 %collective-permute-start.4 = (f32[64,128]{1,0:T(8,128)S(1)}, f32[64,128]{1,0:T(8,128)S(1)}, u32[]{:S(2)}, u32[]{:S(2)}) collective-permute-start(f32[64,128]{1,0:T(8,128)S(1)} %get-tuple-element.37), channel_id=1, source_target_pairs={{0,24},{4,28},{8,16},{12,20},{16,8},{20,12},{24,0},{28,4},{1,25},{... | collective-permute-start | bytes 98312 | tf_op jit(solution)/shard_map/ppermute | solution.py:71
  14.8 0.2 collective-permute-start.5
  15.0 0.6 %collective-permute-done.3.refs_2_ = f32[64,128]{1,0:T(8,128)S(1)} collective-permute-done((f32[64,128]{1,0:T(8,128)S(1)}, f32[64,128]{1,0:T(8,128)S(1)}, u32[]{:S(2)}, u32[]{:S(2)}) %collective-permute-start.3) | collective-permute-done | bytes 32800 | tf_op jit(solution)/shard_map/ppermute | solution.py:71
  15.6 3.6 %collective-permute-done.4.refs_3_ = f32[64,128]{1,0:T(8,128)S(1)} collective-permute-done((f32[64,128]{1,0:T(8,128)S(1)}, f32[64,128]{1,0:T(8,128)S(1)}, u32[]{:S(2)}, u32[]{:S(2)}) %collective-permute-start.4) | collective-permute-done | bytes 32800 | tf_op jit(solution)/shard_map/ppermute | solution.py:71
  19.1 0.0 collective-permute-done.5.refs_4_
  19.1 3.4 %shard_map.91 = (bf16[3712,256]{1,0:T(8,128)(2,1)S(1)}, f32[128,128]{1,0:T(8,128)S(1)}, f32[128,128]{1,0:T(8,128)S(1)}) custom-call(f32[128,128]{1,0:T(8,128)S(1)} %get-tuple-element.33.own_ref.refs_0_, f32[128,128]{1,0:T(8,128)S(1)} %collective-permute-done.2.got_ref.refs_1_, ...), custom_call_target="tpu_custom_call", output_to_operand_aliasing={{0}: (5, {})} | custom-call | bytes 15000000 | tf_op jit(solution)/shard_map/pallas_call | solution.py:35
  22.6 1.6 %collective-permute-start.6 = (f32[128,128]{1,0:T(8,128)S(1)}, f32[128,128]{1,0:T(8,128)S(1)}, u32[]{:S(2)}, u32[]{:S(2)}) collective-permute-start(f32[128,128]{1,0:T(8,128)S(1)} %get-tuple-element.45), channel_id=1, source_target_pairs={{0,4},{4,0},{8,12},{12,8},{16,20},{20,16},{24,28},{28,24},{1,5},{5... | collective-permute-start | bytes 196616 | tf_op jit(solution)/shard_map/ppermute | solution.py:71
  24.1 2.8 %collective-permute-done.6.got_ref.refs_1_ = f32[128,128]{1,0:T(8,128)S(1)} collective-permute-done((f32[128,128]{1,0:T(8,128)S(1)}, f32[128,128]{1,0:T(8,128)S(1)}, u32[]{:S(2)}, u32[]{:S(2)}) %collective-permute-start.6) | collective-permute-done | bytes 65568 | tf_op jit(solution)/shard_map/ppermute | solution.py:71
  26.9 2.1 %collective-permute-start.7 = (f32[64,128]{1,0:T(8,128)S(1)}, f32[64,128]{1,0:T(8,128)S(1)}, u32[]{:S(2)}, u32[]{:S(2)}) collective-permute-start(f32[64,128]{1,0:T(8,128)S(1)} %get-tuple-element.46), channel_id=1, source_target_pairs={{0,24},{4,28},{8,16},{12,20},{16,8},{20,12},{24,0},{28,4},{1,25},{... | collective-permute-start | bytes 98312 | tf_op jit(solution)/shard_map/ppermute | solution.py:71
  29.0 2.4 %collective-permute-start.9 = (f32[64,128]{1,0:T(8,128)S(1)}, f32[64,128]{1,0:T(8,128)S(1)}, u32[]{:S(2)}, u32[]{:S(2)}) collective-permute-start(f32[64,128]{1,0:T(8,128)S(1)} %get-tuple-element.48), channel_id=1, source_target_pairs={{0,8},{4,12},{8,0},{12,4},{16,24},{20,28},{24,16},{28,20},{1,9},{5... | collective-permute-start | bytes 98312 | tf_op jit(solution)/shard_map/ppermute | solution.py:71
  31.3 1.9 %shard_map.94 = bf16[58,16384]{1,0:T(8,128)(2,1)} custom-call(bf16[3712,256]{1,0:T(8,128)(2,1)S(1)} %get-tuple-element.49.y_ref), custom_call_target="tpu_custom_call" | custom-call | bytes 9000000 | tf_op jit(solution)/shard_map/pallas_call | solution.py:35
  33.2 0.0 collective-permute-done.7.refs_2_
  33.2 0.6 %collective-permute-done.8.refs_3_ = f32[64,128]{1,0:T(8,128)S(1)} collective-permute-done((f32[64,128]{1,0:T(8,128)S(1)}, f32[64,128]{1,0:T(8,128)S(1)}, u32[]{:S(2)}, u32[]{:S(2)}) %collective-permute-start.8) | collective-permute-done | bytes 32800 | tf_op jit(solution)/shard_map/ppermute | solution.py:71
  33.8 0.0 collective-permute-done.9.refs_4_
  33.8 0.8 %shard_map.93 = f32[128,512]{1,0:T(8,128)} custom-call(f32[128,512]{1,0:T(8,128)S(1)} %get-tuple-element.31.moved_ref, bf16[128,256]{1,0:T(8,128)(2,1)S(1)} %get-tuple-element.32.take_ref, f32[128,128]{1,0:T(8,128)S(1)} %get-tuple-element.44.own_ref.refs_0_, f32[128,128]{1,0:T(8,128)S(1)} %collective-permute-done.6.got_ref.refs_1_, ...), custom_call_target="tpu_custom_call" | custom-call | bytes 2100000 | tf_op jit(solution)/shard_map/pallas_call | solution.py:35
  (5 shorter events, 0.0 us)
Async XLA Ops:
  1.4 4.2 %collective-permute-start = (f32[8,512]{1,0:T(8,128)S(1)}, f32[8,512]{1,0:T(8,128)S(1)}, u32[]{:S(2)}, u32[]{:S(2)}) collective-permute-start(f32[8,512]{1,0:T(8,128)S(1)} %get-tuple-element.27), channel_id=1, source_target_pairs={{1,2},{2,1},{3,0},{0,3},{5,6},{6,5},{7,4},{4,7},{9,10},{10,9},{11,... | collective-permute-start | bytes 49160 | tf_op jit(solution)/shard_map/ppermute | solution.py:52
  3.9 1.7 %collective-permute-start.1 = (f32[8,512]{1,0:T(8,128)S(1)}, f32[8,512]{1,0:T(8,128)S(1)}, u32[]{:S(2)}, u32[]{:S(2)}) collective-permute-start(f32[8,512]{1,0:T(8,128)S(1)} %get-tuple-element.28), channel_id=1, source_target_pairs={{0,1},{1,0},{2,3},{3,2},{4,5},{5,4},{6,7},{7,6},{8,9},{9,8},{10,11... | collective-permute-start | bytes 49160 | tf_op jit(solution)/shard_map/ppermute | solution.py:52
  5.8 4.6 %collective-permute-start.2 = (f32[128,128]{1,0:T(8,128)S(1)}, f32[128,128]{1,0:T(8,128)S(1)}, u32[]{:S(2)}, u32[]{:S(2)}) collective-permute-start(f32[128,128]{1,0:T(8,128)S(1)} %get-tuple-element.34), channel_id=1, source_target_pairs={{0,4},{4,0},{8,12},{12,8},{16,20},{20,16},{24,28},{28,24},{1,5},{5... | collective-permute-start | bytes 196616 | tf_op jit(solution)/shard_map/ppermute | solution.py:71
  10.5 5.1 %collective-permute-start.3 = (f32[64,128]{1,0:T(8,128)S(1)}, f32[64,128]{1,0:T(8,128)S(1)}, u32[]{:S(2)}, u32[]{:S(2)}) collective-permute-start(f32[64,128]{1,0:T(8,128)S(1)} %get-tuple-element.36), channel_id=1, source_target_pairs={{0,16},{4,20},{8,24},{12,28},{16,0},{20,4},{24,8},{28,12},{1,17},{... | collective-permute-start | bytes 98312 | tf_op jit(solution)/shard_map/ppermute | solution.py:71
  13.4 5.7 %collective-permute-start.4 = (f32[64,128]{1,0:T(8,128)S(1)}, f32[64,128]{1,0:T(8,128)S(1)}, u32[]{:S(2)}, u32[]{:S(2)}) collective-permute-start(f32[64,128]{1,0:T(8,128)S(1)} %get-tuple-element.37), channel_id=1, source_target_pairs={{0,24},{4,28},{8,16},{12,20},{16,8},{20,12},{24,0},{28,4},{1,25},{... | collective-permute-start | bytes 98312 | tf_op jit(solution)/shard_map/ppermute | solution.py:71
  14.8 4.4 %collective-permute-start.5 = (f32[64,128]{1,0:T(8,128)S(1)}, f32[64,128]{1,0:T(8,128)S(1)}, u32[]{:S(2)}, u32[]{:S(2)}) collective-permute-start(f32[64,128]{1,0:T(8,128)S(1)} %get-tuple-element.38), channel_id=1, source_target_pairs={{0,8},{4,12},{8,0},{12,4},{16,24},{20,28},{24,16},{28,20},{1,9},{5... | collective-permute-start | bytes 98312 | tf_op jit(solution)/shard_map/ppermute | solution.py:71
  22.6 4.3 %collective-permute-start.6 = (f32[128,128]{1,0:T(8,128)S(1)}, f32[128,128]{1,0:T(8,128)S(1)}, u32[]{:S(2)}, u32[]{:S(2)}) collective-permute-start(f32[128,128]{1,0:T(8,128)S(1)} %get-tuple-element.45), channel_id=1, source_target_pairs={{0,4},{4,0},{8,12},{12,8},{16,20},{20,16},{24,28},{28,24},{1,5},{5... | collective-permute-start | bytes 196616 | tf_op jit(solution)/shard_map/ppermute | solution.py:71
  26.9 6.3 %collective-permute-start.7 = (f32[64,128]{1,0:T(8,128)S(1)}, f32[64,128]{1,0:T(8,128)S(1)}, u32[]{:S(2)}, u32[]{:S(2)}) collective-permute-start(f32[64,128]{1,0:T(8,128)S(1)} %get-tuple-element.46), channel_id=1, source_target_pairs={{0,24},{4,28},{8,16},{12,20},{16,8},{20,12},{24,0},{28,4},{1,25},{... | collective-permute-start | bytes 98312 | tf_op jit(solution)/shard_map/ppermute | solution.py:71
  29.0 4.8 %collective-permute-start.8 = (f32[64,128]{1,0:T(8,128)S(1)}, f32[64,128]{1,0:T(8,128)S(1)}, u32[]{:S(2)}, u32[]{:S(2)}) collective-permute-start(f32[64,128]{1,0:T(8,128)S(1)} %get-tuple-element.47), channel_id=1, source_target_pairs={{0,16},{4,20},{8,24},{12,28},{16,0},{20,4},{24,8},{28,12},{1,17},{... | collective-permute-start | bytes 98312 | tf_op jit(solution)/shard_map/ppermute | solution.py:71
  29.0 4.8 %collective-permute-start.9 = (f32[64,128]{1,0:T(8,128)S(1)}, f32[64,128]{1,0:T(8,128)S(1)}, u32[]{:S(2)}, u32[]{:S(2)}) collective-permute-start(f32[64,128]{1,0:T(8,128)S(1)} %get-tuple-element.48), channel_id=1, source_target_pairs={{0,8},{4,12},{8,0},{12,4},{16,24},{20,28},{24,16},{28,20},{1,9},{5... | collective-permute-start | bytes 98312 | tf_op jit(solution)/shard_map/ppermute | solution.py:71

commit v12 on v11

--- a/solution.py
+++ b/solution.py
@@ -17,8 +17,8 @@
 SUB = 8
 NI = CX // SUB
 STAGED = 8
-ORDER_OUT = (2, 3, 1)
-ORDER_BACK = (3, 2, 1)
+ORDER_OUT = (3, 2, 1)
+ORDER_BACK = (2, 3, 1)
 TZ = 16
 
 kappa_edge = 0.25

time: 35 us -> 36 us (1.029)
  waiting for transfers between devices: 7.49 us -> 9.32 us
  starting transfers between devices: 15.8 us -> 15 us
    ppermute x8, waiting for transfers between devices: 7.48 us -> 9.31 us  [trade(): return lax.ppermute(value, 'cols', [(c, c ^ k) for c in range(count)])]
    ppermute x8, starting transfers between devices: 12.7 us -> 11.9 us  [trade(): return lax.ppermute(value, 'cols', [(c, c ^ k) for c in range(count)])]
where the time goes in v12:
time: 36 us; the launch traced here: 35.6 us
  starting transfers between devices  15 us (42%)
  Pallas kernels  10.6 us (29%)
  waiting for transfers between devices  9.32 us (26%)
  between operations  0.73 us (2%)
    ppermute x8, starting transfers between devices, trade(): return lax.ppermute(value, 'cols', [(c, c ^ k) for c in range(count)])  11.9 us
    pallas_call x9, Pallas kernels, call(): pl.pallas_call(body, out_shape=outs, scratch_shapes=list(scratch), compil...  10.6 us
    ppermute x8, waiting for transfers between devices, trade(): return lax.ppermute(value, 'cols', [(c, c ^ k) for c in range(count)])  9.31 us
    ppermute x2, starting transfers between devices, swap(): return lax.ppermute(value, axis, pairs)  3.15 us
  transfers between devices with their start and end apart: 10, of which 4 were waited for; matrix products, arithmetic and copies ran while one was open for 0% of the time, Pallas kernels for 15%

profile of v12, /device:TPU:0, one launch (start us, length us, event | category | flops | bytes accessed | tf_op | source)
XLA Modules:
  0.0 35.6 jit_solution(1345427011993566618)
XLA Ops:
  0.6 0.8 %shard_map.87 = (f32[8,512]{1,0:T(8,128)S(1)}, f32[8,512]{1,0:T(8,128)S(1)}) custom-call(f32[128,512]{1,0:T(8,128)} %bitcast.9), custom_call_target="tpu_custom_call" | custom-call | bytes 1500000 | tf_op jit(solution)/shard_map/pallas_call | solution.py:35
  1.4 2.5 %collective-permute-start = (f32[8,512]{1,0:T(8,128)S(1)}, f32[8,512]{1,0:T(8,128)S(1)}, u32[]{:S(2)}, u32[]{:S(2)}) collective-permute-start(f32[8,512]{1,0:T(8,128)S(1)} %get-tuple-element.27), channel_id=1, source_target_pairs={{1,2},{2,1},{3,0},{0,3},{5,6},{6,5},{7,4},{4,7},{9,10},{10,9},{11,... | collective-permute-start | bytes 49160 | tf_op jit(solution)/shard_map/ppermute | solution.py:52
  3.9 0.7 %collective-permute-start.1 = (f32[8,512]{1,0:T(8,128)S(1)}, f32[8,512]{1,0:T(8,128)S(1)}, u32[]{:S(2)}, u32[]{:S(2)}) collective-permute-start(f32[8,512]{1,0:T(8,128)S(1)} %get-tuple-element.28), channel_id=1, source_target_pairs={{0,1},{1,0},{2,3},{3,2},{4,5},{5,4},{6,7},{7,6},{8,9},{9,8},{10,11... | collective-permute-start | bytes 49160 | tf_op jit(solution)/shard_map/ppermute | solution.py:52
  4.5 1.0 %shard_map.86 = (f32[128,512]{1,0:T(8,128)S(1)}, bf16[256,128]{1,0:T(8,128)(2,1)S(1)}, bf16[128,256]{1,0:T(8,128)(2,1)S(1)}, s32[2,8,128]{2,1,0:T(8,128)S(1)}) custom-call(f32[128,512]{1,0:T(8,128)} %bitcast.10, s32[1,128]{1,0:T(1,128)} %bitcast.13, s32[1,2]{1,0:T(1,128)} %bitcast.14), custom_call_target="tpu_custom_call" | custom-call | bytes 3000000 | tf_op jit(solution)/shard_map/pallas_call | solution.py:35
  5.6 0.0 collective-permute-done.outer_ref
  5.6 0.0 collective-permute-done.1.inner_ref
  5.6 0.2 shard_map.88
  5.8 2.1 %collective-permute-start.2 = (f32[128,128]{1,0:T(8,128)S(1)}, f32[128,128]{1,0:T(8,128)S(1)}, u32[]{:S(2)}, u32[]{:S(2)}) collective-permute-start(f32[128,128]{1,0:T(8,128)S(1)} %get-tuple-element.34), channel_id=1, source_target_pairs={{0,4},{4,0},{8,12},{12,8},{16,20},{20,16},{24,28},{28,24},{1,5},{5... | collective-permute-start | bytes 196616 | tf_op jit(solution)/shard_map/ppermute | solution.py:71
  8.0 2.5 %shard_map.89 = (bf16[3712,256]{1,0:T(8,128)(2,1)S(1)}, f32[64,256]{1,0:T(8,128)S(1)}, f32[64,256]{1,0:T(8,128)S(1)}, f32[6,64,256]{2,1,0:T(8,128)S(1)}, bf16[12...) custom-call(bf16[58,16384]{1,0:T(8,128)(2,1)} %bitcast.7, s32[1,256]{1,0:T(1,128)} %bitcast.12, f32[57]{0:T(128)} %diff_hbm.1, ...), custom_call_target="tpu_custom_call" | custom-call | bytes 12000000 | tf_op jit(solution)/shard_map/pallas_call | solution.py:35
  10.5 4.0 %collective-permute-start.3 = (f32[64,128]{1,0:T(8,128)S(1)}, f32[64,128]{1,0:T(8,128)S(1)}, u32[]{:S(2)}, u32[]{:S(2)}) collective-permute-start(f32[64,128]{1,0:T(8,128)S(1)} %get-tuple-element.36), channel_id=1, source_target_pairs={{0,24},{4,28},{8,16},{12,20},{16,8},{20,12},{24,0},{28,4},{1,25},{... | collective-permute-start | bytes 98312 | tf_op jit(solution)/shard_map/ppermute | solution.py:71
  14.4 0.0 collective-permute-start.4
  14.4 0.6 %collective-permute-start.5 = (f32[64,128]{1,0:T(8,128)S(1)}, f32[64,128]{1,0:T(8,128)S(1)}, u32[]{:S(2)}, u32[]{:S(2)}) collective-permute-start(f32[64,128]{1,0:T(8,128)S(1)} %get-tuple-element.38), channel_id=1, source_target_pairs={{0,8},{4,12},{8,0},{12,4},{16,24},{20,28},{24,16},{28,20},{1,9},{5... | collective-permute-start | bytes 98312 | tf_op jit(solution)/shard_map/ppermute | solution.py:71
  15.1 1.4 %collective-permute-done.3.refs_2_ = f32[64,128]{1,0:T(8,128)S(1)} collective-permute-done((f32[64,128]{1,0:T(8,128)S(1)}, f32[64,128]{1,0:T(8,128)S(1)}, u32[]{:S(2)}, u32[]{:S(2)}) %collective-permute-start.3) | collective-permute-done | bytes 32800 | tf_op jit(solution)/shard_map/ppermute | solution.py:71
  16.5 2.8 %collective-permute-done.4.refs_3_ = f32[64,128]{1,0:T(8,128)S(1)} collective-permute-done((f32[64,128]{1,0:T(8,128)S(1)}, f32[64,128]{1,0:T(8,128)S(1)}, u32[]{:S(2)}, u32[]{:S(2)}) %collective-permute-start.4) | collective-permute-done | bytes 32800 | tf_op jit(solution)/shard_map/ppermute | solution.py:71
  19.2 3.4 %shard_map.91 = (bf16[3712,256]{1,0:T(8,128)(2,1)S(1)}, f32[128,128]{1,0:T(8,128)S(1)}, f32[128,128]{1,0:T(8,128)S(1)}) custom-call(f32[128,128]{1,0:T(8,128)S(1)} %get-tuple-element.33.own_ref.refs_0_, f32[128,128]{1,0:T(8,128)S(1)} %collective-permute-done.2.got_ref.refs_1_, ...), custom_call_target="tpu_custom_call", output_to_operand_aliasing={{0}: (5, {})} | custom-call | bytes 15000000 | tf_op jit(solution)/shard_map/pallas_call | solution.py:35
  22.7 1.6 %collective-permute-start.6 = (f32[128,128]{1,0:T(8,128)S(1)}, f32[128,128]{1,0:T(8,128)S(1)}, u32[]{:S(2)}, u32[]{:S(2)}) collective-permute-start(f32[128,128]{1,0:T(8,128)S(1)} %get-tuple-element.45), channel_id=1, source_target_pairs={{0,4},{4,0},{8,12},{12,8},{16,20},{20,16},{24,28},{28,24},{1,5},{5... | collective-permute-start | bytes 196616 | tf_op jit(solution)/shard_map/ppermute | solution.py:71
  24.2 2.8 %collective-permute-done.6.got_ref.refs_1_ = f32[128,128]{1,0:T(8,128)S(1)} collective-permute-done((f32[128,128]{1,0:T(8,128)S(1)}, f32[128,128]{1,0:T(8,128)S(1)}, u32[]{:S(2)}, u32[]{:S(2)}) %collective-permute-start.6) | collective-permute-done | bytes 65568 | tf_op jit(solution)/shard_map/ppermute | solution.py:71
  27.0 2.1 %collective-permute-start.7 = (f32[64,128]{1,0:T(8,128)S(1)}, f32[64,128]{1,0:T(8,128)S(1)}, u32[]{:S(2)}, u32[]{:S(2)}) collective-permute-start(f32[64,128]{1,0:T(8,128)S(1)} %get-tuple-element.46), channel_id=1, source_target_pairs={{0,16},{4,20},{8,24},{12,28},{16,0},{20,4},{24,8},{28,12},{1,17},{... | collective-permute-start | bytes 98312 | tf_op jit(solution)/shard_map/ppermute | solution.py:71
  29.1 0.1 collective-permute-start.8
  29.2 1.3 %collective-permute-start.9 = (f32[64,128]{1,0:T(8,128)S(1)}, f32[64,128]{1,0:T(8,128)S(1)}, u32[]{:S(2)}, u32[]{:S(2)}) collective-permute-start(f32[64,128]{1,0:T(8,128)S(1)} %get-tuple-element.48), channel_id=1, source_target_pairs={{0,8},{4,12},{8,0},{12,4},{16,24},{20,28},{24,16},{28,20},{1,9},{5... | collective-permute-start | bytes 98312 | tf_op jit(solution)/shard_map/ppermute | solution.py:71
  30.6 1.9 %shard_map.94 = bf16[58,16384]{1,0:T(8,128)(2,1)} custom-call(bf16[3712,256]{1,0:T(8,128)(2,1)S(1)} %get-tuple-element.49.y_ref), custom_call_target="tpu_custom_call" | custom-call | bytes 9000000 | tf_op jit(solution)/shard_map/pallas_call | solution.py:35
  32.5 2.4 %collective-permute-done.8.refs_3_ = f32[64,128]{1,0:T(8,128)S(1)} collective-permute-done((f32[64,128]{1,0:T(8,128)S(1)}, f32[64,128]{1,0:T(8,128)S(1)}, u32[]{:S(2)}, u32[]{:S(2)}) %collective-permute-start.8) | collective-permute-done | bytes 32800 | tf_op jit(solution)/shard_map/ppermute | solution.py:71
  34.8 0.0 collective-permute-done.9.refs_4_
  34.8 0.8 %shard_map.93 = f32[128,512]{1,0:T(8,128)} custom-call(f32[128,512]{1,0:T(8,128)S(1)} %get-tuple-element.31.moved_ref, bf16[128,256]{1,0:T(8,128)(2,1)S(1)} %get-tuple-element.32.take_ref, f32[128,128]{1,0:T(8,128)S(1)} %get-tuple-element.44.own_ref.refs_0_, f32[128,128]{1,0:T(8,128)S(1)} %collective-permute-done.6.got_ref.refs_1_, ...), custom_call_target="tpu_custom_call" | custom-call | bytes 2100000 | tf_op jit(solution)/shard_map/pallas_call | solution.py:35
  (5 shorter events, 0.0 us)
Async XLA Ops:
  1.4 4.2 %collective-permute-start = (f32[8,512]{1,0:T(8,128)S(1)}, f32[8,512]{1,0:T(8,128)S(1)}, u32[]{:S(2)}, u32[]{:S(2)}) collective-permute-start(f32[8,512]{1,0:T(8,128)S(1)} %get-tuple-element.27), channel_id=1, source_target_pairs={{1,2},{2,1},{3,0},{0,3},{5,6},{6,5},{7,4},{4,7},{9,10},{10,9},{11,... | collective-permute-start | bytes 49160 | tf_op jit(solution)/shard_map/ppermute | solution.py:52
  3.9 1.7 %collective-permute-start.1 = (f32[8,512]{1,0:T(8,128)S(1)}, f32[8,512]{1,0:T(8,128)S(1)}, u32[]{:S(2)}, u32[]{:S(2)}) collective-permute-start(f32[8,512]{1,0:T(8,128)S(1)} %get-tuple-element.28), channel_id=1, source_target_pairs={{0,1},{1,0},{2,3},{3,2},{4,5},{5,4},{6,7},{7,6},{8,9},{9,8},{10,11... | collective-permute-start | bytes 49160 | tf_op jit(solution)/shard_map/ppermute | solution.py:52
  5.8 4.6 %collective-permute-start.2 = (f32[128,128]{1,0:T(8,128)S(1)}, f32[128,128]{1,0:T(8,128)S(1)}, u32[]{:S(2)}, u32[]{:S(2)}) collective-permute-start(f32[128,128]{1,0:T(8,128)S(1)} %get-tuple-element.34), channel_id=1, source_target_pairs={{0,4},{4,0},{8,12},{12,8},{16,20},{20,16},{24,28},{28,24},{1,5},{5... | collective-permute-start | bytes 196616 | tf_op jit(solution)/shard_map/ppermute | solution.py:71
  10.5 6.0 %collective-permute-start.3 = (f32[64,128]{1,0:T(8,128)S(1)}, f32[64,128]{1,0:T(8,128)S(1)}, u32[]{:S(2)}, u32[]{:S(2)}) collective-permute-start(f32[64,128]{1,0:T(8,128)S(1)} %get-tuple-element.36), channel_id=1, source_target_pairs={{0,24},{4,28},{8,16},{12,20},{16,8},{20,12},{24,0},{28,4},{1,25},{... | collective-permute-start | bytes 98312 | tf_op jit(solution)/shard_map/ppermute | solution.py:71
  14.4 4.8 %collective-permute-start.4 = (f32[64,128]{1,0:T(8,128)S(1)}, f32[64,128]{1,0:T(8,128)S(1)}, u32[]{:S(2)}, u32[]{:S(2)}) collective-permute-start(f32[64,128]{1,0:T(8,128)S(1)} %get-tuple-element.37), channel_id=1, source_target_pairs={{0,16},{4,20},{8,24},{12,28},{16,0},{20,4},{24,8},{28,12},{1,17},{... | collective-permute-start | bytes 98312 | tf_op jit(solution)/shard_map/ppermute | solution.py:71
  14.4 4.8 %collective-permute-start.5 = (f32[64,128]{1,0:T(8,128)S(1)}, f32[64,128]{1,0:T(8,128)S(1)}, u32[]{:S(2)}, u32[]{:S(2)}) collective-permute-start(f32[64,128]{1,0:T(8,128)S(1)} %get-tuple-element.38), channel_id=1, source_target_pairs={{0,8},{4,12},{8,0},{12,4},{16,24},{20,28},{24,16},{28,20},{1,9},{5... | collective-permute-start | bytes 98312 | tf_op jit(solution)/shard_map/ppermute | solution.py:71
  22.7 4.3 %collective-permute-start.6 = (f32[128,128]{1,0:T(8,128)S(1)}, f32[128,128]{1,0:T(8,128)S(1)}, u32[]{:S(2)}, u32[]{:S(2)}) collective-permute-start(f32[128,128]{1,0:T(8,128)S(1)} %get-tuple-element.45), channel_id=1, source_target_pairs={{0,4},{4,0},{8,12},{12,8},{16,20},{20,16},{24,28},{28,24},{1,5},{5... | collective-permute-start | bytes 196616 | tf_op jit(solution)/shard_map/ppermute | solution.py:71
  27.0 5.4 %collective-permute-start.7 = (f32[64,128]{1,0:T(8,128)S(1)}, f32[64,128]{1,0:T(8,128)S(1)}, u32[]{:S(2)}, u32[]{:S(2)}) collective-permute-start(f32[64,128]{1,0:T(8,128)S(1)} %get-tuple-element.46), channel_id=1, source_target_pairs={{0,16},{4,20},{8,24},{12,28},{16,0},{20,4},{24,8},{28,12},{1,17},{... | collective-permute-start | bytes 98312 | tf_op jit(solution)/shard_map/ppermute | solution.py:71
  29.1 5.7 %collective-permute-start.8 = (f32[64,128]{1,0:T(8,128)S(1)}, f32[64,128]{1,0:T(8,128)S(1)}, u32[]{:S(2)}, u32[]{:S(2)}) collective-permute-start(f32[64,128]{1,0:T(8,128)S(1)} %get-tuple-element.47), channel_id=1, source_target_pairs={{0,24},{4,28},{8,16},{12,20},{16,8},{20,12},{24,0},{28,4},{1,25},{... | collective-permute-start | bytes 98312 | tf_op jit(solution)/shard_map/ppermute | solution.py:71
  29.2 5.6 %collective-permute-start.9 = (f32[64,128]{1,0:T(8,128)S(1)}, f32[64,128]{1,0:T(8,128)S(1)}, u32[]{:S(2)}, u32[]{:S(2)}) collective-permute-start(f32[64,128]{1,0:T(8,128)S(1)} %get-tuple-element.48), channel_id=1, source_target_pairs={{0,8},{4,12},{8,0},{12,4},{16,24},{20,28},{24,16},{28,20},{1,9},{5... | collective-permute-start | bytes 98312 | tf_op jit(solution)/shard_map/ppermute | solution.py:71

commit v13 on v10

--- a/solution.py
+++ b/solution.py
@@ -492,7 +492,6 @@
         aliases={len(received): 0},
         cost=cost(5),
     )
-    returned = exchange(tend)
     crm_new = call(
         store_kernel,
         jax.ShapeDtypeStruct((CZ, CX * slots), bf16),
@@ -501,6 +500,7 @@
         out_specs=hbm,
         cost=cost(3),
     )
+    returned = exchange(tend, (crm_new,))
     new_state = call(
         functools.partial(finish_kernel, staged),
         jax.ShapeDtypeStruct((per_tile, width), f32),

time: 34.9 us -> 36.5 us (1.046)
  local copies, waits for them, and re-layouts: 0 us -> 1.59 us
    unnamed x0 -> x2, local copies, waits for them, and re-layouts: none -> 1.59 us
  transfers between devices with their start and end apart: 10 -> 10, of which waited for: 4 -> 6; matrix products, arithmetic and copies ran while one was open for 0% -> 0% of each run, Pallas kernels for 15% -> 15%
where the time goes in v13:
time: 36.5 us; the launch traced here: 36.1 us
  starting transfers between devices  15.9 us (44%)
  Pallas kernels  10.6 us (29%)
  waiting for transfers between devices  7.32 us (20%)
  local copies, waits for them, and re-layouts  1.59 us (4%)
  between operations  0.72 us (2%)
    ppermute x8, starting transfers between devices, trade(): return lax.ppermute(value, 'cols', [(c, c ^ k) for c in range(count)])  12.7 us
    pallas_call x9, Pallas kernels, call(): pl.pallas_call(body, out_shape=outs, scratch_shapes=list(scratch), compil...  10.6 us
    ppermute x8, waiting for transfers between devices, trade(): return lax.ppermute(value, 'cols', [(c, c ^ k) for c in range(count)])  7.31 us
    ppermute x2, starting transfers between devices, swap(): return lax.ppermute(value, axis, pairs)  3.15 us
    unnamed x2, local copies, waits for them, and re-layouts  1.59 us
  transfers between devices with their start and end apart: 10, of which 6 were waited for; matrix products, arithmetic and copies ran while one was open for 0% of the time, Pallas kernels for 15%

profile of v13, /device:TPU:0, one launch (start us, length us, event | category | flops | bytes accessed | tf_op | source)
XLA Modules:
  0.0 36.1 jit_solution(13656998195159404608)
XLA Ops:
  0.6 0.8 %shard_map.87 = (f32[8,512]{1,0:T(8,128)S(1)}, f32[8,512]{1,0:T(8,128)S(1)}) custom-call(f32[128,512]{1,0:T(8,128)} %bitcast.9), custom_call_target="tpu_custom_call" | custom-call | bytes 1500000 | tf_op jit(solution)/shard_map/pallas_call | solution.py:33
  1.4 2.5 %collective-permute-start = (f32[8,512]{1,0:T(8,128)S(1)}, f32[8,512]{1,0:T(8,128)S(1)}, u32[]{:S(2)}, u32[]{:S(2)}) collective-permute-start(f32[8,512]{1,0:T(8,128)S(1)} %get-tuple-element.27), channel_id=1, source_target_pairs={{1,2},{2,1},{3,0},{0,3},{5,6},{6,5},{7,4},{4,7},{9,10},{10,9},{11,... | collective-permute-start | bytes 49160 | tf_op jit(solution)/shard_map/ppermute | solution.py:50
  3.9 0.7 %collective-permute-start.1 = (f32[8,512]{1,0:T(8,128)S(1)}, f32[8,512]{1,0:T(8,128)S(1)}, u32[]{:S(2)}, u32[]{:S(2)}) collective-permute-start(f32[8,512]{1,0:T(8,128)S(1)} %get-tuple-element.28), channel_id=1, source_target_pairs={{0,1},{1,0},{2,3},{3,2},{4,5},{5,4},{6,7},{7,6},{8,9},{9,8},{10,11... | collective-permute-start | bytes 49160 | tf_op jit(solution)/shard_map/ppermute | solution.py:50
  4.5 1.0 %shard_map.86 = (f32[128,512]{1,0:T(8,128)S(1)}, bf16[256,128]{1,0:T(8,128)(2,1)S(1)}, bf16[128,256]{1,0:T(8,128)(2,1)S(1)}, s32[2,8,128]{2,1,0:T(8,128)S(1)}) custom-call(f32[128,512]{1,0:T(8,128)} %bitcast.10, s32[1,128]{1,0:T(1,128)} %bitcast.13, s32[1,2]{1,0:T(1,128)} %bitcast.14), custom_call_target="tpu_custom_call" | custom-call | bytes 3000000 | tf_op jit(solution)/shard_map/pallas_call | solution.py:33
  5.6 0.0 collective-permute-done.1.inner_ref
  5.6 0.2 shard_map.88
  5.8 2.1 %collective-permute-start.2 = (f32[128,128]{1,0:T(8,128)S(1)}, f32[128,128]{1,0:T(8,128)S(1)}, u32[]{:S(2)}, u32[]{:S(2)}) collective-permute-start(f32[128,128]{1,0:T(8,128)S(1)} %get-tuple-element.34), channel_id=1, source_target_pairs={{0,4},{4,0},{8,12},{12,8},{16,20},{20,16},{24,28},{28,24},{1,5},{5... | collective-permute-start | bytes 196616 | tf_op jit(solution)/shard_map/ppermute | solution.py:70
  8.0 2.5 %shard_map.89 = (bf16[3712,256]{1,0:T(8,128)(2,1)S(1)}, f32[64,256]{1,0:T(8,128)S(1)}, f32[64,256]{1,0:T(8,128)S(1)}, f32[6,64,256]{2,1,0:T(8,128)S(1)}, bf16[12...) custom-call(bf16[58,16384]{1,0:T(8,128)(2,1)} %bitcast.8, s32[1,256]{1,0:T(1,128)} %bitcast.12, f32[57]{0:T(128)} %diff_hbm.1, ...), custom_call_target="tpu_custom_call" | custom-call | bytes 12000000 | tf_op jit(solution)/shard_map/pallas_call | solution.py:33
  10.5 4.0 %collective-permute-start.3 = (f32[64,128]{1,0:T(8,128)S(1)}, f32[64,128]{1,0:T(8,128)S(1)}, u32[]{:S(2)}, u32[]{:S(2)}) collective-permute-start(f32[64,128]{1,0:T(8,128)S(1)} %get-tuple-element.36), channel_id=1, source_target_pairs={{0,24},{4,28},{8,16},{12,20},{16,8},{20,12},{24,0},{28,4},{1,25},{... | collective-permute-start | bytes 98312 | tf_op jit(solution)/shard_map/ppermute | solution.py:70
  14.4 0.6 %collective-permute-start.5 = (f32[64,128]{1,0:T(8,128)S(1)}, f32[64,128]{1,0:T(8,128)S(1)}, u32[]{:S(2)}, u32[]{:S(2)}) collective-permute-start(f32[64,128]{1,0:T(8,128)S(1)} %get-tuple-element.38), channel_id=1, source_target_pairs={{0,8},{4,12},{8,0},{12,4},{16,24},{20,28},{24,16},{28,20},{1,9},{5... | collective-permute-start | bytes 98312 | tf_op jit(solution)/shard_map/ppermute | solution.py:70
  15.1 1.4 %collective-permute-done.3.refs_2_ = f32[64,128]{1,0:T(8,128)S(1)} collective-permute-done((f32[64,128]{1,0:T(8,128)S(1)}, f32[64,128]{1,0:T(8,128)S(1)}, u32[]{:S(2)}, u32[]{:S(2)}) %collective-permute-start.3) | collective-permute-done | bytes 32800 | tf_op jit(solution)/shard_map/ppermute | solution.py:70
  16.5 2.8 %collective-permute-done.4.refs_3_ = f32[64,128]{1,0:T(8,128)S(1)} collective-permute-done((f32[64,128]{1,0:T(8,128)S(1)}, f32[64,128]{1,0:T(8,128)S(1)}, u32[]{:S(2)}, u32[]{:S(2)}) %collective-permute-start.4) | collective-permute-done | bytes 32800 | tf_op jit(solution)/shard_map/ppermute | solution.py:70
  19.2 3.4 %shard_map.91 = (bf16[3712,256]{1,0:T(8,128)(2,1)S(1)}, f32[128,128]{1,0:T(8,128)S(1)}, f32[128,128]{1,0:T(8,128)S(1)}) custom-call(f32[128,128]{1,0:T(8,128)S(1)} %get-tuple-element.33.own_ref.refs_0_, f32[128,128]{1,0:T(8,128)S(1)} %collective-permute-done.2.got_ref.refs_1_, ...), custom_call_target="tpu_custom_call", output_to_operand_aliasing={{0}: (5, {})} | custom-call | bytes 15000000 | tf_op jit(solution)/shard_map/pallas_call | solution.py:33
  22.7 1.6 %collective-permute-start.6 = (f32[128,128]{1,0:T(8,128)S(1)}, f32[128,128]{1,0:T(8,128)S(1)}, u32[]{:S(2)}, u32[]{:S(2)}) collective-permute-start(f32[128,128]{1,0:T(8,128)S(1)} %get-tuple-element.45), channel_id=1, source_target_pairs={{0,4},{4,0},{8,12},{12,8},{16,20},{20,16},{24,28},{28,24},{1,5},{5... | collective-permute-start | bytes 196616 | tf_op jit(solution)/shard_map/ppermute | solution.py:70
  24.2 1.9 %shard_map.92.refs_0_ = bf16[58,16384]{1,0:T(8,128)(2,1)} custom-call(bf16[3712,256]{1,0:T(8,128)(2,1)S(1)} %get-tuple-element.46.y_ref), custom_call_target="tpu_custom_call" | custom-call | bytes 9000000 | tf_op jit(solution)/shard_map/pallas_call | solution.py:33
  26.1 0.9 %collective-permute-done.6.got_ref.refs_1_ = f32[128,128]{1,0:T(8,128)S(1)} collective-permute-done((f32[128,128]{1,0:T(8,128)S(1)}, f32[128,128]{1,0:T(8,128)S(1)}, u32[]{:S(2)}, u32[]{:S(2)}) %collective-permute-start.6) | collective-permute-done | bytes 65568 | tf_op jit(solution)/shard_map/ppermute | solution.py:70
  27.0 1.6 %copy-done = bf16[58,16384]{1,0:T(8,128)(2,1)S(1)} copy-done((bf16[58,16384]{1,0:T(8,128)(2,1)S(1)}, bf16[58,16384]{1,0:T(8,128)(2,1)}, u32[]{:S(2)}) %copy-start) | copy-done | bytes 1900568
  28.6 1.5 %collective-permute-start.7 = (f32[64,128]{1,0:T(8,128)S(1)}, f32[64,128]{1,0:T(8,128)S(1)}, u32[]{:S(2)}, u32[]{:S(2)}) collective-permute-start(f32[64,128]{1,0:T(8,128)S(1)} %get-tuple-element.47), channel_id=1, source_target_pairs={{0,24},{4,28},{8,16},{12,20},{16,8},{20,12},{24,0},{28,4},{1,25},{... | collective-permute-start | bytes 98312 | tf_op jit(solution)/shard_map/ppermute | solution.py:70
  30.1 0.6 %collective-permute-start.8 = (f32[64,128]{1,0:T(8,128)S(1)}, f32[64,128]{1,0:T(8,128)S(1)}, u32[]{:S(2)}, u32[]{:S(2)}) collective-permute-start(f32[64,128]{1,0:T(8,128)S(1)} %get-tuple-element.48), channel_id=1, source_target_pairs={{0,16},{4,20},{8,24},{12,28},{16,0},{20,4},{24,8},{28,12},{1,17},{... | collective-permute-start | bytes 98312 | tf_op jit(solution)/shard_map/ppermute | solution.py:70
  30.8 2.3 %collective-permute-start.9 = (f32[64,128]{1,0:T(8,128)S(1)}, f32[64,128]{1,0:T(8,128)S(1)}, u32[]{:S(2)}, u32[]{:S(2)}) collective-permute-start(f32[64,128]{1,0:T(8,128)S(1)} %get-tuple-element.49), channel_id=1, source_target_pairs={{0,8},{4,12},{8,0},{12,4},{16,24},{20,28},{24,16},{28,20},{1,9},{5... | collective-permute-start | bytes 98312 | tf_op jit(solution)/shard_map/ppermute | solution.py:70
  33.0 1.3 %collective-permute-done.7.refs_2_ = f32[64,128]{1,0:T(8,128)S(1)} collective-permute-done((f32[64,128]{1,0:T(8,128)S(1)}, f32[64,128]{1,0:T(8,128)S(1)}, u32[]{:S(2)}, u32[]{:S(2)}) %collective-permute-start.7) | collective-permute-done | bytes 32800 | tf_op jit(solution)/shard_map/ppermute | solution.py:70
  34.4 0.6 %collective-permute-done.8.refs_3_ = f32[64,128]{1,0:T(8,128)S(1)} collective-permute-done((f32[64,128]{1,0:T(8,128)S(1)}, f32[64,128]{1,0:T(8,128)S(1)}, u32[]{:S(2)}, u32[]{:S(2)}) %collective-permute-start.8) | collective-permute-done | bytes 32800 | tf_op jit(solution)/shard_map/ppermute | solution.py:70
  35.0 0.3 collective-permute-done.9.refs_4_
  35.3 0.8 %shard_map.94 = f32[128,512]{1,0:T(8,128)} custom-call(f32[128,512]{1,0:T(8,128)S(1)} %get-tuple-element.31.moved_ref, bf16[128,256]{1,0:T(8,128)(2,1)S(1)} %get-tuple-element.32.take_ref, f32[128,128]{1,0:T(8,128)S(1)} %get-tuple-element.44.own_ref.refs_0_, f32[128,128]{1,0:T(8,128)S(1)} %collective-permute-done.6.got_ref.refs_1_, ...), custom_call_target="tpu_custom_call" | custom-call | bytes 2100000 | tf_op jit(solution)/shard_map/pallas_call | solution.py:33
  (7 shorter events, 0.0 us)
Async XLA Ops:
  1.4 4.2 %collective-permute-start = (f32[8,512]{1,0:T(8,128)S(1)}, f32[8,512]{1,0:T(8,128)S(1)}, u32[]{:S(2)}, u32[]{:S(2)}) collective-permute-start(f32[8,512]{1,0:T(8,128)S(1)} %get-tuple-element.27), channel_id=1, source_target_pairs={{1,2},{2,1},{3,0},{0,3},{5,6},{6,5},{7,4},{4,7},{9,10},{10,9},{11,... | collective-permute-start | bytes 49160 | tf_op jit(solution)/shard_map/ppermute | solution.py:50
  3.9 1.7 %collective-permute-start.1 = (f32[8,512]{1,0:T(8,128)S(1)}, f32[8,512]{1,0:T(8,128)S(1)}, u32[]{:S(2)}, u32[]{:S(2)}) collective-permute-start(f32[8,512]{1,0:T(8,128)S(1)} %get-tuple-element.28), channel_id=1, source_target_pairs={{0,1},{1,0},{2,3},{3,2},{4,5},{5,4},{6,7},{7,6},{8,9},{9,8},{10,11... | collective-permute-start | bytes 49160 | tf_op jit(solution)/shard_map/ppermute | solution.py:50
  5.8 4.6 %collective-permute-start.2 = (f32[128,128]{1,0:T(8,128)S(1)}, f32[128,128]{1,0:T(8,128)S(1)}, u32[]{:S(2)}, u32[]{:S(2)}) collective-permute-start(f32[128,128]{1,0:T(8,128)S(1)} %get-tuple-element.34), channel_id=1, source_target_pairs={{0,4},{4,0},{8,12},{12,8},{16,20},{20,16},{24,28},{28,24},{1,5},{5... | collective-permute-start | bytes 196616 | tf_op jit(solution)/shard_map/ppermute | solution.py:70
  10.5 6.0 %collective-permute-start.3 = (f32[64,128]{1,0:T(8,128)S(1)}, f32[64,128]{1,0:T(8,128)S(1)}, u32[]{:S(2)}, u32[]{:S(2)}) collective-permute-start(f32[64,128]{1,0:T(8,128)S(1)} %get-tuple-element.36), channel_id=1, source_target_pairs={{0,24},{4,28},{8,16},{12,20},{16,8},{20,12},{24,0},{28,4},{1,25},{... | collective-permute-start | bytes 98312 | tf_op jit(solution)/shard_map/ppermute | solution.py:70
  14.4 4.8 %collective-permute-start.4 = (f32[64,128]{1,0:T(8,128)S(1)}, f32[64,128]{1,0:T(8,128)S(1)}, u32[]{:S(2)}, u32[]{:S(2)}) collective-permute-start(f32[64,128]{1,0:T(8,128)S(1)} %get-tuple-element.37), channel_id=1, source_target_pairs={{0,16},{4,20},{8,24},{12,28},{16,0},{20,4},{24,8},{28,12},{1,17},{... | collective-permute-start | bytes 98312 | tf_op jit(solution)/shard_map/ppermute | solution.py:70
  14.4 4.8 %collective-permute-start.5 = (f32[64,128]{1,0:T(8,128)S(1)}, f32[64,128]{1,0:T(8,128)S(1)}, u32[]{:S(2)}, u32[]{:S(2)}) collective-permute-start(f32[64,128]{1,0:T(8,128)S(1)} %get-tuple-element.38), channel_id=1, source_target_pairs={{0,8},{4,12},{8,0},{12,4},{16,24},{20,28},{24,16},{28,20},{1,9},{5... | collective-permute-start | bytes 98312 | tf_op jit(solution)/shard_map/ppermute | solution.py:70
  22.7 4.3 %collective-permute-start.6 = (f32[128,128]{1,0:T(8,128)S(1)}, f32[128,128]{1,0:T(8,128)S(1)}, u32[]{:S(2)}, u32[]{:S(2)}) collective-permute-start(f32[128,128]{1,0:T(8,128)S(1)} %get-tuple-element.45), channel_id=1, source_target_pairs={{0,4},{4,0},{8,12},{12,8},{16,20},{20,16},{24,28},{28,24},{1,5},{5... | collective-permute-start | bytes 196616 | tf_op jit(solution)/shard_map/ppermute | solution.py:70
  27.0 1.6 %copy-start = (bf16[58,16384]{1,0:T(8,128)(2,1)S(1)}, bf16[58,16384]{1,0:T(8,128)(2,1)}, u32[]{:S(2)}) copy-start(bf16[58,16384]{1,0:T(8,128)(2,1)} %shard_map.92.refs_0_) | copy-start | bytes 5701636
  28.6 5.8 %collective-permute-start.7 = (f32[64,128]{1,0:T(8,128)S(1)}, f32[64,128]{1,0:T(8,128)S(1)}, u32[]{:S(2)}, u32[]{:S(2)}) collective-permute-start(f32[64,128]{1,0:T(8,128)S(1)} %get-tuple-element.47), channel_id=1, source_target_pairs={{0,24},{4,28},{8,16},{12,20},{16,8},{20,12},{24,0},{28,4},{1,25},{... | collective-permute-start | bytes 98312 | tf_op jit(solution)/shard_map/ppermute | solution.py:70
  30.1 4.8 %collective-permute-start.8 = (f32[64,128]{1,0:T(8,128)S(1)}, f32[64,128]{1,0:T(8,128)S(1)}, u32[]{:S(2)}, u32[]{:S(2)}) collective-permute-start(f32[64,128]{1,0:T(8,128)S(1)} %get-tuple-element.48), channel_id=1, source_target_pairs={{0,16},{4,20},{8,24},{12,28},{16,0},{20,4},{24,8},{28,12},{1,17},{... | collective-permute-start | bytes 98312 | tf_op jit(solution)/shard_map/ppermute | solution.py:70
  30.8 4.5 %collective-permute-start.9 = (f32[64,128]{1,0:T(8,128)S(1)}, f32[64,128]{1,0:T(8,128)S(1)}, u32[]{:S(2)}, u32[]{:S(2)}) collective-permute-start(f32[64,128]{1,0:T(8,128)S(1)} %get-tuple-element.49), channel_id=1, source_target_pairs={{0,8},{4,12},{8,0},{12,4},{16,24},{20,28},{24,16},{28,20},{1,9},{5... | collective-permute-start | bytes 98312 | tf_op jit(solution)/shard_map/ppermute | solution.py:70
